TPU v7x, 32 devices: a whole 2x2x4 slice. The times are simulated.
32 devices in a mesh: clip: 2 (over x), frame: 8 (over z, y), band: 2 (over core).
Axes of the slice: x: 2, y: 2, z: 4, core: 2. Of those that a mesh axis runs over, the one named last changes fastest.
Arguments:
- pixels: bfloat16 [16, 16, 32, 256], P(('clip', 'frame'), 'band'), parts along dimension 0, may hold values from -40 to 40
- gru_state: bfloat16 [16, 16, 32, 128], P(('clip', 'frame'), 'band'), parts along dimension 0, may hold values from -1 to 1
- tokens: bfloat16 [16, 1024, 256], P(('clip', 'frame'), 'band'), parts along dimension 0, may hold values from -30 to 30
- visible: int32 [16, 1024], P(('clip', 'frame'), 'band'), parts along dimension 0, may hold values from 0 to 1, as said below
- query_frame: int32 [2048], P(('clip', 'band')), parts along dimension 0, may hold values from 0 to 7, as said below
- pixel_query: bfloat16 [256, 256], replicated, may hold values from -2 to 2
- pixel_key: bfloat16 [256, 256], replicated, may hold values from -2 to 2
- pixel_value: bfloat16 [256, 256], replicated, may hold values from -0.375 to 0.375
- pixel_out: bfloat16 [256, 128], replicated, may hold values from -1.5 to 1.5
- time_query: bfloat16 [256, 256], replicated, may hold values from -2 to 2
- time_key: bfloat16 [256, 256], replicated, may hold values from -2 to 2
- time_value: bfloat16 [256, 256], replicated, may hold values from -0.375 to 0.375
- time_out: bfloat16 [256, 256], replicated, may hold values from -0.75 to 0.75
- gru_gates: bfloat16 [3, 3, 256, 256], replicated, may hold values from -0.125 to 0.125
- gru_candidate: bfloat16 [3, 3, 256, 128], replicated, may hold values from -0.125 to 0.125
Outputs:
- refined_state: bfloat16 [16, 16, 32, 128], P(('clip', 'frame'), 'band'), parts along dimension 0
- track_out: bfloat16 [16, 1024, 256], P(('clip', 'frame'), 'band'), parts along dimension 0
There are 2 independent parts, one for each index of `clip`. A program takes and returns all parts, laid end to end along the dimension named above; an argument that names none is the same for every part. Nothing has to cross between parts.
Inputs may be any that keep to these rules, and one draw needn't show every extreme that they name: Each track is visible in the frame named by its query frame index. `query_frame`: every frame is the query frame of exactly 128 tracks.
All inputs are finite; a program needn't handle non-finite values.
Results may differ from a plain program's by a relative error of at most 0.0095.
The roundings to bfloat16 on the way count: a program that leaves them out, or rounds other values in their place, can miss the bound.
Values may be sent and summed in bfloat16 or wider, within the bound.
No kernel may reach another device: no remote copies, remote signals or barrier semaphores. Data moves between devices by JAX's collectives and lax.ppermute only.
A program may use at most 64 MiB of HBM per device.

v0:
```python
import jax
import jax.numpy as jnp
from jax import lax
from jax.sharding import PartitionSpec as P

HEADS = 8
HEAD_DIM = 32
GRU_WIDTH = 128
ITERS = 2


def with_halo(x, sides, width):
    for axis, dim in sides:
        devices, length = (lax.axis_size(axis), x.shape[dim])
        up = [(i, (i + 1) % devices) for i in range(devices - 1)]
        down = [(j, i) for i, j in up]
        last = lax.slice_in_dim(x, length - width, length, axis=dim)
        first = lax.slice_in_dim(x, 0, width, axis=dim)
        before = lax.ppermute(last, axis, up)
        after = lax.ppermute(first, axis, down)
        x = jnp.concatenate([before, x, after], axis=dim)
    return x


def attend_heads(queries, key_rows, value_rows, key_mask):
    score_scale = HEAD_DIM ** (-0.5)
    head_outputs = []
    for head_index in range(HEADS):
        offset = head_index * HEAD_DIM
        scores = (
            jnp.dot(
                queries[:, offset : offset + HEAD_DIM],
                key_rows[:, offset : offset + HEAD_DIM].T,
                preferred_element_type=jnp.float32,
            )
            * score_scale
        )
        scores = jnp.where(key_mask[None, :], scores, -jnp.inf)
        weights = jax.nn.softmax(scores, axis=-1).astype(jnp.bfloat16)
        head_outputs.append(
            jnp.dot(
                weights,
                value_rows[:, offset : offset + HEAD_DIM],
                preferred_element_type=jnp.float32,
            )
        )
    return jnp.concatenate(head_outputs, axis=-1).astype(jnp.bfloat16)


def conv_rows(padded, weight, rows, columns):
    widened = jnp.pad(padded, ((0, 0), (1, 1), (0, 0)))
    summed = jnp.zeros((rows * columns, weight.shape[3]), jnp.float32)
    for row_shift in range(3):
        for col_shift in range(3):
            window = widened[row_shift : row_shift + rows, col_shift : col_shift + columns]
            summed = summed + jnp.dot(
                window.reshape(rows * columns, -1),
                weight[row_shift, col_shift],
                preferred_element_type=jnp.float32,
            )
    return summed


def temporal_core(query_part, key_part, value_part, seen_part, anchor_part):
    frames_here, track_count, channels = query_part.shape
    anchor = jnp.einsum("fk,fkc->kc", anchor_part, query_part, preferred_element_type=jnp.float32)
    joint_query = (query_part.astype(jnp.float32) + anchor[None]).astype(jnp.bfloat16)
    shaped = (frames_here, track_count, HEADS, HEAD_DIM)
    scores = jnp.einsum(
        "fkhd,gkhd->khfg",
        joint_query.reshape(shaped),
        key_part.reshape(shaped),
        preferred_element_type=jnp.float32,
    ) * HEAD_DIM ** (-0.5)
    key_mask = jnp.transpose(seen_part) > 0
    scores = jnp.where(key_mask[:, None, None, :], scores, -jnp.inf)
    weights = jax.nn.softmax(scores, axis=-1).astype(jnp.bfloat16)
    attended = jnp.einsum(
        "khfg,gkhd->fkhd", weights, value_part.reshape(shaped), preferred_element_type=jnp.float32
    )
    return attended.astype(jnp.bfloat16).reshape(frames_here, track_count, channels)


def on_device(
    pixels,
    gru_state,
    tokens,
    visible,
    query_frame,
    pixel_query,
    pixel_key,
    pixel_value,
    pixel_out,
    time_query,
    time_key,
    time_value,
    time_out,
    gru_gates,
    gru_candidate,
):
    frame_pos = lax.axis_index("frame")
    frames = lax.axis_size("frame")
    channels = tokens.shape[2]
    half_tracks = tokens.shape[1]
    per_device = half_tracks // frames
    band_rows = pixels.shape[1]
    columns = pixels.shape[2]
    local_tokens = tokens[0]
    seen_mask = visible[0].astype(jnp.bfloat16)
    anchor_mask = (query_frame == frame_pos).astype(jnp.bfloat16)
    seen_split = seen_mask.reshape(1, frames, per_device)
    anchor_split = anchor_mask.reshape(1, frames, per_device)
    token_part = lax.all_to_all(
        local_tokens.reshape(1, frames, per_device, channels),
        "frame",
        split_axis=1,
        concat_axis=0,
        tiled=True,
    )
    seen_part = lax.all_to_all(seen_split, "frame", split_axis=1, concat_axis=0, tiled=True)
    anchor_part = lax.all_to_all(anchor_split, "frame", split_axis=1, concat_axis=0, tiled=True)
    token_rows = token_part[:, 0]
    frames_here, track_count, width_here = token_rows.shape
    flat_rows = token_rows.reshape(frames_here * track_count, width_here)
    outputs = []
    for weight in (time_query, time_key, time_value):
        outputs.append(
            jnp.dot(flat_rows, weight, preferred_element_type=jnp.float32)
            .astype(jnp.bfloat16)
            .reshape(frames_here, track_count, width_here)
        )
    result = temporal_core(outputs[0], outputs[1], outputs[2], seen_part[:, 0], anchor_part[:, 0])
    track_result = result[:, None]
    flat_pixels = pixels[0].reshape(band_rows * columns, channels)
    queries = jnp.dot(flat_pixels, pixel_query, preferred_element_type=jnp.float32).astype(
        jnp.bfloat16
    )
    key_local = jnp.dot(local_tokens, pixel_key, preferred_element_type=jnp.float32).astype(
        jnp.bfloat16
    )
    value_local = jnp.dot(local_tokens, pixel_value, preferred_element_type=jnp.float32).astype(
        jnp.bfloat16
    )
    key_rows, value_rows, seen_all = (
        lax.all_gather(key_local, "band", axis=0, tiled=True),
        lax.all_gather(value_local, "band", axis=0, tiled=True),
        lax.all_gather(seen_mask, "band", axis=0, tiled=True),
    )
    attended = attend_heads(queries, key_rows, value_rows, seen_all > 0)
    context = (
        jnp.dot(attended, pixel_out, preferred_element_type=jnp.float32)
        .astype(jnp.bfloat16)
        .reshape(band_rows, columns, GRU_WIDTH)
    )
    returned = lax.all_to_all(track_result, "frame", split_axis=0, concat_axis=1, tiled=True)
    returned_rows = returned.reshape(half_tracks, channels)
    track_update = jnp.dot(returned_rows, time_out, preferred_element_type=jnp.float32)
    track_out = (local_tokens.astype(jnp.float32) + track_update).astype(jnp.bfloat16)[None]
    state_now = gru_state[0]
    for iteration in range(ITERS):
        combined = jnp.concatenate([state_now, context], axis=-1)
        padded = with_halo(combined, (("band", 0),), 1)
        gate_terms = conv_rows(padded, gru_gates, band_rows, columns)
        update = jax.nn.sigmoid(gate_terms[:, :GRU_WIDTH])
        reset_gate = jax.nn.sigmoid(gate_terms[:, GRU_WIDTH:])
        state_flat = state_now.reshape(band_rows * columns, GRU_WIDTH).astype(jnp.float32)
        reset_state = (
            (reset_gate * state_flat).astype(jnp.bfloat16).reshape(band_rows, columns, GRU_WIDTH)
        )
        mixed_in = jnp.concatenate([reset_state, context], axis=-1)
        padded_mix = with_halo(mixed_in, (("band", 0),), 1)
        candidate = jnp.tanh(conv_rows(padded_mix, gru_candidate, band_rows, columns))
        state_now = (
            ((1.0 - update) * state_flat + update * candidate)
            .astype(jnp.bfloat16)
            .reshape(band_rows, columns, GRU_WIDTH)
        )
    refined_state = state_now[None]
    return (refined_state, track_out)


def solution(mesh):
    placed = (
        P(("clip", "frame"), "band", None, None),
        P(("clip", "frame"), "band", None, None),
        P(("clip", "frame"), "band", None),
        P(("clip", "frame"), "band"),
        P(("clip", "band")),
        P(),
        P(),
        P(),
        P(),
        P(),
        P(),
        P(),
        P(),
        P(),
        P(),
    )
    return jax.shard_map(
        on_device,
        mesh=mesh,
        in_specs=placed,
        out_specs=(P(("clip", "frame"), "band", None, None), P(("clip", "frame"), "band", None)),
        check_vma=False,
    )
```

profile of v0, /device:TPU:0, one launch (start us, length us, event | category | flops | bytes accessed | tf_op | source)
XLA Modules:
  0.0 105.7 jit_solution(6565268605685878097)
XLA Ops:
  1.5 1.2 %convolution_convert_fusion.5 = bf16[512,256]{1,0:T(8,128)(2,1)S(1)} fusion(bf16[256,256]{1,0:T(8,128)(2,1)S(1)} %copy-done, bf16[1,512,256]{2,1,0:T(8,128)(2,1)} %param.17), kind=kOutput, calls=%fused_computation.25 | convolution fusion | flops 67239936 | bytes 655360 | tf_op jit(solution)/shard_map/dot_general | solution.py:138
  2.7 2.3 %all_gather.10 = bf16[1024,256]{1,0:T(8,128)(2,1)S(1)} all-gather(bf16[512,256]{1,0:T(8,128)(2,1)S(1)} %convolution_convert_fusion.5), channel_id=1, replica_groups=mesh['clip'=2,'frame'=8,'band'=2] {'band'}, dimensions={0}, use_global_device_ids=true | all-gather | bytes 786432 | tf_op jit(solution)/shard_map/all_gather | solution.py:145
  5.0 1.9 %all-gather = bf16[1,1024]{1,0:T(2,128)(2,1)S(1)} all-gather(bf16[1,512]{1,0:T(2,128)(2,1)S(1)} %convert_element_type.112), channel_id=2, replica_groups=mesh['clip'=2,'frame'=8,'band'=2] {'band'}, dimensions={1}, use_global_device_ids=true | all-gather | bytes 3072 | tf_op jit(solution)/shard_map/all_gather | solution.py:147
  10.9 1.2 %convolution_convert_fusion.4 = bf16[512,256]{1,0:T(8,128)(2,1)S(1)} fusion(bf16[256,256]{1,0:T(8,128)(2,1)S(1)} %copy-done.11, bf16[1,512,256]{2,1,0:T(8,128)(2,1)} %param.17), kind=kOutput, calls=%fused_computation.24 | convolution fusion | flops 67239936 | bytes 655360 | tf_op jit(solution)/shard_map/dot_general | solution.py:141
  12.0 2.2 %all_gather.11 = bf16[1024,256]{1,0:T(8,128)(2,1)S(1)} all-gather(bf16[512,256]{1,0:T(8,128)(2,1)S(1)} %convolution_convert_fusion.4), channel_id=1, replica_groups=mesh['clip'=2,'frame'=8,'band'=2] {'band'}, dimensions={0}, use_global_device_ids=true | all-gather | bytes 786432 | tf_op jit(solution)/shard_map/all_gather | solution.py:146
  21.0 2.3 %collective-permute-start = (bf16[1,32,256]{2,1,0:T(8,128)(2,1)S(1)}, bf16[1,32,256]{2,1,0:T(8,128)(2,1)S(1)}, u32[]{:S(2)}, u32[]{:S(2)}) collective-permute-start(bf16[1,32,256]{2,1,0:T(8,128)(2,1)S(1)} %get-tuple-element.42), channel_id=1, source_target_pairs={{0,1},{2,3},{4,5},{6,7},{8,9},{10,11},{12,13},{14,15},{16,17},{18,... | collective-permute-start | bytes 49160 | tf_op jit(solution)/shard_map/ppermute | solution.py:19
  23.3 1.3 %collective-permute-start.1 = (bf16[1,32,256]{2,1,0:T(8,128)(2,1)S(1)}, bf16[1,32,256]{2,1,0:T(8,128)(2,1)S(1)}, u32[]{:S(2)}, u32[]{:S(2)}) collective-permute-start(bf16[1,32,256]{2,1,0:T(8,128)(2,1)S(1)} %get-tuple-element.2), channel_id=1, source_target_pairs={{1,0},{3,2},{5,4},{7,6},{9,8},{11,10},{13,12},{15,14},{17,16},{19,... | collective-permute-start | bytes 49160 | tf_op jit(solution)/shard_map/ppermute | solution.py:20
  25.3 7.1 %all-to-all-start.2 = ((bf16[1,8,64]{2,0,1:T(2,128)(2,1)}), bf16[1,8,64]{2,0,1:T(2,128)(2,1)S(1)}, u32[]{:S(2)}, u32[]{:S(2)}) async-start(bf16[1,8,64]{2,0,1:T(2,128)(2,1)} %reshape.250), calls=%async_computation.2 | async-start | bytes 8192 | tf_op jit(solution)/shard_map/all_to_all | solution.py:121
  34.4 2.7 %collective-permute-start.2 = (bf16[1,32,256]{2,1,0:T(8,128)(2,1)S(1)}, bf16[1,32,256]{2,1,0:T(8,128)(2,1)S(1)}, u32[]{:S(2)}, u32[]{:S(2)}) collective-permute-start(bf16[1,32,256]{2,1,0:T(8,128)(2,1)S(1)} %get-tuple-element.40), channel_id=1, source_target_pairs={{0,1},{2,3},{4,5},{6,7},{8,9},{10,11},{12,13},{14,15},{16,17},{18,... | collective-permute-start | bytes 49160 | tf_op jit(solution)/shard_map/ppermute | solution.py:19
  37.2 1.3 %collective-permute-start.3 = (bf16[1,32,256]{2,1,0:T(8,128)(2,1)S(1)}, bf16[1,32,256]{2,1,0:T(8,128)(2,1)S(1)}, u32[]{:S(2)}, u32[]{:S(2)}) collective-permute-start(bf16[1,32,256]{2,1,0:T(8,128)(2,1)S(1)} %get-tuple-element.41), channel_id=1, source_target_pairs={{1,0},{3,2},{5,4},{7,6},{9,8},{11,10},{13,12},{15,14},{17,16},{19,... | collective-permute-start | bytes 49160 | tf_op jit(solution)/shard_map/ppermute | solution.py:20
  39.2 1.1 %collective-permute-done.3 = bf16[1,32,256]{2,1,0:T(8,128)(2,1)S(1)} collective-permute-done((bf16[1,32,256]{2,1,0:T(8,128)(2,1)S(1)}, bf16[1,32,256]{2,1,0:T(8,128)(2,1)S(1)}, u32[]{:S(2)}, u32[]{:S(2)}) %collective-permute-start.3) | collective-permute-done | bytes 16416 | tf_op jit(solution)/shard_map/ppermute | solution.py:20
  42.1 2.1 %collective-permute-start.4 = (bf16[1,32,256]{2,1,0:T(8,128)(2,1)S(1)}, bf16[1,32,256]{2,1,0:T(8,128)(2,1)S(1)}, u32[]{:S(2)}, u32[]{:S(2)}) collective-permute-start(bf16[1,32,256]{2,1,0:T(8,128)(2,1)S(1)} %get-tuple-element.38), channel_id=1, source_target_pairs={{0,1},{2,3},{4,5},{6,7},{8,9},{10,11},{12,13},{14,15},{16,17},{18,... | collective-permute-start | bytes 49160 | tf_op jit(solution)/shard_map/ppermute | solution.py:19
  44.1 1.3 %collective-permute-start.5 = (bf16[1,32,256]{2,1,0:T(8,128)(2,1)S(1)}, bf16[1,32,256]{2,1,0:T(8,128)(2,1)S(1)}, u32[]{:S(2)}, u32[]{:S(2)}) collective-permute-start(bf16[1,32,256]{2,1,0:T(8,128)(2,1)S(1)} %get-tuple-element.39), channel_id=1, source_target_pairs={{1,0},{3,2},{5,4},{7,6},{9,8},{11,10},{13,12},{15,14},{17,16},{19,... | collective-permute-start | bytes 49160 | tf_op jit(solution)/shard_map/ppermute | solution.py:20
  45.5 5.7 %all-to-all-start.1 = ((bf16[1,8,64]{2,0,1:T(2,128)(2,1)}), bf16[1,8,64]{2,0,1:T(2,128)(2,1)S(1)}, u32[]{:S(2)}, u32[]{:S(2)}) async-start(bf16[1,8,64]{2,0,1:T(2,128)(2,1)} %convert_element_type.145), calls=%async_computation.1 | async-start | bytes 8192 | tf_op jit(solution)/shard_map/all_to_all | solution.py:120
  53.8 2.7 %collective-permute-start.6 = (bf16[1,32,256]{2,1,0:T(8,128)(2,1)S(1)}, bf16[1,32,256]{2,1,0:T(8,128)(2,1)S(1)}, u32[]{:S(2)}, u32[]{:S(2)}) collective-permute-start(bf16[1,32,256]{2,1,0:T(8,128)(2,1)S(1)} %get-tuple-element.36), channel_id=1, source_target_pairs={{0,1},{2,3},{4,5},{6,7},{8,9},{10,11},{12,13},{14,15},{16,17},{18,... | collective-permute-start | bytes 49160 | tf_op jit(solution)/shard_map/ppermute | solution.py:19
  56.6 1.3 %collective-permute-start.7 = (bf16[1,32,256]{2,1,0:T(8,128)(2,1)S(1)}, bf16[1,32,256]{2,1,0:T(8,128)(2,1)S(1)}, u32[]{:S(2)}, u32[]{:S(2)}) collective-permute-start(bf16[1,32,256]{2,1,0:T(8,128)(2,1)S(1)} %get-tuple-element.37), channel_id=1, source_target_pairs={{1,0},{3,2},{5,4},{7,6},{9,8},{11,10},{13,12},{15,14},{17,16},{19,... | collective-permute-start | bytes 49160 | tf_op jit(solution)/shard_map/ppermute | solution.py:20
  57.9 5.7 %all-to-all-start = ((bf16[1,8,64,256]{3,2,0,1:T(8,128)(2,1)}), bf16[1,8,64,256]{3,2,0,1:T(8,128)(2,1)S(1)}, u32[]{:S(2)}, u32[]{:S(2)}) async-start(bf16[1,8,64,256]{3,2,0,1:T(8,128)(2,1)} %bitcast.61), calls=%async_computation | async-start | bytes 524288 | tf_op jit(solution)/shard_map/all_to_all | solution.py:113
  67.0 6.8 %all-to-all-done = bf16[1,8,64,256]{3,2,0,1:T(8,128)(2,1)S(1)} async-done(((bf16[1,8,64,256]{3,2,0,1:T(8,128)(2,1)}), bf16[1,8,64,256]{3,2,0,1:T(8,128)(2,1)S(1)}, u32[]{:S(2)}, u32[]{:S(2)}) %all-to-all-start) | async-done | bytes 262176 | tf_op jit(solution)/shard_map/all_to_all | solution.py:113
  74.8 1.8 %copy.70 = bf16[8,64,8,32]{3,0,2,1:T(8,128)(2,1)S(1)} copy(bf16[8,64,8,32]{1,0,3,2:T(8,128)(2,1)S(1)} %add_convert_fusion) | data formatting | bytes 524288 | tf_op jit(solution)/shard_map/convert_element_type | solution.py:67
  77.2 2.7 %copy.71 = bf16[8,64,8,32]{3,0,2,1:T(8,128)(2,1)} copy(bf16[8,64,8,32]{1,0,3,2:T(8,128)(2,1)S(1)} %reshape_reshape.7) | data formatting | bytes 524288 | tf_op jit(solution)/shard_map/reshape;reshape | solution.py:72
  79.9 1.9 %fusion.205 = f32[64,8,8,8]{2,3,1,0:T(8,128)S(1)} fusion(bf16[8,64,8,32]{3,0,2,1:T(8,128)(2,1)S(1)} %copy.70, bf16[8,64,8,32]{3,0,2,1:T(8,128)(2,1)} %copy.71), kind=kOutput, calls=%fused_computation.340 | convolution fusion | flops 2097152 | bytes 655360 | tf_op jit(solution)/shard_map/fkhd,gkhd->khfg/dot_general | solution.py:69
  81.8 1.1 %copy.72 = f32[64,8,8,8]{0,3,2,1:T(8,128)S(1)} copy(f32[64,8,8,8]{2,3,1,0:T(8,128)S(1)} %fusion.205) | data formatting | bytes 262144 | tf_op jit(solution)/shard_map/fkhd,gkhd->khfg/dot_general | solution.py:69
  82.9 1.2 %fusion.204 = (f32[64,8,8]{0,2,1:T(8,128)S(1)}, f32[64,8,8,8]{0,3,2,1:T(8,128)S(1)}) fusion(f32[64,8,8,8]{0,3,2,1:T(8,128)S(1)} %copy.72, pred[64,8]{0,1:T(8,128)(4,1)S(1)} %compare_bitcast_fusion), kind=kOutput, calls=%fused_computation.339 | output fusion | flops 131079 | bytes 279040 | tf_op jit(solution)/shard_map/sub | solution.py:77
  84.2 1.6 %copy.74 = bf16[64,8,8,8]{3,2,1,0:T(8,128)(2,1)S(1)} copy(bf16[64,8,8,8]{0,3,2,1:T(8,128)(2,1)S(1)} %divide_convert_fusion.16) | data formatting | bytes 131072 | tf_op jit(solution)/shard_map/convert_element_type | solution.py:77
  86.4 1.8 %copy.73 = bf16[8,64,8,32]{3,0,2,1:T(8,128)(2,1)S(1)} copy(bf16[8,64,8,32]{1,0,3,2:T(8,128)(2,1)S(1)} %reshape_reshape.6) | data formatting | bytes 524288 | tf_op jit(solution)/shard_map/reshape;reshape | solution.py:79
  88.9 1.2 %copy.75 = bf16[8,64,8,32]{1,3,2,0:T(8,128)(2,1)S(1)} copy(bf16[8,64,8,32]{3,0,2,1:T(8,128)(2,1)S(1)} %fusion.1) | data formatting | bytes 524288 | tf_op jit(solution)/shard_map/convert_element_type | solution.py:81
  90.1 0.9 copy.76
  91.0 3.6 %all-to-all-start.3 = ((bf16[8,1,64,256]{3,2,1,0:T(8,128)(2,1)}), bf16[8,1,64,256]{3,2,1,0:T(8,128)(2,1)S(1)}, u32[]{:S(2)}, u32[]{:S(2)}) async-start(bf16[8,1,64,256]{3,2,1,0:T(8,128)(2,1)} %copy.76), calls=%async_computation.3 | async-start | bytes 524288 | tf_op jit(solution)/shard_map/all_to_all | solution.py:155
  94.6 1.0 fusion.138
  95.7 1.7 %fusion.24 = bf16[256,128]{1,0:T(8,128)(2,1)} fusion(f32[256,128]{1,0:T(8,128)S(1)} %fusion.138, f32[256,128]{1,0:T(8,128)S(1)} %copy-done.16, bf16[256,256]{1,0:T(8,128)(2,1)S(1)} %bitcast.277, bf16[256,128]{1,0:T(8,128)(2,1)S(1)} %copy-done.5, f32[256,256]{1,0:T(8,128)S(1)} %copy-done.7, bf16[3,3,256,128]{3,2,1,0:T(8,128)(2,1)} %param.29), kind=kOutput, calls=%fused_computation.68 | convolution fusion | flops 17137664 | bytes 720896 | tf_op jit(solution)/shard_map/dot_general | solution.py:56
  97.3 6.5 %all-to-all-done.3 = bf16[8,1,64,256]{3,2,1,0:T(8,128)(2,1)S(1)} async-done(((bf16[8,1,64,256]{3,2,1,0:T(8,128)(2,1)}), bf16[8,1,64,256]{3,2,1,0:T(8,128)(2,1)S(1)}, u32[]{:S(2)}, u32[]{:S(2)}) %all-to-all-start.3) | async-done | bytes 262176 | tf_op jit(solution)/shard_map/all_to_all | solution.py:155
  103.8 1.9 %fusion.12 = bf16[1,512,256]{2,1,0:T(8,128)(2,1)} fusion(bf16[512,256]{1,0:T(8,128)(2,1)S(1)} %bitcast.244, bf16[256,256]{1,0:T(8,128)(2,1)S(1)} %copy-done.15, bf16[1,512,256]{2,1,0:T(8,128)(2,1)} %param.17), kind=kOutput, calls=%fused_computation.27 | convolution fusion | flops 67502080 | bytes 917504 | tf_op jit(solution)/shard_map/dot_general | solution.py:157
  (151 shorter events, 25.3 us)
Async XLA Ops:
  0.6 0.9 copy-start
  0.6 4.3 %copy-start.19 = (s32[1,512]{1,0:T(1,128)S(1)}, s32[1,512]{1,0:T(1,128)}, u32[]{:S(2)}) copy-start(s32[1,512]{1,0:T(1,128)} %param.18) | copy-start | bytes 6148
  0.7 6.2 %copy-start.9 = (bf16[1,8,32,256]{3,2,1,0:T(8,128)(2,1)S(1)}, bf16[1,8,32,256]{3,2,1,0:T(8,128)(2,1)}, u32[]{:S(2)}) copy-start(bf16[1,8,32,256]{3,2,1,0:T(8,128)(2,1)} %param.15) | copy-start | bytes 393220
  0.7 6.2 %copy-start.10 = (bf16[256,256]{1,0:T(8,128)(2,1)S(1)}, bf16[256,256]{1,0:T(8,128)(2,1)}, u32[]{:S(2)}) copy-start(bf16[256,256]{1,0:T(8,128)(2,1)} %param.20) | copy-start | bytes 393220
  9.9 1.0 copy-start.11
  19.9 0.8 copy-start.18
  19.9 1.1 %copy-start.3 = (bf16[1,8,32,128]{3,2,1,0:T(8,128)(2,1)S(1)}, bf16[1,8,32,128]{3,2,1,0:T(8,128)(2,1)}, u32[]{:S(2)}) copy-start(bf16[1,8,32,128]{3,2,1,0:T(8,128)(2,1)} %param.16) | copy-start | bytes 196612
  19.9 4.7 %copy-start.20 = (s32[512]{0:T(512)S(1)}, s32[512]{0:T(512)}, u32[]{:S(2)}) copy-start(s32[512]{0:T(512)} %param.19) | copy-start | bytes 6148
  20.7 11.8 %copy-start.1 = (bf16[3,3,256,256]{3,2,1,0:T(8,128)(2,1)S(1)}, bf16[3,3,256,256]{3,2,1,0:T(8,128)(2,1)}, u32[]{:S(2)}) copy-start(bf16[3,3,256,256]{3,2,1,0:T(8,128)(2,1)} %param.28) | copy-start | bytes 3538948
  21.0 11.4 %collective-permute-start = (bf16[1,32,256]{2,1,0:T(8,128)(2,1)S(1)}, bf16[1,32,256]{2,1,0:T(8,128)(2,1)S(1)}, u32[]{:S(2)}, u32[]{:S(2)}) collective-permute-start(bf16[1,32,256]{2,1,0:T(8,128)(2,1)S(1)} %get-tuple-element.42), channel_id=1, source_target_pairs={{0,1},{2,3},{4,5},{6,7},{8,9},{10,11},{12,13},{14,15},{16,17},{18,... | collective-permute-start | bytes 49160 | tf_op jit(solution)/shard_map/ppermute | solution.py:19
  23.3 9.1 %collective-permute-start.1 = (bf16[1,32,256]{2,1,0:T(8,128)(2,1)S(1)}, bf16[1,32,256]{2,1,0:T(8,128)(2,1)S(1)}, u32[]{:S(2)}, u32[]{:S(2)}) collective-permute-start(bf16[1,32,256]{2,1,0:T(8,128)(2,1)S(1)} %get-tuple-element.2), channel_id=1, source_target_pairs={{1,0},{3,2},{5,4},{7,6},{9,8},{11,10},{13,12},{15,14},{17,16},{19,... | collective-permute-start | bytes 49160 | tf_op jit(solution)/shard_map/ppermute | solution.py:20
  25.3 20.1 %all-to-all-start.2 = ((bf16[1,8,64]{2,0,1:T(2,128)(2,1)}), bf16[1,8,64]{2,0,1:T(2,128)(2,1)S(1)}, u32[]{:S(2)}, u32[]{:S(2)}) async-start(bf16[1,8,64]{2,0,1:T(2,128)(2,1)} %reshape.250), calls=%async_computation.2 | async-start | bytes 8192 | tf_op jit(solution)/shard_map/all_to_all | solution.py:121
  34.1 6.3 %copy-start.2 = (bf16[3,3,256,128]{3,2,1,0:T(8,128)(2,1)S(1)}, bf16[3,3,256,128]{3,2,1,0:T(8,128)(2,1)}, u32[]{:S(2)}) copy-start(bf16[3,3,256,128]{3,2,1,0:T(8,128)(2,1)} %param.29) | copy-start | bytes 1769476
  34.4 4.8 %collective-permute-start.2 = (bf16[1,32,256]{2,1,0:T(8,128)(2,1)S(1)}, bf16[1,32,256]{2,1,0:T(8,128)(2,1)S(1)}, u32[]{:S(2)}, u32[]{:S(2)}) collective-permute-start(bf16[1,32,256]{2,1,0:T(8,128)(2,1)S(1)} %get-tuple-element.40), channel_id=1, source_target_pairs={{0,1},{2,3},{4,5},{6,7},{8,9},{10,11},{12,13},{14,15},{16,17},{18,... | collective-permute-start | bytes 49160 | tf_op jit(solution)/shard_map/ppermute | solution.py:19
  37.2 3.1 %collective-permute-start.3 = (bf16[1,32,256]{2,1,0:T(8,128)(2,1)S(1)}, bf16[1,32,256]{2,1,0:T(8,128)(2,1)S(1)}, u32[]{:S(2)}, u32[]{:S(2)}) collective-permute-start(bf16[1,32,256]{2,1,0:T(8,128)(2,1)S(1)} %get-tuple-element.41), channel_id=1, source_target_pairs={{1,0},{3,2},{5,4},{7,6},{9,8},{11,10},{13,12},{15,14},{17,16},{19,... | collective-permute-start | bytes 49160 | tf_op jit(solution)/shard_map/ppermute | solution.py:20
  42.0 11.1 %copy-start.4 = (bf16[256,128]{1,0:T(8,128)(2,1)}, bf16[256,128]{1,0:T(8,128)(2,1)S(1)}, u32[]{:S(2)}) copy-start(bf16[256,128]{1,0:T(8,128)(2,1)S(1)} %fusion.25) | copy-start | bytes 196612
  42.1 9.1 %collective-permute-start.4 = (bf16[1,32,256]{2,1,0:T(8,128)(2,1)S(1)}, bf16[1,32,256]{2,1,0:T(8,128)(2,1)S(1)}, u32[]{:S(2)}, u32[]{:S(2)}) collective-permute-start(bf16[1,32,256]{2,1,0:T(8,128)(2,1)S(1)} %get-tuple-element.38), channel_id=1, source_target_pairs={{0,1},{2,3},{4,5},{6,7},{8,9},{10,11},{12,13},{14,15},{16,17},{18,... | collective-permute-start | bytes 49160 | tf_op jit(solution)/shard_map/ppermute | solution.py:19
  44.1 7.0 %collective-permute-start.5 = (bf16[1,32,256]{2,1,0:T(8,128)(2,1)S(1)}, bf16[1,32,256]{2,1,0:T(8,128)(2,1)S(1)}, u32[]{:S(2)}, u32[]{:S(2)}) collective-permute-start(bf16[1,32,256]{2,1,0:T(8,128)(2,1)S(1)} %get-tuple-element.39), channel_id=1, source_target_pairs={{1,0},{3,2},{5,4},{7,6},{9,8},{11,10},{13,12},{15,14},{17,16},{19,... | collective-permute-start | bytes 49160 | tf_op jit(solution)/shard_map/ppermute | solution.py:20
  45.5 12.4 %all-to-all-start.1 = ((bf16[1,8,64]{2,0,1:T(2,128)(2,1)}), bf16[1,8,64]{2,0,1:T(2,128)(2,1)S(1)}, u32[]{:S(2)}, u32[]{:S(2)}) async-start(bf16[1,8,64]{2,0,1:T(2,128)(2,1)} %convert_element_type.145), calls=%async_computation.1 | async-start | bytes 8192 | tf_op jit(solution)/shard_map/all_to_all | solution.py:120
  53.8 9.8 %collective-permute-start.6 = (bf16[1,32,256]{2,1,0:T(8,128)(2,1)S(1)}, bf16[1,32,256]{2,1,0:T(8,128)(2,1)S(1)}, u32[]{:S(2)}, u32[]{:S(2)}) collective-permute-start(bf16[1,32,256]{2,1,0:T(8,128)(2,1)S(1)} %get-tuple-element.36), channel_id=1, source_target_pairs={{0,1},{2,3},{4,5},{6,7},{8,9},{10,11},{12,13},{14,15},{16,17},{18,... | collective-permute-start | bytes 49160 | tf_op jit(solution)/shard_map/ppermute | solution.py:19
  56.6 7.1 %collective-permute-start.7 = (bf16[1,32,256]{2,1,0:T(8,128)(2,1)S(1)}, bf16[1,32,256]{2,1,0:T(8,128)(2,1)S(1)}, u32[]{:S(2)}, u32[]{:S(2)}) collective-permute-start(bf16[1,32,256]{2,1,0:T(8,128)(2,1)S(1)} %get-tuple-element.37), channel_id=1, source_target_pairs={{1,0},{3,2},{5,4},{7,6},{9,8},{11,10},{13,12},{15,14},{17,16},{19,... | collective-permute-start | bytes 49160 | tf_op jit(solution)/shard_map/ppermute | solution.py:20
  57.9 15.9 %all-to-all-start = ((bf16[1,8,64,256]{3,2,0,1:T(8,128)(2,1)}), bf16[1,8,64,256]{3,2,0,1:T(8,128)(2,1)S(1)}, u32[]{:S(2)}, u32[]{:S(2)}) async-start(bf16[1,8,64,256]{3,2,0,1:T(8,128)(2,1)} %bitcast.61), calls=%async_computation | async-start | bytes 524288 | tf_op jit(solution)/shard_map/all_to_all | solution.py:113
  65.5 8.3 %copy-start.12 = (bf16[256,256]{1,0:T(8,128)(2,1)S(1)}, bf16[256,256]{1,0:T(8,128)(2,1)}, u32[]{:S(2)}) copy-start(bf16[256,256]{1,0:T(8,128)(2,1)} %param.24) | copy-start | bytes 393220
  74.7 1.8 %copy-start.13 = (bf16[256,256]{1,0:T(8,128)(2,1)S(1)}, bf16[256,256]{1,0:T(8,128)(2,1)}, u32[]{:S(2)}) copy-start(bf16[256,256]{1,0:T(8,128)(2,1)} %param.25) | copy-start | bytes 393220
  82.9 2.8 %copy-start.14 = (bf16[256,256]{1,0:T(8,128)(2,1)S(1)}, bf16[256,256]{1,0:T(8,128)(2,1)}, u32[]{:S(2)}) copy-start(bf16[256,256]{1,0:T(8,128)(2,1)} %param.26) | copy-start | bytes 393220
  88.9 5.8 %copy-start.8 = (bf16[8,32,256]{2,1,0:T(8,128)(2,1)S(1)}, bf16[8,32,256]{2,1,0:T(8,128)(2,1)}, u32[]{:S(2)}) copy-start(bf16[8,32,256]{2,1,0:T(8,128)(2,1)} %get-tuple-element.8) | copy-start | bytes 393220
  90.0 5.6 %copy-start.5 = (bf16[256,128]{1,0:T(8,128)(2,1)S(1)}, bf16[256,128]{1,0:T(8,128)(2,1)}, u32[]{:S(2)}) copy-start(bf16[256,128]{1,0:T(8,128)(2,1)} %copy-done.4) | copy-start | bytes 196612
  90.0 5.6 %copy-start.7 = (f32[256,256]{1,0:T(8,128)S(1)}, f32[256,256]{1,0:T(8,128)}, u32[]{:S(2)}) copy-start(f32[256,256]{1,0:T(8,128)} %copy-done.6) | copy-start | bytes 786436
  90.1 5.6 %copy-start.16 = (f32[256,128]{1,0:T(8,128)S(1)}, f32[256,128]{1,0:T(8,128)}, u32[]{:S(2)}) copy-start(f32[256,128]{1,0:T(8,128)} %convolution_add_fusion.16) | copy-start | bytes 393220
  90.1 5.6 %copy-start.17 = (bf16[8,32,256]{2,1,0:T(8,128)(2,1)S(1)}, bf16[8,32,256]{2,1,0:T(8,128)(2,1)}, u32[]{:S(2)}) copy-start(bf16[8,32,256]{2,1,0:T(8,128)(2,1)} %get-tuple-element.28) | copy-start | bytes 393220
  90.1 13.7 %copy-start.15 = (bf16[256,256]{1,0:T(8,128)(2,1)S(1)}, bf16[256,256]{1,0:T(8,128)(2,1)}, u32[]{:S(2)}) copy-start(bf16[256,256]{1,0:T(8,128)(2,1)} %param.27) | copy-start | bytes 393220
  91.0 12.8 %all-to-all-start.3 = ((bf16[8,1,64,256]{3,2,1,0:T(8,128)(2,1)}), bf16[8,1,64,256]{3,2,1,0:T(8,128)(2,1)S(1)}, u32[]{:S(2)}, u32[]{:S(2)}) async-start(bf16[8,1,64,256]{3,2,1,0:T(8,128)(2,1)} %copy.76), calls=%async_computation.3 | async-start | bytes 524288 | tf_op jit(solution)/shard_map/all_to_all | solution.py:155
  (1 other events, 0.7 us)
where the time goes:
time: 107 us; the launch traced here: 106 us
  starting transfers between devices  37.2 us (35%)
  matrix products  24.6 us (23%)
  local copies, waits for them, and re-layouts  16.6 us (16%)
  waiting for transfers between devices  14.3 us (13%)
  blocking collectives  6.3 us (6%)
  other arithmetic  5.05 us (5%)
  between operations  1.63 us (2%)
    ppermute x4, starting transfers between devices, with_halo(): before = lax.ppermute(last, axis, up)  9.89 us
    dot_general x36, matrix products, conv_rows(): jnp.dot(window.reshape(rows * columns, -1), weight[row_shift, col_shift],...  9.4 us
    all_to_all x1, starting transfers between devices, on_device(): lax.all_to_all(anchor_split, 'frame', split_axis=1, concat_axis=0, tiled=...  7.06 us
    all_to_all x1, waiting for transfers between devices, on_device(): lax.all_to_all(local_tokens.reshape(1, frames, per_device, channels), 'fr...  6.77 us
    all_to_all x1, waiting for transfers between devices, on_device(): lax.all_to_all(track_result, 'frame', split_axis=0, concat_axis=1, tiled=...  6.47 us
    all_to_all x1, starting transfers between devices, on_device(): lax.all_to_all(local_tokens.reshape(1, frames, per_device, channels), 'fr...  5.72 us
    all_to_all x1, starting transfers between devices, on_device(): lax.all_to_all(seen_split, 'frame', split_axis=1, concat_axis=0, tiled=True)  5.72 us
    ppermute x4, starting transfers between devices, with_halo(): after = lax.ppermute(first, axis, down)  5.17 us
  transfers between devices with their start and end apart: 12, of which 3 were waited for; matrix products, arithmetic and copies ran while one was open for 12% of the time, Pallas kernels for 0%

commit v1 on v0

v1 whole, which is shorter than its diff:
```python
import jax
import jax.numpy as jnp
from jax import lax
from jax.experimental import pallas as pl
from jax.experimental.pallas import tpu as pltpu
from jax.sharding import PartitionSpec as P

HEADS = 8
ITERS = 2
LANES = 128
MASK_ROWS = 16
HIDDEN = -1e30

f32 = jnp.float32
bf16 = jnp.bfloat16
VMEM = pl.BlockSpec(memory_space=pltpu.VMEM)


def dot(a, b):
    return jnp.dot(a, b, preferred_element_type=f32)


def call(body, out, scratch, flops, *args, after=()):
    moved = sum(x.size * x.dtype.itemsize for x in args)
    return pl.pallas_call(
        lambda *refs: body(*refs[len(after) :]),
        out_shape=out,
        in_specs=[pl.BlockSpec(memory_space=pl.ANY)] * len(after) + [VMEM] * len(args),
        out_specs=jax.tree.map(lambda _: VMEM, out),
        scratch_shapes=scratch,
        compiler_params=pltpu.CompilerParams(vmem_limit_bytes=24 * 2**20),
        cost_estimate=pl.CostEstimate(flops=flops, bytes_accessed=moved, transcendentals=0),
    )(*after, *args)


def pack_body(tokens, visible, out):
    frames, rows, _ = out.shape
    share = tokens.shape[0] // frames
    flags = visible[...].astype(f32)
    for g in range(frames):
        part = tokens[g * share : (g + 1) * share, :]
        out[g, :share, :] = part[:, :LANES]
        out[g, share : 2 * share, :] = part[:, LANES:]
        first = g * share // LANES * LANES
        group = flags[:, first : first + LANES]
        out[g, 2 * share :, :] = jnp.broadcast_to(group, (MASK_ROWS, LANES)).astype(bf16)


def unpack(packed, share):
    frames = packed.shape[0]
    left = packed[:, :share, :].reshape(frames * share, LANES)
    right = packed[:, share : 2 * share, :].reshape(frames * share, LANES)
    return jnp.concatenate([left, right], axis=1)


def attend_body(
    tokens, visible, other, pixels, state, w_query, w_key, w_value, w_out, context, edge
):
    half, channels = tokens.shape
    frames = other.shape[0]
    share = half // frames
    head_dim = channels // HEADS
    rows = jnp.concatenate([tokens[...], unpack(other, share)], axis=0)
    key = dot(rows, w_key[...]).astype(bf16)
    value = dot(rows, w_value[...]).astype(bf16)
    query = dot(pixels[...], w_query[...]).astype(bf16)
    flags = [visible[...].astype(f32)]
    for first in range(0, half, LANES):
        flags.append(other[first // share, 2 * share :, :].astype(f32)[:1])
    bias = jnp.where(jnp.concatenate(flags, axis=1) > 0.5, 0.0, HIDDEN)
    head_of = lax.broadcasted_iota(jnp.int32, (1, channels), 1) // head_dim
    scale = head_dim**-0.5
    attended = jnp.zeros((pixels.shape[0], channels), f32)
    for head in range(HEADS):
        mine = head_of == head
        masked = jnp.where(mine, query, jnp.zeros_like(query))
        scores = lax.dot_general(
            masked, key, (((1,), (1,)), ((), ())), preferred_element_type=f32
        )
        scores = scores + bias
        top = jnp.max(scores, axis=1, keepdims=True)
        weights = jnp.exp((scores - top) * scale)
        total = jnp.sum(weights, axis=1, keepdims=True)
        summed = dot(weights.astype(bf16), value)
        attended = jnp.where(mine, summed / total, attended)
    context[...] = dot(attended.astype(bf16), w_out[...]).astype(bf16)
    count = edge.shape[0]
    start = pl.multiple_of((1 - lax.axis_index("band")) * (pixels.shape[0] - count), count)
    edge[:, :LANES] = state[pl.ds(start, count), :]
    edge[:, LANES:] = context[pl.ds(start, count), :]


def temporal_body(packed, query_frame, w_query, w_key, w_value, out, flag_cols, frame_cols):
    frames, share, channels = out.shape
    head_dim = channels // HEADS
    columns = -(-frames * HEADS // LANES) * LANES
    first = lax.axis_index("frame") * share
    group, start = first // LANES, pl.multiple_of(first % LANES, share)
    flags = packed[:, 2 * share :, :].reshape(frames * MASK_ROWS, LANES)
    flag_cols[...] = flags.astype(f32).T
    asked = query_frame[pl.ds(group, 1), :].astype(f32)
    frame_cols[...] = jnp.broadcast_to(asked, (LANES, LANES)).T
    flags = flag_cols[pl.ds(start, share), :]
    asked = frame_cols[pl.ds(start, share), :1]

    rows = unpack(packed, share)
    query = dot(rows, w_query[...]).astype(bf16).astype(f32).reshape(frames, share, channels)
    key = dot(rows, w_key[...]).astype(bf16).astype(f32).reshape(frames, share, channels)
    value = dot(rows, w_value[...]).astype(bf16).astype(f32).reshape(frames, share, channels)
    anchor = jnp.zeros((share, channels), f32)
    for f in range(frames):
        anchor = jnp.where(asked == f, query[f], anchor)

    head_of_row = lax.broadcasted_iota(jnp.int32, (channels, columns), 0) // head_dim
    column = lax.broadcasted_iota(jnp.int32, (channels, columns), 1)
    head_of_col = lax.broadcasted_iota(jnp.int32, (columns, channels), 1) // head_dim
    line = lax.broadcasted_iota(jnp.int32, (columns, channels), 0)
    scores = jnp.zeros((frames * share, columns), f32)
    for f in range(frames):
        joint = (query[f] + anchor).astype(bf16).astype(f32)
        product = (key * joint[None]).reshape(frames * share, channels)
        high = product.astype(bf16)
        low = (product - high.astype(f32)).astype(bf16)
        gather = jnp.where(column == head_of_row + f * HEADS, 1.0, 0.0).astype(bf16)
        scores = scores + dot(high, gather) + dot(low, gather)
    scores = scores.reshape(frames, share, columns) * head_dim**-0.5
    seen = [
        jnp.where(flags[:, g * MASK_ROWS : g * MASK_ROWS + 1] > 0.5, scores[g], HIDDEN)
        for g in range(frames)
    ]
    top = seen[0]
    for g in range(1, frames):
        top = jnp.maximum(top, seen[g])
    raised = [jnp.exp(s - top) for s in seen]
    total = raised[0]
    for g in range(1, frames):
        total = total + raised[g]
    weights = jnp.concatenate([r / total for r in raised], axis=0).astype(bf16)
    for f in range(frames):
        spread = jnp.where(line == head_of_col + f * HEADS, 1.0, 0.0).astype(bf16)
        wide = dot(weights, spread).reshape(frames, share, channels)
        out[f] = jnp.sum(wide * value, axis=0).astype(bf16)


def refine_body(state, context, halo, w_gates, w_cand, out, field, wide):
    taps, both, _ = w_gates.shape
    local, hidden = state.shape
    beyond = halo.shape[0]
    pixels = local + beyond
    width = (wide.shape[0] - pixels) // 2
    band = lax.axis_index("band")
    here = pl.multiple_of(band * beyond, beyond)
    there = pl.multiple_of((1 - band) * local, beyond)
    col = lax.broadcasted_iota(jnp.int32, (pixels, hidden), 0) % width
    wide[:width, :] = jnp.zeros((width, 3 * both), bf16)
    wide[width + pixels :, :] = jnp.zeros((width, 3 * both), bf16)

    def spread(values, lane):
        before = jnp.where(col == 0, 0.0, pltpu.roll(values, 1, 0))
        after = jnp.where(col == width - 1, 0.0, pltpu.roll(values, pixels - 1, 0))
        for c, shifted in enumerate((before, values, after)):
            first = c * both + lane
            wide[width : width + pixels, first : first + hidden] = shifted.astype(bf16)

    def conv(weight):
        rows = [wide[r * width : r * width + pixels, :] for r in range(3)]
        return dot(jnp.concatenate(rows, axis=1), weight[...].reshape(taps * both, -1))

    field[pl.ds(here, local), :] = context[...]
    field[pl.ds(there, beyond), :] = halo[:, hidden:]
    spread(field[...].astype(f32), hidden)
    field[pl.ds(here, local), :] = state[...]
    field[pl.ds(there, beyond), :] = halo[:, :hidden]
    now = field[...].astype(f32)
    for _ in range(ITERS):
        spread(now, 0)
        gates = conv(w_gates)
        update = jax.nn.sigmoid(gates[:, :hidden])
        reset = jax.nn.sigmoid(gates[:, hidden:])
        spread((reset * now).astype(bf16).astype(f32), 0)
        cand = jnp.tanh(conv(w_cand))
        now = ((1.0 - update) * now + update * cand).astype(bf16).astype(f32)
    field[...] = now.astype(bf16)
    out[...] = field[pl.ds(here, local), :]


def output_body(tokens, returned, w_out, out):
    out[...] = (tokens[...].astype(f32) + dot(returned[...], w_out[...])).astype(bf16)


def on_device(
    pixels,
    gru_state,
    tokens,
    visible,
    query_frame,
    pixel_query,
    pixel_key,
    pixel_value,
    pixel_out,
    time_query,
    time_key,
    time_value,
    time_out,
    gru_gates,
    gru_candidate,
):
    frames = lax.axis_size("frame")
    _, band_rows, width, channels = pixels.shape
    hidden = gru_state.shape[3]
    half = tokens.shape[1]
    share = half // frames
    local = band_rows * width
    beyond = 2 * ITERS * width
    assert lax.axis_size("band") == 2 and channels == 2 * LANES and hidden == LANES
    swap = [(0, 1), (1, 0)]
    local_tokens = tokens[0]
    flat_pixels = pixels.reshape(local, channels)
    flat_state = gru_state.reshape(local, hidden)

    packed = call(
        pack_body,
        jax.ShapeDtypeStruct((frames, 2 * share + MASK_ROWS, LANES), bf16),
        [],
        0,
        local_tokens,
        visible,
    )
    other = lax.ppermute(packed, "band", swap)
    arrived = lax.all_to_all(packed, "frame", split_axis=0, concat_axis=0, tiled=True)

    context, edge = call(
        attend_body,
        (
            jax.ShapeDtypeStruct((local, hidden), bf16),
            jax.ShapeDtypeStruct((beyond, 2 * hidden), bf16),
        ),
        [],
        4 * local * 2 * half * channels * HEADS,
        local_tokens,
        visible,
        other,
        flat_pixels,
        flat_state,
        pixel_query,
        pixel_key,
        pixel_value,
        pixel_out,
    )
    halo = lax.ppermute(edge, "band", swap)

    attended = call(
        temporal_body,
        jax.ShapeDtypeStruct((frames, share, channels), bf16),
        [
            pltpu.VMEM((LANES, frames * MASK_ROWS), f32),
            pltpu.VMEM((LANES, LANES), f32),
        ],
        6 * half * channels * channels * 4,
        arrived,
        query_frame.reshape(half // LANES, LANES),
        time_query,
        time_key,
        time_value,
        after=(edge,),
    )
    returned = lax.all_to_all(attended, "frame", split_axis=0, concat_axis=0, tiled=True)

    refined = call(
        refine_body,
        jax.ShapeDtypeStruct((local, hidden), bf16),
        [
            pltpu.VMEM((local + beyond, hidden), bf16),
            pltpu.VMEM((local + beyond + 2 * width, 6 * hidden), bf16),
        ],
        2 * (local + beyond) * 9 * 2 * hidden * 3 * hidden * ITERS,
        flat_state,
        context,
        halo,
        gru_gates.reshape(9, 2 * hidden, 2 * hidden),
        gru_candidate.reshape(9, 2 * hidden, hidden),
    )
    track_out = call(
        output_body,
        jax.ShapeDtypeStruct((half, channels), bf16),
        [],
        2 * half * channels * channels,
        local_tokens,
        returned.reshape(half, channels),
        time_out,
    )
    return refined.reshape(gru_state.shape), track_out[None]


def solution(mesh):
    placed = (
        P(("clip", "frame"), "band", None, None),
        P(("clip", "frame"), "band", None, None),
        P(("clip", "frame"), "band", None),
        P(("clip", "frame"), "band"),
        P(("clip", "band")),
        P(),
        P(),
        P(),
        P(),
        P(),
        P(),
        P(),
        P(),
        P(),
        P(),
    )
    return jax.shard_map(
        on_device,
        mesh=mesh,
        in_specs=placed,
        out_specs=(P(("clip", "frame"), "band", None, None), P(("clip", "frame"), "band", None)),
        check_vma=False,
    )
```

time: 107 us -> 44 us (0.41)
  matrix products: 24.6 us -> 0 us
  starting transfers between devices: 37.2 us -> 13.3 us
  Pallas kernels: 0 us -> 14.7 us
  waiting for transfers between devices: 14.3 us -> 6.08 us
  local copies, waits for them, and re-layouts: 16.6 us -> 8.6 us
  blocking collectives: 6.3 us -> 0 us
  other arithmetic: 5.05 us -> 0 us
    dot_general x62 -> x0, matrix products: 24.6 us -> none  [the longest x36 9.4 us: conv_rows(): jnp.dot(window.reshape(rows * columns, -1), weight[row_shift, col_shift],...]
    ppermute x8 -> x2, starting transfers between devices: 15.1 us -> 0.01 us  [the longest x1 0.01 us: on_device(): other = lax.ppermute(packed, 'band', swap)]
    pallas_call x0 -> x5, Pallas kernels: none -> 14.7 us  [call(): pl.pallas_call(lambda *refs: body(*refs[len(after):]), out_shape=out, in_...]
    all_to_all x4 -> x2, waiting for transfers between devices: 13.2 us -> 3.05 us  [the longest x1 3.05 us: on_device(): lax.all_to_all(attended, 'frame', split_axis=0, concat_axis=0, tiled=True)]
    all_to_all x4 -> x2, starting transfers between devices: 22.1 us -> 13.3 us  [the longest x1 7.28 us: on_device(): lax.all_to_all(packed, 'frame', split_axis=0, concat_axis=0, tiled=True)]
    unnamed x42 -> x38, local copies, waits for them, and re-layouts: 1.96 us -> 8.6 us
    all_gather x3 -> x0, blocking collectives: 6.3 us -> none  [the longest x1 2.26 us: on_device(): lax.all_gather(key_local, 'band', axis=0, tiled=True)]
    another operation x5 -> x0, local copies, waits for them, and re-layouts: 5.9 us -> none  [the longest x2 2.98 us: temporal_core(): key_part.reshape(shaped)]
  transfers between devices with their start and end apart: 12 -> 4, of which waited for: 3 -> 3; matrix products, arithmetic and copies ran while one was open for 12% -> 0% of each run, Pallas kernels for 0% -> 20%
where the time goes in v1:
time: 44 us; the launch traced here: 43.4 us
  Pallas kernels  14.7 us (33%)
  starting transfers between devices  13.3 us (30%)
  local copies, waits for them, and re-layouts  8.6 us (20%)
  waiting for transfers between devices  6.08 us (14%)
  between operations  0.75 us (2%)
    pallas_call x5, Pallas kernels, call(): pl.pallas_call(lambda *refs: body(*refs[len(after):]), out_shape=out, in_...  14.7 us
    unnamed x38, local copies, waits for them, and re-layouts  8.6 us
    all_to_all x1, starting transfers between devices, on_device(): lax.all_to_all(packed, 'frame', split_axis=0, concat_axis=0, tiled=True)  7.28 us
    all_to_all x1, starting transfers between devices, on_device(): lax.all_to_all(attended, 'frame', split_axis=0, concat_axis=0, tiled=True)  6 us
    all_to_all x1, waiting for transfers between devices, on_device(): lax.all_to_all(attended, 'frame', split_axis=0, concat_axis=0, tiled=True)  3.05 us
    ppermute x1, waiting for transfers between devices, on_device(): other = lax.ppermute(packed, 'band', swap)  1.78 us
    ppermute x1, waiting for transfers between devices, on_device(): halo = lax.ppermute(edge, 'band', swap)  1.25 us
  transfers between devices with their start and end apart: 4, of which 3 were waited for; matrix products, arithmetic and copies ran while one was open for 0% of the time, Pallas kernels for 20%

profile of v1, /device:TPU:0, one launch (start us, length us, event | category | flops | bytes accessed | tf_op | source)
XLA Modules:
  0.0 43.4 jit_solution(13916326576558837711)
XLA Ops:
  0.6 0.0 copy-start
  0.6 0.9 %copy-done = bf16[1,512,256]{2,1,0:T(8,128)(2,1)S(1)} copy-done((bf16[1,512,256]{2,1,0:T(8,128)(2,1)S(1)}, bf16[1,512,256]{2,1,0:T(8,128)(2,1)}, u32[]{:S(2)}) %copy-start) | copy-done | bytes 262168
  1.6 0.7 %copy-done.4 = s32[1,512]{1,0:T(1,128)S(1)} copy-done((s32[1,512]{1,0:T(1,128)S(1)}, s32[1,512]{1,0:T(1,128)}, u32[]{:S(2)}) %copy-start.4) | copy-done | bytes 2072
  2.3 0.7 %shard_map.158 = bf16[8,144,128]{2,1,0:T(8,128)(2,1)} custom-call(bf16[512,256]{1,0:T(8,128)(2,1)S(1)} %bitcast.9, s32[1,512]{1,0:T(1,128)S(1)} %copy-done.4), custom_call_target="tpu_custom_call" | custom-call | bytes 264192 | tf_op jit(solution)/shard_map/pallas_call | solution.py:25
  3.0 7.3 %all-to-all-start = ((bf16[8,144,128]{2,1,0:T(8,128)(2,1)}), bf16[8,144,128]{2,1,0:T(8,128)(2,1)S(1)}, u32[]{:S(2)}, u32[]{:S(2)}) async-start(bf16[8,144,128]{2,1,0:T(8,128)(2,1)} %shard_map.158), calls=%async_computation | async-start | bytes 589824 | tf_op jit(solution)/shard_map/all_to_all | solution.py:230
  10.3 0.0 collective-permute-start
  10.3 1.8 %collective-permute-done.refs_2_ = bf16[8,144,128]{2,1,0:T(8,128)(2,1)S(1)} collective-permute-done((bf16[8,144,128]{2,1,0:T(8,128)(2,1)}, bf16[8,144,128]{2,1,0:T(8,128)(2,1)S(1)}, u32[]{:S(2)}, u32[]{:S(2)}) %collective-permute-start) | collective-permute-done | bytes 294944 | tf_op jit(solution)/shard_map/ppermute | solution.py:229
  12.1 0.9 %copy-done.1 = bf16[1,512,256]{2,1,0:T(8,128)(2,1)S(1)} copy-done((bf16[1,512,256]{2,1,0:T(8,128)(2,1)S(1)}, bf16[1,512,256]{2,1,0:T(8,128)(2,1)}, u32[]{:S(2)}) %copy-start.1) | copy-done | bytes 262168
  13.0 0.7 %copy-done.5 = s32[1,512]{1,0:T(1,128)S(1)} copy-done((s32[1,512]{1,0:T(1,128)S(1)}, s32[1,512]{1,0:T(1,128)}, u32[]{:S(2)}) %copy-start.5) | copy-done | bytes 2072
  13.7 0.9 %copy-done.8 = bf16[1,8,32,256]{3,2,1,0:T(8,128)(2,1)S(1)} copy-done((bf16[1,8,32,256]{3,2,1,0:T(8,128)(2,1)S(1)}, bf16[1,8,32,256]{3,2,1,0:T(8,128)(2,1)}, u32[]{:S(2)}) %copy-start.8) | copy-done | bytes 131096
  14.6 0.9 %copy-done.9 = bf16[256,256]{1,0:T(8,128)(2,1)S(1)} copy-done((bf16[256,256]{1,0:T(8,128)(2,1)S(1)}, bf16[256,256]{1,0:T(8,128)(2,1)}, u32[]{:S(2)}) %copy-start.9) | copy-done | bytes 131096
  15.5 0.9 %copy-done.10 = bf16[256,256]{1,0:T(8,128)(2,1)S(1)} copy-done((bf16[256,256]{1,0:T(8,128)(2,1)S(1)}, bf16[256,256]{1,0:T(8,128)(2,1)}, u32[]{:S(2)}) %copy-start.10) | copy-done | bytes 131096
  16.4 0.9 %copy-done.11 = bf16[256,256]{1,0:T(8,128)(2,1)S(1)} copy-done((bf16[256,256]{1,0:T(8,128)(2,1)S(1)}, bf16[256,256]{1,0:T(8,128)(2,1)}, u32[]{:S(2)}) %copy-start.11) | copy-done | bytes 131096
  17.3 0.8 %copy-done.15 = bf16[256,128]{1,0:T(8,128)(2,1)S(1)} copy-done((bf16[256,128]{1,0:T(8,128)(2,1)S(1)}, bf16[256,128]{1,0:T(8,128)(2,1)}, u32[]{:S(2)}) %copy-start.15) | copy-done | bytes 65560
  18.2 0.8 %copy-done.16 = bf16[1,8,32,128]{3,2,1,0:T(8,128)(2,1)S(1)} copy-done((bf16[1,8,32,128]{3,2,1,0:T(8,128)(2,1)S(1)}, bf16[1,8,32,128]{3,2,1,0:T(8,128)(2,1)}, u32[]{:S(2)}) %copy-start.16) | copy-done | bytes 65560
  19.0 3.8 %shard_map.159 = (bf16[256,128]{1,0:T(8,128)(2,1)S(1)}, bf16[128,256]{1,0:T(8,128)(2,1)S(1)}) custom-call(bf16[512,256]{1,0:T(8,128)(2,1)S(1)} %bitcast.10, s32[1,512]{1,0:T(1,128)S(1)} %copy-done.5, bf16[8,144,128]{2,1,0:T(8,128)(2,1)S(1)} %collective-permute-done.refs_2_, bf16[256,256]{1,0:T(8,128)(2,1)S(1)} %bitcast.15, bf16[256,128]{1,0:T(8,128)(2,1)S(1)} %bitcast.16, ...), custom_call_target="tpu_custom_call" | custom-call | flops 2147483648 | bytes 1214464 | tf_op jit(solution)/shard_map/pallas_call | solution.py:25
  22.8 0.0 all-to-all-done.refs_1_
  22.8 0.0 copy-done.12
  22.8 0.0 copy-done.13
  22.9 0.0 copy-start.6
  22.9 0.0 copy-start.7
  22.9 0.0 copy-start.17
  22.9 4.3 %shard_map.161 = bf16[8,64,256]{2,1,0:T(8,128)(2,1)} custom-call(bf16[128,256]{1,0:T(8,128)(2,1)S(1)} %get-tuple-element.5.refs_0_, bf16[8,144,128]{2,1,0:T(8,128)(2,1)S(1)} %all-to-all-done.refs_1_, s32[4,128]{1,0:T(4,128)S(1)} %bitcast.18, bf16[256,256]{1,0:T(8,128)(2,1)S(1)} %copy-done.12, bf16[256,256]{1,0:T(8,128)(2,1)S(1)} %copy-done.13, ...), custom_call_target="tpu_custom_call" | custom-call | flops 805306368 | bytes 690176 | tf_op jit(solution)/shard_map/pallas_call | solution.py:25
  27.2 6.0 %all-to-all-start.1 = ((bf16[8,64,256]{2,1,0:T(8,128)(2,1)}), bf16[8,64,256]{2,1,0:T(8,128)(2,1)S(1)}, u32[]{:S(2)}, u32[]{:S(2)}) async-start(bf16[8,64,256]{2,1,0:T(8,128)(2,1)} %shard_map.161), calls=%async_computation.1 | async-start | bytes 524288 | tf_op jit(solution)/shard_map/all_to_all | solution.py:267
  33.2 0.0 collective-permute-start.1
  33.2 1.2 %collective-permute-done.1.refs_2_ = bf16[128,256]{1,0:T(8,128)(2,1)S(1)} collective-permute-done((bf16[128,256]{1,0:T(8,128)(2,1)S(1)}, bf16[128,256]{1,0:T(8,128)(2,1)S(1)}, u32[]{:S(2)}, u32[]{:S(2)}) %collective-permute-start.1) | collective-permute-done | bytes 65568 | tf_op jit(solution)/shard_map/ppermute | solution.py:250
  34.5 0.0 copy-done.7
  34.5 0.0 copy-start.2
  34.5 0.0 copy-start.3
  34.5 4.9 %shard_map.160 = bf16[256,128]{1,0:T(8,128)(2,1)} custom-call(bf16[256,128]{1,0:T(8,128)(2,1)S(1)} %bitcast.17, bf16[256,128]{1,0:T(8,128)(2,1)S(1)} %get-tuple-element.4.refs_1_, bf16[128,256]{1,0:T(8,128)(2,1)S(1)} %collective-permute-done.1.refs_2_, bf16[9,256,256]{2,1,0:T(8,128)(2,1)S(1)} %bitcast.13, bf16[9,256,128]{2,1,0:T(8,128)(2,1)S(1)} %bitcast.14), custom_call_target="tpu_custom_call" | custom-call | flops 1358954496 | bytes 1966080 | tf_op jit(solution)/shard_map/pallas_call | solution.py:25
  39.4 3.1 %all-to-all-done.1 = bf16[8,64,256]{2,1,0:T(8,128)(2,1)S(1)} async-done(((bf16[8,64,256]{2,1,0:T(8,128)(2,1)}), bf16[8,64,256]{2,1,0:T(8,128)(2,1)S(1)}, u32[]{:S(2)}, u32[]{:S(2)}) %all-to-all-start.1) | async-done | bytes 262176 | tf_op jit(solution)/shard_map/all_to_all | solution.py:267
  42.4 0.9 %shard_map.162 = bf16[512,256]{1,0:T(8,128)(2,1)} custom-call(bf16[512,256]{1,0:T(8,128)(2,1)S(1)} %bitcast.11, bf16[512,256]{1,0:T(8,128)(2,1)S(1)} %bitcast.12, bf16[256,256]{1,0:T(8,128)(2,1)S(1)} %copy-done.3), custom_call_target="tpu_custom_call" | custom-call | flops 67108864 | bytes 655360 | tf_op jit(solution)/shard_map/pallas_call | solution.py:25
  (19 shorter events, 0.0 us)
Async XLA Ops:
  0.6 1.0 %copy-start = (bf16[1,512,256]{2,1,0:T(8,128)(2,1)S(1)}, bf16[1,512,256]{2,1,0:T(8,128)(2,1)}, u32[]{:S(2)}) copy-start(bf16[1,512,256]{2,1,0:T(8,128)(2,1)} %param.17) | copy-start | bytes 786436
  1.6 0.7 %copy-start.4 = (s32[1,512]{1,0:T(1,128)S(1)}, s32[1,512]{1,0:T(1,128)}, u32[]{:S(2)}) copy-start(s32[1,512]{1,0:T(1,128)} %refs_1_.3) | copy-start | bytes 6148
  3.0 19.8 %all-to-all-start = ((bf16[8,144,128]{2,1,0:T(8,128)(2,1)}), bf16[8,144,128]{2,1,0:T(8,128)(2,1)S(1)}, u32[]{:S(2)}, u32[]{:S(2)}) async-start(bf16[8,144,128]{2,1,0:T(8,128)(2,1)} %shard_map.158), calls=%async_computation | async-start | bytes 589824 | tf_op jit(solution)/shard_map/all_to_all | solution.py:230
  10.3 1.8 %collective-permute-start = (bf16[8,144,128]{2,1,0:T(8,128)(2,1)}, bf16[8,144,128]{2,1,0:T(8,128)(2,1)S(1)}, u32[]{:S(2)}, u32[]{:S(2)}) collective-permute-start(bf16[8,144,128]{2,1,0:T(8,128)(2,1)} %shard_map.158), channel_id=1, source_target_pairs={{0,1},{1,0},{2,3},{3,2},{4,5},{5,4},{6,7},{7,6},{8,9},{9,8},{10,11... | collective-permute-start | bytes 884744 | tf_op jit(solution)/shard_map/ppermute | solution.py:229
  12.1 1.0 %copy-start.1 = (bf16[1,512,256]{2,1,0:T(8,128)(2,1)S(1)}, bf16[1,512,256]{2,1,0:T(8,128)(2,1)}, u32[]{:S(2)}) copy-start(bf16[1,512,256]{2,1,0:T(8,128)(2,1)} %param.17) | copy-start | bytes 786436
  13.0 0.7 %copy-start.5 = (s32[1,512]{1,0:T(1,128)S(1)}, s32[1,512]{1,0:T(1,128)}, u32[]{:S(2)}) copy-start(s32[1,512]{1,0:T(1,128)} %refs_1_.3) | copy-start | bytes 6148
  13.7 0.9 %copy-start.8 = (bf16[1,8,32,256]{3,2,1,0:T(8,128)(2,1)S(1)}, bf16[1,8,32,256]{3,2,1,0:T(8,128)(2,1)}, u32[]{:S(2)}) copy-start(bf16[1,8,32,256]{3,2,1,0:T(8,128)(2,1)} %param.15) | copy-start | bytes 393220
  14.6 0.9 %copy-start.9 = (bf16[256,256]{1,0:T(8,128)(2,1)S(1)}, bf16[256,256]{1,0:T(8,128)(2,1)}, u32[]{:S(2)}) copy-start(bf16[256,256]{1,0:T(8,128)(2,1)} %refs_5_.2) | copy-start | bytes 393220
  15.5 0.9 %copy-start.10 = (bf16[256,256]{1,0:T(8,128)(2,1)S(1)}, bf16[256,256]{1,0:T(8,128)(2,1)}, u32[]{:S(2)}) copy-start(bf16[256,256]{1,0:T(8,128)(2,1)} %refs_6_.1) | copy-start | bytes 393220
  16.4 0.9 %copy-start.11 = (bf16[256,256]{1,0:T(8,128)(2,1)S(1)}, bf16[256,256]{1,0:T(8,128)(2,1)}, u32[]{:S(2)}) copy-start(bf16[256,256]{1,0:T(8,128)(2,1)} %refs_7_.1) | copy-start | bytes 393220
  17.3 0.8 %copy-start.15 = (bf16[256,128]{1,0:T(8,128)(2,1)S(1)}, bf16[256,128]{1,0:T(8,128)(2,1)}, u32[]{:S(2)}) copy-start(bf16[256,128]{1,0:T(8,128)(2,1)} %refs_8_.1) | copy-start | bytes 196612
  18.2 0.8 %copy-start.16 = (bf16[1,8,32,128]{3,2,1,0:T(8,128)(2,1)S(1)}, bf16[1,8,32,128]{3,2,1,0:T(8,128)(2,1)}, u32[]{:S(2)}) copy-start(bf16[1,8,32,128]{3,2,1,0:T(8,128)(2,1)} %param.16) | copy-start | bytes 196612
  19.0 3.8 %copy-start.12 = (bf16[256,256]{1,0:T(8,128)(2,1)S(1)}, bf16[256,256]{1,0:T(8,128)(2,1)}, u32[]{:S(2)}) copy-start(bf16[256,256]{1,0:T(8,128)(2,1)} %refs_3_.1) | copy-start | bytes 393220
  19.0 3.8 %copy-start.13 = (bf16[256,256]{1,0:T(8,128)(2,1)S(1)}, bf16[256,256]{1,0:T(8,128)(2,1)}, u32[]{:S(2)}) copy-start(bf16[256,256]{1,0:T(8,128)(2,1)} %refs_4_.1) | copy-start | bytes 393220
  19.0 3.8 %copy-start.14 = (bf16[256,256]{1,0:T(8,128)(2,1)S(1)}, bf16[256,256]{1,0:T(8,128)(2,1)}, u32[]{:S(2)}) copy-start(bf16[256,256]{1,0:T(8,128)(2,1)} %refs_5_.3) | copy-start | bytes 393220
  19.0 3.8 %copy-start.18 = (s32[512]{0:T(512)S(1)}, s32[512]{0:T(512)}, u32[]{:S(2)}) copy-start(s32[512]{0:T(512)} %param.19) | copy-start | bytes 6148
  22.9 11.6 %copy-start.6 = (bf16[3,3,256,256]{3,2,1,0:T(8,128)(2,1)S(1)}, bf16[3,3,256,256]{3,2,1,0:T(8,128)(2,1)}, u32[]{:S(2)}) copy-start(bf16[3,3,256,256]{3,2,1,0:T(8,128)(2,1)} %param.28) | copy-start | bytes 3538948
  22.9 11.6 %copy-start.7 = (bf16[3,3,256,128]{3,2,1,0:T(8,128)(2,1)S(1)}, bf16[3,3,256,128]{3,2,1,0:T(8,128)(2,1)}, u32[]{:S(2)}) copy-start(bf16[3,3,256,128]{3,2,1,0:T(8,128)(2,1)} %param.29) | copy-start | bytes 1769476
  22.9 11.6 %copy-start.17 = (bf16[1,8,32,128]{3,2,1,0:T(8,128)(2,1)S(1)}, bf16[1,8,32,128]{3,2,1,0:T(8,128)(2,1)}, u32[]{:S(2)}) copy-start(bf16[1,8,32,128]{3,2,1,0:T(8,128)(2,1)} %param.16) | copy-start | bytes 196612
  27.2 15.2 %all-to-all-start.1 = ((bf16[8,64,256]{2,1,0:T(8,128)(2,1)}), bf16[8,64,256]{2,1,0:T(8,128)(2,1)S(1)}, u32[]{:S(2)}, u32[]{:S(2)}) async-start(bf16[8,64,256]{2,1,0:T(8,128)(2,1)} %shard_map.161), calls=%async_computation.1 | async-start | bytes 524288 | tf_op jit(solution)/shard_map/all_to_all | solution.py:267
  33.2 1.3 %collective-permute-start.1 = (bf16[128,256]{1,0:T(8,128)(2,1)S(1)}, bf16[128,256]{1,0:T(8,128)(2,1)S(1)}, u32[]{:S(2)}, u32[]{:S(2)}) collective-permute-start(bf16[128,256]{1,0:T(8,128)(2,1)S(1)} %get-tuple-element.5.refs_0_), channel_id=1, source_target_pairs={{0,1},{1,0},{2,3},{3,2},{4,5},{5,4},{6,7},{7,6},{8,9},{9,8},{10,11... | collective-permute-start | bytes 196616 | tf_op jit(solution)/shard_map/ppermute | solution.py:250
  34.5 7.9 %copy-start.2 = (bf16[1,512,256]{2,1,0:T(8,128)(2,1)S(1)}, bf16[1,512,256]{2,1,0:T(8,128)(2,1)}, u32[]{:S(2)}) copy-start(bf16[1,512,256]{2,1,0:T(8,128)(2,1)} %param.17) | copy-start | bytes 786436
  34.5 7.9 %copy-start.3 = (bf16[256,256]{1,0:T(8,128)(2,1)S(1)}, bf16[256,256]{1,0:T(8,128)(2,1)}, u32[]{:S(2)}) copy-start(bf16[256,256]{1,0:T(8,128)(2,1)} %refs_2_.1) | copy-start | bytes 393220

commit v2 on v1

v2 whole, which is shorter than its diff:
```python
import jax
import jax.numpy as jnp
from jax import lax
from jax.experimental import pallas as pl
from jax.experimental.pallas import tpu as pltpu
from jax.sharding import PartitionSpec as P

HEADS = 8
ITERS = 2
LANES = 128
MASK_ROWS = 16
HIDDEN = -1e30

f32 = jnp.float32
bf16 = jnp.bfloat16
VMEM = pl.BlockSpec(memory_space=pltpu.VMEM)
HBM = pl.BlockSpec(memory_space=pltpu.HBM)
LATER = pl.BlockSpec(memory_space=pl.ANY)


def dot(a, b):
    return jnp.dot(a, b, preferred_element_type=f32)


def call(body, out, near, far=(), scratch=(), flops=0, after=(), raw=(), grant=24 * 2**20, place=VMEM):
    moved = sum(x.size * x.dtype.itemsize for x in (*near, *far))

    def whole(*refs):
        refs = refs[len(after) :]
        if not far:
            return body(*refs)
        sources = refs[: len(far)]
        buffers, arrived = refs[-len(far) - 1 : -1], refs[-1]
        copies = [
            pltpu.make_async_copy(source, buffer, arrived.at[i])
            for i, (source, buffer) in enumerate(zip(sources, buffers))
        ]
        for copy in copies:
            copy.start()

        def fetch(copy, buffer):
            def wait():
                copy.wait()
                return buffer

            return wait

        fetched = [fetch(c, b) for c, b in zip(copies, buffers)]
        return body(*fetched, *refs[len(far) : -len(far) - 1])

    buffers = [pltpu.VMEM(x.shape, x.dtype) for x in far]
    if far:
        buffers.append(pltpu.SemaphoreType.DMA((len(far),)))
    return pl.pallas_call(
        whole,
        out_shape=out,
        in_specs=[LATER] * len(after) + [HBM] * len(raw + far) + [VMEM] * len(near),
        out_specs=jax.tree.map(lambda _: place, out),
        scratch_shapes=[*scratch, *buffers],
        compiler_params=pltpu.CompilerParams(vmem_limit_bytes=grant),
        cost_estimate=pl.CostEstimate(flops=flops, bytes_accessed=moved, transcendentals=0),
    )(*after, *raw, *far, *near)


def pack_body(tokens, visible, out, flags, packed, sems):
    frames, rows, _ = out.shape
    share = tokens.shape[1]
    chunks = 2
    step = frames // chunks
    first = pltpu.make_async_copy(visible, flags, sems.at[0])
    first.start()
    coming = []
    for i in range(chunks):
        some = pl.ds(i * step, step)
        coming.append(
            [
                pltpu.make_async_copy(
                    tokens.at[some, :, pl.ds(c * LANES, LANES)],
                    packed.at[some, pl.ds(c * share, share), :],
                    sems.at[1 + 2 * i + c],
                )
                for c in range(2)
            ]
        )
    for copies in coming:
        for copy in copies:
            copy.start()
    first.wait()
    for g in range(frames):
        group = flags[g * share // LANES, :].astype(f32)
        packed[g, 2 * share :, :] = jnp.broadcast_to(group[None], (MASK_ROWS, LANES)).astype(bf16)
    going = []
    for i, copies in enumerate(coming):
        for copy in copies:
            copy.wait()
        some = pl.ds(i * step, step)
        going.append(pltpu.make_async_copy(packed.at[some], out.at[some], sems.at[1 + 2 * chunks + i]))
        going[-1].start()
    for copy in going:
        copy.wait()


def attend_body(
    pixels, tokens, w_query, w_key, w_value, visible, w_out, state, other, flags, context, edge
):
    half, channels = other.shape
    head_dim = channels // HEADS
    query = dot(pixels()[...], w_query()[...]).astype(bf16)
    rows = jnp.concatenate([tokens()[...], other[...]], axis=0)
    key = dot(rows, w_key()[...]).astype(bf16)
    value = dot(rows, w_value()[...]).astype(bf16)
    bias = jnp.where(jnp.concatenate([visible()[...], flags[...]], axis=1) > 0, 0.0, HIDDEN)
    head_of = lax.broadcasted_iota(jnp.int32, (1, channels), 1) // head_dim
    scale = head_dim**-0.5
    attended = jnp.zeros(query.shape, f32)
    for head in range(HEADS):
        mine = head_of == head
        masked = jnp.where(mine, query, jnp.zeros_like(query))
        scores = lax.dot_general(
            masked, key, (((1,), (1,)), ((), ())), preferred_element_type=f32
        )
        scores = scores + bias
        top = jnp.max(scores, axis=1, keepdims=True)
        weights = jnp.exp((scores - top) * scale)
        total = jnp.sum(weights, axis=1, keepdims=True)
        summed = dot(weights.astype(bf16), value)
        attended = jnp.where(mine, summed / total, attended)
    context[...] = dot(attended.astype(bf16), w_out()[...]).astype(bf16)
    count = edge.shape[0]
    start = pl.multiple_of((1 - lax.axis_index("band")) * (query.shape[0] - count), count)
    edge[:, :LANES] = state()[pl.ds(start, count), :]
    edge[:, LANES:] = context[pl.ds(start, count), :]


def temporal_body(packed, query_frame, w_query, w_key, w_value, out, flag_cols, frame_cols, result, sems):
    frames, share, channels = out.shape
    head_dim = channels // HEADS
    columns = -(-frames * HEADS // LANES) * LANES
    me = lax.axis_index("frame")
    first = me * share
    group, start = first // LANES, pl.multiple_of(first % LANES, share)
    flags = packed[:, 2 * share :, :].reshape(frames * MASK_ROWS, LANES)
    flag_cols[...] = flags.astype(f32).T
    asked = query_frame[pl.ds(group, 1), :].astype(f32)
    frame_cols[...] = jnp.broadcast_to(asked, (LANES, LANES)).T
    flags = flag_cols[pl.ds(start, share), :]
    asked = frame_cols[pl.ds(start, share), :1]

    left = packed[:, :share, :].reshape(frames * share, LANES)
    right = packed[:, share : 2 * share, :].reshape(frames * share, LANES)
    rows = jnp.concatenate([left, right], axis=1)
    shape = (frames, share, channels)
    query = dot(rows, w_query[...]).astype(bf16).astype(f32).reshape(shape)
    key = dot(rows, w_key[...]).astype(bf16).astype(f32).reshape(shape)
    value = dot(rows, w_value[...]).astype(bf16).astype(f32).reshape(shape)
    anchor = jnp.zeros((share, channels), f32)
    for s in range(frames):
        anchor = jnp.where(asked == s, query[s], anchor)

    head_of_row = lax.broadcasted_iota(jnp.int32, (channels, columns), 0) // head_dim
    column = lax.broadcasted_iota(jnp.int32, (channels, columns), 1)
    head_of_col = lax.broadcasted_iota(jnp.int32, (columns, channels), 1) // head_dim
    line = lax.broadcasted_iota(jnp.int32, (columns, channels), 0)
    scores = jnp.zeros((frames * share, columns), f32)
    for s in range(frames):
        joint = (query[s] + anchor).astype(bf16).astype(f32)
        product = (key * joint[None]).reshape(frames * share, channels)
        high = product.astype(bf16)
        low = (product - high.astype(f32)).astype(bf16)
        gather = jnp.where(column == head_of_row + s * HEADS, 1.0, 0.0).astype(bf16)
        scores = scores + dot(high, gather) + dot(low, gather)
    scores = scores.reshape(frames, share, columns) * head_dim**-0.5
    seen = [
        jnp.where(flags[:, g * MASK_ROWS : g * MASK_ROWS + 1] > 0.5, scores[g], HIDDEN)
        for g in range(frames)
    ]
    top = seen[0]
    for g in range(1, frames):
        top = jnp.maximum(top, seen[g])
    raised = [jnp.exp(x - top) for x in seen]
    total = raised[0]
    for g in range(1, frames):
        total = total + raised[g]
    weights = jnp.concatenate([x / total for x in raised], axis=0).astype(bf16)
    copies = []
    for s in range(frames):
        spread = jnp.where(line == head_of_col + s * HEADS, 1.0, 0.0).astype(bf16)
        wide = dot(weights, spread).reshape(shape)
        result[s] = jnp.sum(wide * value, axis=0).astype(bf16)
        copies.append(pltpu.make_async_copy(result.at[s], out.at[s], sems.at[s]))
        copies[-1].start()
    for copy in copies:
        copy.wait()


def refine_body(state, context, halo, w_gates, w_cand, out, field, wide):
    taps, both, _ = w_gates.shape
    local, hidden = state.shape
    beyond = halo.shape[0]
    pixels = local + beyond
    width = (wide.shape[0] - pixels) // 2
    band = lax.axis_index("band")
    here = pl.multiple_of(band * beyond, beyond)
    there = pl.multiple_of((1 - band) * local, beyond)
    col = lax.broadcasted_iota(jnp.int32, (pixels, hidden), 0) % width
    wide[:width, :] = jnp.zeros((width, 3 * both), bf16)
    wide[width + pixels :, :] = jnp.zeros((width, 3 * both), bf16)

    def spread(values, lane):
        before = jnp.where(col == 0, 0.0, pltpu.roll(values, 1, 0))
        after = jnp.where(col == width - 1, 0.0, pltpu.roll(values, pixels - 1, 0))
        for c, shifted in enumerate((before, values, after)):
            first = c * both + lane
            wide[width : width + pixels, first : first + hidden] = shifted.astype(bf16)

    def conv(weight):
        rows = [wide[r * width : r * width + pixels, :] for r in range(3)]
        return dot(jnp.concatenate(rows, axis=1), weight[...].reshape(taps * both, -1))

    field[pl.ds(here, local), :] = context[...]
    field[pl.ds(there, beyond), :] = halo[:, hidden:]
    spread(field[...].astype(f32), hidden)
    field[pl.ds(here, local), :] = state[...]
    field[pl.ds(there, beyond), :] = halo[:, :hidden]
    now = field[...].astype(f32)
    for _ in range(ITERS):
        spread(now, 0)
        gates = conv(w_gates)
        update = jax.nn.sigmoid(gates[:, :hidden])
        reset = jax.nn.sigmoid(gates[:, hidden:])
        spread((reset * now).astype(bf16).astype(f32), 0)
        cand = jnp.tanh(conv(w_cand))
        now = ((1.0 - update) * now + update * cand).astype(bf16).astype(f32)
    field[...] = now.astype(bf16)
    out[...] = field[pl.ds(here, local), :]


def output_body(returned, tokens, w_out, out):
    out[...] = (tokens[...].astype(f32) + dot(returned[...], w_out[...])).astype(bf16)


def on_device(
    pixels,
    gru_state,
    tokens,
    visible,
    query_frame,
    pixel_query,
    pixel_key,
    pixel_value,
    pixel_out,
    time_query,
    time_key,
    time_value,
    time_out,
    gru_gates,
    gru_candidate,
):
    frames = lax.axis_size("frame")
    _, band_rows, width, channels = pixels.shape
    hidden = gru_state.shape[3]
    half = tokens.shape[1]
    share = half // frames
    local = band_rows * width
    beyond = 2 * ITERS * width
    assert LANES % share == 0
    assert lax.axis_size("band") == 2 and channels == 2 * LANES and hidden == LANES
    swap = [(0, 1), (1, 0)]
    local_tokens = tokens[0]
    flat_state = gru_state.reshape(local, hidden)
    groups = half // LANES

    other = lax.ppermute(local_tokens, "band", swap)
    flags = lax.ppermute(visible, "band", swap)
    packed = call(
        pack_body,
        jax.ShapeDtypeStruct((frames, 2 * share + MASK_ROWS, LANES), bf16),
        (),
        scratch=[
            pltpu.VMEM((groups, LANES), jnp.int32),
            pltpu.VMEM((frames, 2 * share + MASK_ROWS, LANES), bf16),
            pltpu.SemaphoreType.DMA((7,)),
        ],
        raw=(local_tokens.reshape(frames, share, channels), visible.reshape(groups, LANES)),
        flops=10**10,
        grant=60 * 2**20,
        place=HBM,
    )
    arrived = lax.all_to_all(packed, "frame", split_axis=0, concat_axis=0, tiled=True)

    context, edge = call(
        attend_body,
        (
            jax.ShapeDtypeStruct((local, hidden), bf16),
            jax.ShapeDtypeStruct((beyond, 2 * hidden), bf16),
        ),
        (other, flags),
        (
            pixels.reshape(local, channels),
            local_tokens,
            pixel_query,
            pixel_key,
            pixel_value,
            visible,
            pixel_out,
            flat_state,
        ),
        flops=4 * local * 2 * half * channels * HEADS,
    )
    halo = lax.ppermute(edge, "band", swap)

    attended = call(
        temporal_body,
        jax.ShapeDtypeStruct((frames, share, channels), bf16),
        (arrived, query_frame.reshape(groups, LANES), time_query, time_key, time_value),
        scratch=[
            pltpu.VMEM((LANES, frames * MASK_ROWS), f32),
            pltpu.VMEM((LANES, LANES), f32),
            pltpu.VMEM((frames, share, channels), bf16),
            pltpu.SemaphoreType.DMA((frames,)),
        ],
        place=HBM,
        flops=6 * half * channels * channels * 4,
        after=(edge,),
    )
    returned = lax.all_to_all(attended, "frame", split_axis=0, concat_axis=0, tiled=True)

    refined = call(
        refine_body,
        jax.ShapeDtypeStruct((local, hidden), bf16),
        (
            flat_state,
            context,
            halo,
            gru_gates.reshape(9, 2 * hidden, 2 * hidden),
            gru_candidate.reshape(9, 2 * hidden, hidden),
        ),
        scratch=[
            pltpu.VMEM((local + beyond, hidden), bf16),
            pltpu.VMEM((local + beyond + 2 * width, 6 * hidden), bf16),
        ],
        flops=2 * (local + beyond) * 9 * 2 * hidden * 3 * hidden * ITERS,
    )
    track_out = call(
        output_body,
        jax.ShapeDtypeStruct((half, channels), bf16),
        (returned.reshape(half, channels), local_tokens, time_out),
        flops=2 * half * channels * channels,
    )
    return refined.reshape(gru_state.shape), track_out[None]


def solution(mesh):
    placed = (
        P(("clip", "frame"), "band", None, None),
        P(("clip", "frame"), "band", None, None),
        P(("clip", "frame"), "band", None),
        P(("clip", "frame"), "band"),
        P(("clip", "band")),
        P(),
        P(),
        P(),
        P(),
        P(),
        P(),
        P(),
        P(),
        P(),
        P(),
    )
    return jax.shard_map(
        on_device,
        mesh=mesh,
        in_specs=placed,
        out_specs=(P(("clip", "frame"), "band", None, None), P(("clip", "frame"), "band", None)),
        check_vma=False,
    )
```

time: 44 us -> 37.7 us (0.86)
  local copies, waits for them, and re-layouts: 8.6 us -> 0.08 us
  Pallas kernels: 14.7 us -> 17.2 us
  starting transfers between devices: 13.3 us -> 11.5 us
  waiting for transfers between devices: 6.08 us -> 7.73 us
    unnamed x38 -> x30, local copies, waits for them, and re-layouts: 8.6 us -> 0.08 us
    pallas_call x5, Pallas kernels: 14.7 us -> 17.2 us  [call(): pl.pallas_call(whole, out_shape=out, in_specs=[LATER] * len(after) + [HBM...]
    all_to_all x1, waiting for transfers between devices: 0.01 us -> 2.54 us  [on_device(): lax.all_to_all(packed, 'frame', split_axis=0, concat_axis=0, tiled=True)]
    all_to_all x1, starting transfers between devices: 6 us -> 3.6 us  [on_device(): lax.all_to_all(attended, 'frame', split_axis=0, concat_axis=0, tiled=True)]
    ppermute x1 -> x2, waiting for transfers between devices: 1.78 us -> 1.02 us  [the longest x1 1.02 us: on_device(): flags = lax.ppermute(visible, 'band', swap)]
    ppermute x1 -> x2, starting transfers between devices: 0.01 us -> 0.56 us  [the longest x1 0.49 us: on_device(): flags = lax.ppermute(visible, 'band', swap)]
  transfers between devices with their start and end apart: 4 -> 5, of which waited for: 3 -> 4; matrix products, arithmetic and copies ran while one was open for 0% -> 0% of each run, Pallas kernels for 20% -> 27%
where the time goes in v2:
time: 37.7 us; the launch traced here: 37.3 us
  Pallas kernels  17.2 us (46%)
  starting transfers between devices  11.5 us (31%)
  waiting for transfers between devices  7.73 us (21%)
  between operations  0.85 us (2%)
    pallas_call x5, Pallas kernels, call(): pl.pallas_call(whole, out_shape=out, in_specs=[LATER] * len(after) + [HBM...  17.2 us
    all_to_all x1, starting transfers between devices, on_device(): lax.all_to_all(packed, 'frame', split_axis=0, concat_axis=0, tiled=True)  7.29 us
    all_to_all x1, starting transfers between devices, on_device(): lax.all_to_all(attended, 'frame', split_axis=0, concat_axis=0, tiled=True)  3.6 us
    all_to_all x1, waiting for transfers between devices, on_device(): lax.all_to_all(attended, 'frame', split_axis=0, concat_axis=0, tiled=True)  2.92 us
    all_to_all x1, waiting for transfers between devices, on_device(): lax.all_to_all(packed, 'frame', split_axis=0, concat_axis=0, tiled=True)  2.54 us
    ppermute x1, waiting for transfers between devices, on_device(): halo = lax.ppermute(edge, 'band', swap)  1.25 us
    ppermute x1, waiting for transfers between devices, on_device(): flags = lax.ppermute(visible, 'band', swap)  1.02 us
  transfers between devices with their start and end apart: 5, of which 4 were waited for; matrix products, arithmetic and copies ran while one was open for 0% of the time, Pallas kernels for 27%

profile of v2, /device:TPU:0, one launch (start us, length us, event | category | flops | bytes accessed | tf_op | source)
XLA Modules:
  0.0 37.3 jit_solution(18154944825172168298)
XLA Ops:
  0.6 0.0 copy-start
  0.6 0.0 copy-start.13
  0.7 0.0 copy-start.4
  0.7 0.0 copy-start.5
  0.7 0.0 copy-start.6
  0.7 0.0 copy-start.7
  0.7 0.0 copy-start.11
  0.7 0.0 copy-start.12
  0.7 1.8 %shard_map.160 = bf16[8,144,128]{2,1,0:T(8,128)(2,1)} custom-call(bf16[8,64,256]{2,1,0:T(8,128)(2,1)} %bitcast.12, s32[4,128]{1,0:T(4,128)} %bitcast.21), custom_call_target="tpu_custom_call" | custom-call | flops 10000000000 | tf_op jit(solution)/shard_map/pallas_call | solution.py:54
  2.5 7.3 %all-to-all-start = ((bf16[8,144,128]{2,1,0:T(8,128)(2,1)}), bf16[8,144,128]{2,1,0:T(8,128)(2,1)S(1)}, u32[]{:S(2)}, u32[]{:S(2)}) async-start(bf16[8,144,128]{2,1,0:T(8,128)(2,1)} %shard_map.160), calls=%async_computation | async-start | bytes 589824 | tf_op jit(solution)/shard_map/all_to_all | solution.py:289
  9.8 0.0 copy-done
  9.8 0.1 collective-permute-start
  9.9 0.5 %collective-permute-start.1 = (s32[1,512]{1,0:T(1,128)S(1)}, s32[1,512]{1,0:T(1,128)S(1)}, u32[]{:S(2)}, u32[]{:S(2)}) collective-permute-start(s32[1,512]{1,0:T(1,128)S(1)} %copy-done.13), channel_id=1, source_target_pairs={{0,1},{1,0},{2,3},{3,2},{4,5},{5,4},{6,7},{7,6},{8,9},{9,8},{10,11... | collective-permute-start | bytes 6152 | tf_op jit(solution)/shard_map/ppermute | solution.py:274
  10.4 1.0 %collective-permute-done.1.refs_9_ = s32[1,512]{1,0:T(1,128)S(1)} collective-permute-done((s32[1,512]{1,0:T(1,128)S(1)}, s32[1,512]{1,0:T(1,128)S(1)}, u32[]{:S(2)}, u32[]{:S(2)}) %collective-permute-start.1) | collective-permute-done | bytes 2080 | tf_op jit(solution)/shard_map/ppermute | solution.py:274
  11.4 0.0 collective-permute-done.refs_8_
  11.4 0.0 copy-done.4
  11.4 0.0 copy-start.8
  11.5 0.0 copy-start.9
  11.5 0.0 copy-start.10
  11.5 0.0 copy-start.14
  11.5 5.4 %shard_map.158 = (bf16[256,128]{1,0:T(8,128)(2,1)S(1)}, bf16[128,256]{1,0:T(8,128)(2,1)S(1)}) custom-call(bf16[256,256]{1,0:T(8,128)(2,1)S(1)} %bitcast.18, bf16[512,256]{1,0:T(8,128)(2,1)S(1)} %bitcast.14, bf16[256,256]{1,0:T(8,128)(2,1)S(1)} %copy-done.5, bf16[256,256]{1,0:T(8,128)(2,1)S(1)} %copy-done.6, bf16[256,256]{1,0:T(8,128)(2,1)S(1)} %copy-done.7, ...), custom_call_target="tpu_custom_call" | custom-call | flops 2147483648 | bytes 1183744 | tf_op jit(solution)/shard_map/pallas_call | solution.py:54
  16.9 2.5 %all-to-all-done.refs_1_ = bf16[8,144,128]{2,1,0:T(8,128)(2,1)S(1)} async-done(((bf16[8,144,128]{2,1,0:T(8,128)(2,1)}), bf16[8,144,128]{2,1,0:T(8,128)(2,1)S(1)}, u32[]{:S(2)}, u32[]{:S(2)}) %all-to-all-start) | async-done | bytes 294944 | tf_op jit(solution)/shard_map/all_to_all | solution.py:289
  19.4 0.0 copy-done.10
  19.4 0.0 copy-start.2
  19.4 0.0 copy-start.3
  19.4 4.3 %shard_map.161 = bf16[8,64,256]{2,1,0:T(8,128)(2,1)} custom-call(bf16[128,256]{1,0:T(8,128)(2,1)S(1)} %get-tuple-element.5.refs_0_, bf16[8,144,128]{2,1,0:T(8,128)(2,1)S(1)} %all-to-all-done.refs_1_, s32[4,128]{1,0:T(4,128)S(1)} %bitcast.22, bf16[256,256]{1,0:T(8,128)(2,1)S(1)} %copy-done.8, bf16[256,256]{1,0:T(8,128)(2,1)S(1)} %copy-done.9, ...), custom_call_target="tpu_custom_call" | custom-call | flops 805306368 | bytes 690176 | tf_op jit(solution)/shard_map/pallas_call | solution.py:54
  23.8 3.6 %all-to-all-start.1 = ((bf16[8,64,256]{2,1,0:T(8,128)(2,1)}), bf16[8,64,256]{2,1,0:T(8,128)(2,1)S(1)}, u32[]{:S(2)}, u32[]{:S(2)}) async-start(bf16[8,64,256]{2,1,0:T(8,128)(2,1)} %shard_map.161), calls=%async_computation.1 | async-start | bytes 524288 | tf_op jit(solution)/shard_map/all_to_all | solution.py:326
  27.4 0.0 collective-permute-start.2
  27.4 1.2 %collective-permute-done.2.refs_2_ = bf16[128,256]{1,0:T(8,128)(2,1)S(1)} collective-permute-done((bf16[128,256]{1,0:T(8,128)(2,1)S(1)}, bf16[128,256]{1,0:T(8,128)(2,1)S(1)}, u32[]{:S(2)}, u32[]{:S(2)}) %collective-permute-start.2) | collective-permute-done | bytes 65568 | tf_op jit(solution)/shard_map/ppermute | solution.py:310
  28.6 4.9 %shard_map.159 = bf16[256,128]{1,0:T(8,128)(2,1)} custom-call(bf16[256,128]{1,0:T(8,128)(2,1)S(1)} %bitcast.20, bf16[256,128]{1,0:T(8,128)(2,1)S(1)} %get-tuple-element.4.refs_1_, bf16[128,256]{1,0:T(8,128)(2,1)S(1)} %collective-permute-done.2.refs_2_, bf16[9,256,256]{2,1,0:T(8,128)(2,1)S(1)} %bitcast.16, bf16[9,256,128]{2,1,0:T(8,128)(2,1)S(1)} %bitcast.17), custom_call_target="tpu_custom_call" | custom-call | flops 1358954496 | bytes 1966080 | tf_op jit(solution)/shard_map/pallas_call | solution.py:54
  33.5 2.9 %all-to-all-done.1 = bf16[8,64,256]{2,1,0:T(8,128)(2,1)S(1)} async-done(((bf16[8,64,256]{2,1,0:T(8,128)(2,1)}), bf16[8,64,256]{2,1,0:T(8,128)(2,1)S(1)}, u32[]{:S(2)}, u32[]{:S(2)}) %all-to-all-start.1) | async-done | bytes 262176 | tf_op jit(solution)/shard_map/all_to_all | solution.py:326
  36.4 0.9 %shard_map.162 = bf16[512,256]{1,0:T(8,128)(2,1)} custom-call(bf16[512,256]{1,0:T(8,128)(2,1)S(1)} %bitcast.11, bf16[512,256]{1,0:T(8,128)(2,1)S(1)} %bitcast.15, bf16[256,256]{1,0:T(8,128)(2,1)S(1)} %copy-done.1), custom_call_target="tpu_custom_call" | custom-call | flops 67108864 | bytes 655360 | tf_op jit(solution)/shard_map/pallas_call | solution.py:54
  (13 shorter events, 0.0 us)
Async XLA Ops:
  0.6 9.2 %copy-start = (bf16[1,512,256]{2,1,0:T(8,128)(2,1)S(1)}, bf16[1,512,256]{2,1,0:T(8,128)(2,1)}, u32[]{:S(2)}) copy-start(bf16[1,512,256]{2,1,0:T(8,128)(2,1)} %param.17) | copy-start | bytes 786436
  0.6 9.2 %copy-start.13 = (s32[1,512]{1,0:T(1,128)S(1)}, s32[1,512]{1,0:T(1,128)}, u32[]{:S(2)}) copy-start(s32[1,512]{1,0:T(1,128)} %refs_5_.2) | copy-start | bytes 6148
  0.7 10.7 %copy-start.4 = (bf16[1,8,32,256]{3,2,1,0:T(8,128)(2,1)S(1)}, bf16[1,8,32,256]{3,2,1,0:T(8,128)(2,1)}, u32[]{:S(2)}) copy-start(bf16[1,8,32,256]{3,2,1,0:T(8,128)(2,1)} %param.15) | copy-start | bytes 393220
  0.7 10.7 %copy-start.5 = (bf16[256,256]{1,0:T(8,128)(2,1)S(1)}, bf16[256,256]{1,0:T(8,128)(2,1)}, u32[]{:S(2)}) copy-start(bf16[256,256]{1,0:T(8,128)(2,1)} %refs_2_.2) | copy-start | bytes 393220
  0.7 10.7 %copy-start.6 = (bf16[256,256]{1,0:T(8,128)(2,1)S(1)}, bf16[256,256]{1,0:T(8,128)(2,1)}, u32[]{:S(2)}) copy-start(bf16[256,256]{1,0:T(8,128)(2,1)} %refs_3_.2) | copy-start | bytes 393220
  0.7 10.7 %copy-start.7 = (bf16[256,256]{1,0:T(8,128)(2,1)S(1)}, bf16[256,256]{1,0:T(8,128)(2,1)}, u32[]{:S(2)}) copy-start(bf16[256,256]{1,0:T(8,128)(2,1)} %refs_4_.2) | copy-start | bytes 393220
  0.7 10.7 %copy-start.11 = (bf16[256,128]{1,0:T(8,128)(2,1)S(1)}, bf16[256,128]{1,0:T(8,128)(2,1)}, u32[]{:S(2)}) copy-start(bf16[256,128]{1,0:T(8,128)(2,1)} %refs_6_.1) | copy-start | bytes 196612
  0.7 10.7 %copy-start.12 = (bf16[1,8,32,128]{3,2,1,0:T(8,128)(2,1)S(1)}, bf16[1,8,32,128]{3,2,1,0:T(8,128)(2,1)}, u32[]{:S(2)}) copy-start(bf16[1,8,32,128]{3,2,1,0:T(8,128)(2,1)} %param.16) | copy-start | bytes 196612
  2.5 16.9 %all-to-all-start = ((bf16[8,144,128]{2,1,0:T(8,128)(2,1)}), bf16[8,144,128]{2,1,0:T(8,128)(2,1)S(1)}, u32[]{:S(2)}, u32[]{:S(2)}) async-start(bf16[8,144,128]{2,1,0:T(8,128)(2,1)} %shard_map.160), calls=%async_computation | async-start | bytes 589824 | tf_op jit(solution)/shard_map/all_to_all | solution.py:289
  9.8 1.6 %collective-permute-start = (bf16[512,256]{1,0:T(8,128)(2,1)S(1)}, bf16[512,256]{1,0:T(8,128)(2,1)S(1)}, u32[]{:S(2)}, u32[]{:S(2)}) collective-permute-start(bf16[512,256]{1,0:T(8,128)(2,1)S(1)} %bitcast.13), channel_id=1, source_target_pairs={{0,1},{1,0},{2,3},{3,2},{4,5},{5,4},{6,7},{7,6},{8,9},{9,8},{10,11... | collective-permute-start | bytes 786440 | tf_op jit(solution)/shard_map/ppermute | solution.py:273
  9.9 1.5 %collective-permute-start.1 = (s32[1,512]{1,0:T(1,128)S(1)}, s32[1,512]{1,0:T(1,128)S(1)}, u32[]{:S(2)}, u32[]{:S(2)}) collective-permute-start(s32[1,512]{1,0:T(1,128)S(1)} %copy-done.13), channel_id=1, source_target_pairs={{0,1},{1,0},{2,3},{3,2},{4,5},{5,4},{6,7},{7,6},{8,9},{9,8},{10,11... | collective-permute-start | bytes 6152 | tf_op jit(solution)/shard_map/ppermute | solution.py:274
  11.4 8.0 %copy-start.8 = (bf16[256,256]{1,0:T(8,128)(2,1)S(1)}, bf16[256,256]{1,0:T(8,128)(2,1)}, u32[]{:S(2)}) copy-start(bf16[256,256]{1,0:T(8,128)(2,1)} %refs_3_.3) | copy-start | bytes 393220
  11.5 8.0 %copy-start.9 = (bf16[256,256]{1,0:T(8,128)(2,1)S(1)}, bf16[256,256]{1,0:T(8,128)(2,1)}, u32[]{:S(2)}) copy-start(bf16[256,256]{1,0:T(8,128)(2,1)} %refs_4_.3) | copy-start | bytes 393220
  11.5 7.9 %copy-start.10 = (bf16[256,256]{1,0:T(8,128)(2,1)S(1)}, bf16[256,256]{1,0:T(8,128)(2,1)}, u32[]{:S(2)}) copy-start(bf16[256,256]{1,0:T(8,128)(2,1)} %refs_5_.3) | copy-start | bytes 393220
  11.5 7.9 %copy-start.14 = (s32[512]{0:T(512)S(1)}, s32[512]{0:T(512)}, u32[]{:S(2)}) copy-start(s32[512]{0:T(512)} %param.19) | copy-start | bytes 6148
  19.4 9.2 %copy-start.2 = (bf16[3,3,256,256]{3,2,1,0:T(8,128)(2,1)S(1)}, bf16[3,3,256,256]{3,2,1,0:T(8,128)(2,1)}, u32[]{:S(2)}) copy-start(bf16[3,3,256,256]{3,2,1,0:T(8,128)(2,1)} %param.28) | copy-start | bytes 3538948
  19.4 9.2 %copy-start.3 = (bf16[3,3,256,128]{3,2,1,0:T(8,128)(2,1)S(1)}, bf16[3,3,256,128]{3,2,1,0:T(8,128)(2,1)}, u32[]{:S(2)}) copy-start(bf16[3,3,256,128]{3,2,1,0:T(8,128)(2,1)} %param.29) | copy-start | bytes 1769476
  23.8 12.6 %all-to-all-start.1 = ((bf16[8,64,256]{2,1,0:T(8,128)(2,1)}), bf16[8,64,256]{2,1,0:T(8,128)(2,1)S(1)}, u32[]{:S(2)}, u32[]{:S(2)}) async-start(bf16[8,64,256]{2,1,0:T(8,128)(2,1)} %shard_map.161), calls=%async_computation.1 | async-start | bytes 524288 | tf_op jit(solution)/shard_map/all_to_all | solution.py:326
  27.4 1.3 %collective-permute-start.2 = (bf16[128,256]{1,0:T(8,128)(2,1)S(1)}, bf16[128,256]{1,0:T(8,128)(2,1)S(1)}, u32[]{:S(2)}, u32[]{:S(2)}) collective-permute-start(bf16[128,256]{1,0:T(8,128)(2,1)S(1)} %get-tuple-element.5.refs_0_), channel_id=1, source_target_pairs={{0,1},{1,0},{2,3},{3,2},{4,5},{5,4},{6,7},{7,6},{8,9},{9,8},{10,11... | collective-permute-start | bytes 196616 | tf_op jit(solution)/shard_map/ppermute | solution.py:310
  28.6 7.8 %copy-start.1 = (bf16[256,256]{1,0:T(8,128)(2,1)S(1)}, bf16[256,256]{1,0:T(8,128)(2,1)}, u32[]{:S(2)}) copy-start(bf16[256,256]{1,0:T(8,128)(2,1)} %refs_2_.3) | copy-start | bytes 393220

commit v3 on v2

--- a/solution.py
+++ b/solution.py
@@ -101,7 +101,22 @@
 
 
 def attend_body(
-    pixels, tokens, w_query, w_key, w_value, visible, w_out, state, other, flags, context, edge
+    pixels,
+    tokens,
+    w_query,
+    w_key,
+    w_value,
+    visible,
+    w_out,
+    state,
+    w_time_query,
+    w_time_key,
+    w_time_value,
+    other,
+    flags,
+    context,
+    edge,
+    w_time,
 ):
     half, channels = other.shape
     head_dim = channels // HEADS
@@ -130,64 +145,85 @@
     start = pl.multiple_of((1 - lax.axis_index("band")) * (query.shape[0] - count), count)
     edge[:, :LANES] = state()[pl.ds(start, count), :]
     edge[:, LANES:] = context[pl.ds(start, count), :]
-
-
-def temporal_body(packed, query_frame, w_query, w_key, w_value, out, flag_cols, frame_cols, result, sems):
+    for i, weight in enumerate((w_time_query, w_time_key, w_time_value)):
+        w_time[i * channels : (i + 1) * channels, :] = weight()[...].astype(f32).T.astype(bf16)
+
+
+def temporal_body(packed, query_frame, w_all, out, result, sems):
     frames, share, channels = out.shape
     head_dim = channels // HEADS
-    columns = -(-frames * HEADS // LANES) * LANES
+    tiles = frames * share // LANES
+    beside = LANES // share
     me = lax.axis_index("frame")
-    first = me * share
-    group, start = first // LANES, pl.multiple_of(first % LANES, share)
-    flags = packed[:, 2 * share :, :].reshape(frames * MASK_ROWS, LANES)
-    flag_cols[...] = flags.astype(f32).T
-    asked = query_frame[pl.ds(group, 1), :].astype(f32)
-    frame_cols[...] = jnp.broadcast_to(asked, (LANES, LANES)).T
-    flags = flag_cols[pl.ds(start, share), :]
-    asked = frame_cols[pl.ds(start, share), :1]
+    piece = lax.broadcasted_iota(jnp.int32, (1, LANES), 1) // share
+
+    def fold(x, add=jnp.add):
+        shift = share
+        while shift < LANES:
+            x = add(x, pltpu.roll(x, shift, 1))
+            shift *= 2
+        return x
+
+    def everywhere(x, which):
+        return fold(jnp.where(piece == which, x, 0.0))
+
+    asked = query_frame[pl.ds(me * share // LANES, 1), :].astype(f32)
+    asked = everywhere(asked, me % beside)
+    flags = everywhere(packed[:, 2 * share, :].astype(f32), me % beside)
+    seen = []
+    for tile in range(tiles):
+        row = jnp.zeros((1, LANES), f32)
+        for o in range(beside):
+            g = tile * beside + o
+            row = jnp.where(piece == o, flags[g : g + 1, :], row)
+        seen.append(row > 0.5)
 
     left = packed[:, :share, :].reshape(frames * share, LANES)
     right = packed[:, share : 2 * share, :].reshape(frames * share, LANES)
     rows = jnp.concatenate([left, right], axis=1)
-    shape = (frames, share, channels)
-    query = dot(rows, w_query[...]).astype(bf16).astype(f32).reshape(shape)
-    key = dot(rows, w_key[...]).astype(bf16).astype(f32).reshape(shape)
-    value = dot(rows, w_value[...]).astype(bf16).astype(f32).reshape(shape)
-    anchor = jnp.zeros((share, channels), f32)
-    for s in range(frames):
-        anchor = jnp.where(asked == s, query[s], anchor)
-
-    head_of_row = lax.broadcasted_iota(jnp.int32, (channels, columns), 0) // head_dim
-    column = lax.broadcasted_iota(jnp.int32, (channels, columns), 1)
-    head_of_col = lax.broadcasted_iota(jnp.int32, (columns, channels), 1) // head_dim
-    line = lax.broadcasted_iota(jnp.int32, (columns, channels), 0)
-    scores = jnp.zeros((frames * share, columns), f32)
-    for s in range(frames):
-        joint = (query[s] + anchor).astype(bf16).astype(f32)
-        product = (key * joint[None]).reshape(frames * share, channels)
-        high = product.astype(bf16)
-        low = (product - high.astype(f32)).astype(bf16)
-        gather = jnp.where(column == head_of_row + s * HEADS, 1.0, 0.0).astype(bf16)
-        scores = scores + dot(high, gather) + dot(low, gather)
-    scores = scores.reshape(frames, share, columns) * head_dim**-0.5
-    seen = [
-        jnp.where(flags[:, g * MASK_ROWS : g * MASK_ROWS + 1] > 0.5, scores[g], HIDDEN)
-        for g in range(frames)
-    ]
-    top = seen[0]
-    for g in range(1, frames):
-        top = jnp.maximum(top, seen[g])
-    raised = [jnp.exp(x - top) for x in seen]
-    total = raised[0]
-    for g in range(1, frames):
-        total = total + raised[g]
-    weights = jnp.concatenate([x / total for x in raised], axis=0).astype(bf16)
+    projected = lax.dot_general(
+        w_all[...], rows, (((1,), (1,)), ((), ())), preferred_element_type=f32
+    )
+    projected = projected.astype(bf16).astype(f32)
+    query, key, value = (
+        [
+            projected[i * channels : (i + 1) * channels, t * LANES : (t + 1) * LANES]
+            for t in range(tiles)
+        ]
+        for i in range(3)
+    )
+    anchor = jnp.zeros((channels, LANES), f32)
+    for tile in range(tiles):
+        frame = (piece + tile * beside).astype(f32)
+        anchor = anchor + jnp.where(asked == frame, query[tile], 0.0)
+    anchor = fold(anchor)
+
     copies = []
-    for s in range(frames):
-        spread = jnp.where(line == head_of_col + s * HEADS, 1.0, 0.0).astype(bf16)
-        wide = dot(weights, spread).reshape(shape)
-        result[s] = jnp.sum(wide * value, axis=0).astype(bf16)
-        copies.append(pltpu.make_async_copy(result.at[s], out.at[s], sems.at[s]))
+    for tile in range(tiles):
+        attended = jnp.zeros((channels, LANES), f32)
+        for o in range(beside):
+            joint = (everywhere(query[tile], o) + anchor).astype(bf16).astype(f32)
+            scores = []
+            for other in range(tiles):
+                product = (key[other] * joint).reshape(HEADS, head_dim, LANES)
+                score = jnp.sum(product, axis=1) * head_dim**-0.5
+                scores.append(jnp.where(seen[other], score, HIDDEN))
+            top = scores[0]
+            for score in scores[1:]:
+                top = jnp.maximum(top, score)
+            top = fold(top, jnp.maximum)
+            raised = [jnp.exp(score - top) for score in scores]
+            total = fold(sum(raised[1:], raised[0]))
+            summed = jnp.zeros((HEADS, head_dim, LANES), f32)
+            for other in range(tiles):
+                weight = (raised[other] / total).astype(bf16).astype(f32)
+                here = value[other].reshape(HEADS, head_dim, LANES)
+                summed = summed + here * weight[:, None, :]
+            summed = fold(summed.reshape(channels, LANES))
+            attended = jnp.where(piece == o, summed, attended)
+        some = pl.ds(tile * beside, beside)
+        result[some] = attended.T.astype(bf16).reshape(beside, share, channels)
+        copies.append(pltpu.make_async_copy(result.at[some], out.at[some], sems.at[tile]))
         copies[-1].start()
     for copy in copies:
         copy.wait()
@@ -288,11 +324,12 @@
     )
     arrived = lax.all_to_all(packed, "frame", split_axis=0, concat_axis=0, tiled=True)
 
-    context, edge = call(
+    context, edge, w_time = call(
         attend_body,
         (
             jax.ShapeDtypeStruct((local, hidden), bf16),
             jax.ShapeDtypeStruct((beyond, 2 * hidden), bf16),
+            jax.ShapeDtypeStruct((3 * channels, channels), bf16),
         ),
         (other, flags),
         (
@@ -304,6 +341,9 @@
             visible,
             pixel_out,
             flat_state,
+            time_query,
+            time_key,
+            time_value,
         ),
         flops=4 * local * 2 * half * channels * HEADS,
     )
@@ -312,16 +352,13 @@
     attended = call(
         temporal_body,
         jax.ShapeDtypeStruct((frames, share, channels), bf16),
-        (arrived, query_frame.reshape(groups, LANES), time_query, time_key, time_value),
+        (arrived, query_frame.reshape(groups, LANES), w_time),
         scratch=[
-            pltpu.VMEM((LANES, frames * MASK_ROWS), f32),
-            pltpu.VMEM((LANES, LANES), f32),
             pltpu.VMEM((frames, share, channels), bf16),
             pltpu.SemaphoreType.DMA((frames,)),
         ],
         place=HBM,
         flops=6 * half * channels * channels * 4,
-        after=(edge,),
     )
     returned = lax.all_to_all(attended, "frame", split_axis=0, concat_axis=0, tiled=True)
 

time: 37.7 us -> 36.7 us (0.973)
  Pallas kernels: 17.2 us -> 16.3 us
  starting transfers between devices: 11.5 us -> 12.2 us
  waiting for transfers between devices: 7.73 us -> 7.04 us
    pallas_call x5, Pallas kernels: 17.2 us -> 16.3 us  [call(): pl.pallas_call(whole, out_shape=out, in_specs=[LATER] * len(after) + [HBM...]
    all_to_all x1, waiting for transfers between devices: 2.54 us -> 1.66 us  [on_device(): lax.all_to_all(packed, 'frame', split_axis=0, concat_axis=0, tiled=True)]
    all_to_all x1, starting transfers between devices: 3.6 us -> 4.32 us  [on_device(): lax.all_to_all(attended, 'frame', split_axis=0, concat_axis=0, tiled=True)]
  transfers between devices with their start and end apart: 5 -> 5, of which waited for: 4 -> 4; matrix products, arithmetic and copies ran while one was open for 0% -> 0% of each run, Pallas kernels for 27% -> 31%
where the time goes in v3:
time: 36.7 us; the launch traced here: 36.4 us
  Pallas kernels  16.3 us (44%)
  starting transfers between devices  12.2 us (33%)
  waiting for transfers between devices  7.04 us (19%)
  between operations  0.85 us (2%)
    pallas_call x5, Pallas kernels, call(): pl.pallas_call(whole, out_shape=out, in_specs=[LATER] * len(after) + [HBM...  16.3 us
    all_to_all x1, starting transfers between devices, on_device(): lax.all_to_all(packed, 'frame', split_axis=0, concat_axis=0, tiled=True)  7.29 us
    all_to_all x1, starting transfers between devices, on_device(): lax.all_to_all(attended, 'frame', split_axis=0, concat_axis=0, tiled=True)  4.32 us
    all_to_all x1, waiting for transfers between devices, on_device(): lax.all_to_all(attended, 'frame', split_axis=0, concat_axis=0, tiled=True)  3.1 us
    all_to_all x1, waiting for transfers between devices, on_device(): lax.all_to_all(packed, 'frame', split_axis=0, concat_axis=0, tiled=True)  1.66 us
    ppermute x1, waiting for transfers between devices, on_device(): halo = lax.ppermute(edge, 'band', swap)  1.25 us
    ppermute x1, waiting for transfers between devices, on_device(): flags = lax.ppermute(visible, 'band', swap)  1.02 us
  transfers between devices with their start and end apart: 5, of which 4 were waited for; matrix products, arithmetic and copies ran while one was open for 0% of the time, Pallas kernels for 31%

profile of v3, /device:TPU:0, one launch (start us, length us, event | category | flops | bytes accessed | tf_op | source)
XLA Modules:
  0.0 36.4 jit_solution(2489469930142949528)
XLA Ops:
  0.6 0.0 copy-start
  0.6 0.0 copy-start.13
  0.7 0.0 copy-start.4
  0.7 0.0 copy-start.5
  0.7 0.0 copy-start.6
  0.7 0.0 copy-start.7
  0.7 0.0 copy-start.8
  0.7 0.0 copy-start.9
  0.7 0.0 copy-start.10
  0.7 0.0 copy-start.11
  0.7 0.0 copy-start.12
  0.7 1.8 %shard_map.160 = bf16[8,144,128]{2,1,0:T(8,128)(2,1)} custom-call(bf16[8,64,256]{2,1,0:T(8,128)(2,1)} %bitcast.12, s32[4,128]{1,0:T(4,128)} %bitcast.21), custom_call_target="tpu_custom_call" | custom-call | flops 10000000000 | tf_op jit(solution)/shard_map/pallas_call | solution.py:54
  2.5 7.3 %all-to-all-start = ((bf16[8,144,128]{2,1,0:T(8,128)(2,1)}), bf16[8,144,128]{2,1,0:T(8,128)(2,1)S(1)}, u32[]{:S(2)}, u32[]{:S(2)}) async-start(bf16[8,144,128]{2,1,0:T(8,128)(2,1)} %shard_map.160), calls=%async_computation | async-start | bytes 589824 | tf_op jit(solution)/shard_map/all_to_all | solution.py:325
  9.8 0.1 collective-permute-start
  9.9 0.5 %collective-permute-start.1 = (s32[1,512]{1,0:T(1,128)S(1)}, s32[1,512]{1,0:T(1,128)S(1)}, u32[]{:S(2)}, u32[]{:S(2)}) collective-permute-start(s32[1,512]{1,0:T(1,128)S(1)} %copy-done.13), channel_id=1, source_target_pairs={{0,1},{1,0},{2,3},{3,2},{4,5},{5,4},{6,7},{7,6},{8,9},{9,8},{10,11... | collective-permute-start | bytes 6152 | tf_op jit(solution)/shard_map/ppermute | solution.py:310
  10.4 1.0 %collective-permute-done.1.refs_12_ = s32[1,512]{1,0:T(1,128)S(1)} collective-permute-done((s32[1,512]{1,0:T(1,128)S(1)}, s32[1,512]{1,0:T(1,128)S(1)}, u32[]{:S(2)}, u32[]{:S(2)}) %collective-permute-start.1) | collective-permute-done | bytes 2080 | tf_op jit(solution)/shard_map/ppermute | solution.py:310
  11.4 0.0 collective-permute-done.refs_11_
  11.4 0.0 copy-done.5
  11.5 0.0 copy-done.6
  11.5 0.0 copy-done.7
  11.5 0.0 copy-done.8
  11.5 0.0 copy-done.9
  11.5 0.0 copy-start.14
  11.5 6.2 %shard_map.158 = (bf16[256,128]{1,0:T(8,128)(2,1)S(1)}, bf16[128,256]{1,0:T(8,128)(2,1)S(1)}, bf16[768,256]{1,0:T(8,128)(2,1)S(1)}) custom-call(bf16[256,256]{1,0:T(8,128)(2,1)S(1)} %bitcast.18, bf16[512,256]{1,0:T(8,128)(2,1)S(1)} %bitcast.14, bf16[256,256]{1,0:T(8,128)(2,1)S(1)} %copy-done.5, bf16[256,256]{1,0:T(8,128)(2,1)S(1)} %copy-done.6, ...), custom_call_target="tpu_custom_call" | custom-call | flops 2147483648 | bytes 1576960 | tf_op jit(solution)/shard_map/pallas_call | solution.py:54
  17.8 1.7 %all-to-all-done.refs_0_ = bf16[8,144,128]{2,1,0:T(8,128)(2,1)S(1)} async-done(((bf16[8,144,128]{2,1,0:T(8,128)(2,1)}), bf16[8,144,128]{2,1,0:T(8,128)(2,1)S(1)}, u32[]{:S(2)}, u32[]{:S(2)}) %all-to-all-start) | async-done | bytes 294944 | tf_op jit(solution)/shard_map/all_to_all | solution.py:325
  19.5 2.5 %shard_map.161 = bf16[8,64,256]{2,1,0:T(8,128)(2,1)} custom-call(bf16[8,144,128]{2,1,0:T(8,128)(2,1)S(1)} %all-to-all-done.refs_0_, s32[4,128]{1,0:T(4,128)S(1)} %bitcast.22, bf16[768,256]{1,0:T(8,128)(2,1)S(1)} %get-tuple-element.7.refs_2_), custom_call_target="tpu_custom_call" | custom-call | flops 805306368 | bytes 690176 | tf_op jit(solution)/shard_map/pallas_call | solution.py:54
  21.9 4.3 %all-to-all-start.1 = ((bf16[8,64,256]{2,1,0:T(8,128)(2,1)}), bf16[8,64,256]{2,1,0:T(8,128)(2,1)S(1)}, u32[]{:S(2)}, u32[]{:S(2)}) async-start(bf16[8,64,256]{2,1,0:T(8,128)(2,1)} %shard_map.161), calls=%async_computation.1 | async-start | bytes 524288 | tf_op jit(solution)/shard_map/all_to_all | solution.py:363
  26.2 0.0 collective-permute-start.2
  26.2 1.2 %collective-permute-done.2.refs_2_ = bf16[128,256]{1,0:T(8,128)(2,1)S(1)} collective-permute-done((bf16[128,256]{1,0:T(8,128)(2,1)S(1)}, bf16[128,256]{1,0:T(8,128)(2,1)S(1)}, u32[]{:S(2)}, u32[]{:S(2)}) %collective-permute-start.2) | collective-permute-done | bytes 65568 | tf_op jit(solution)/shard_map/ppermute | solution.py:350
  27.5 4.9 %shard_map.159 = bf16[256,128]{1,0:T(8,128)(2,1)} custom-call(bf16[256,128]{1,0:T(8,128)(2,1)S(1)} %bitcast.20, bf16[256,128]{1,0:T(8,128)(2,1)S(1)} %get-tuple-element.5.refs_1_, bf16[128,256]{1,0:T(8,128)(2,1)S(1)} %collective-permute-done.2.refs_2_, bf16[9,256,256]{2,1,0:T(8,128)(2,1)S(1)} %bitcast.16, bf16[9,256,128]{2,1,0:T(8,128)(2,1)S(1)} %bitcast.17), custom_call_target="tpu_custom_call" | custom-call | flops 1358954496 | bytes 1966080 | tf_op jit(solution)/shard_map/pallas_call | solution.py:54
  32.4 3.1 %all-to-all-done.1 = bf16[8,64,256]{2,1,0:T(8,128)(2,1)S(1)} async-done(((bf16[8,64,256]{2,1,0:T(8,128)(2,1)}), bf16[8,64,256]{2,1,0:T(8,128)(2,1)S(1)}, u32[]{:S(2)}, u32[]{:S(2)}) %all-to-all-start.1) | async-done | bytes 262176 | tf_op jit(solution)/shard_map/all_to_all | solution.py:363
  35.5 0.9 %shard_map.162 = bf16[512,256]{1,0:T(8,128)(2,1)} custom-call(bf16[512,256]{1,0:T(8,128)(2,1)S(1)} %bitcast.11, bf16[512,256]{1,0:T(8,128)(2,1)S(1)} %bitcast.15, bf16[256,256]{1,0:T(8,128)(2,1)S(1)} %copy-done.1), custom_call_target="tpu_custom_call" | custom-call | flops 67108864 | bytes 655360 | tf_op jit(solution)/shard_map/pallas_call | solution.py:54
  (13 shorter events, 0.0 us)
Async XLA Ops:
  0.6 9.2 %copy-start = (bf16[1,512,256]{2,1,0:T(8,128)(2,1)S(1)}, bf16[1,512,256]{2,1,0:T(8,128)(2,1)}, u32[]{:S(2)}) copy-start(bf16[1,512,256]{2,1,0:T(8,128)(2,1)} %param.17) | copy-start | bytes 786436
  0.6 9.3 %copy-start.13 = (s32[1,512]{1,0:T(1,128)S(1)}, s32[1,512]{1,0:T(1,128)}, u32[]{:S(2)}) copy-start(s32[1,512]{1,0:T(1,128)} %refs_5_.1) | copy-start | bytes 6148
  0.7 10.8 %copy-start.4 = (bf16[1,8,32,256]{3,2,1,0:T(8,128)(2,1)S(1)}, bf16[1,8,32,256]{3,2,1,0:T(8,128)(2,1)}, u32[]{:S(2)}) copy-start(bf16[1,8,32,256]{3,2,1,0:T(8,128)(2,1)} %param.15) | copy-start | bytes 393220
  0.7 10.8 %copy-start.5 = (bf16[256,256]{1,0:T(8,128)(2,1)S(1)}, bf16[256,256]{1,0:T(8,128)(2,1)}, u32[]{:S(2)}) copy-start(bf16[256,256]{1,0:T(8,128)(2,1)} %refs_2_.2) | copy-start | bytes 393220
  0.7 10.8 %copy-start.6 = (bf16[256,256]{1,0:T(8,128)(2,1)S(1)}, bf16[256,256]{1,0:T(8,128)(2,1)}, u32[]{:S(2)}) copy-start(bf16[256,256]{1,0:T(8,128)(2,1)} %refs_3_.1) | copy-start | bytes 393220
  0.7 10.8 %copy-start.7 = (bf16[256,256]{1,0:T(8,128)(2,1)S(1)}, bf16[256,256]{1,0:T(8,128)(2,1)}, u32[]{:S(2)}) copy-start(bf16[256,256]{1,0:T(8,128)(2,1)} %refs_4_.1) | copy-start | bytes 393220
  0.7 10.8 %copy-start.8 = (bf16[256,256]{1,0:T(8,128)(2,1)S(1)}, bf16[256,256]{1,0:T(8,128)(2,1)}, u32[]{:S(2)}) copy-start(bf16[256,256]{1,0:T(8,128)(2,1)} %refs_8_.1) | copy-start | bytes 393220
  0.7 10.8 %copy-start.9 = (bf16[256,256]{1,0:T(8,128)(2,1)S(1)}, bf16[256,256]{1,0:T(8,128)(2,1)}, u32[]{:S(2)}) copy-start(bf16[256,256]{1,0:T(8,128)(2,1)} %refs_9_.1) | copy-start | bytes 393220
  0.7 10.8 %copy-start.10 = (bf16[256,256]{1,0:T(8,128)(2,1)S(1)}, bf16[256,256]{1,0:T(8,128)(2,1)}, u32[]{:S(2)}) copy-start(bf16[256,256]{1,0:T(8,128)(2,1)} %refs_10_.1) | copy-start | bytes 393220
  0.7 10.8 %copy-start.11 = (bf16[256,128]{1,0:T(8,128)(2,1)S(1)}, bf16[256,128]{1,0:T(8,128)(2,1)}, u32[]{:S(2)}) copy-start(bf16[256,128]{1,0:T(8,128)(2,1)} %refs_6_.1) | copy-start | bytes 196612
  0.7 10.8 %copy-start.12 = (bf16[1,8,32,128]{3,2,1,0:T(8,128)(2,1)S(1)}, bf16[1,8,32,128]{3,2,1,0:T(8,128)(2,1)}, u32[]{:S(2)}) copy-start(bf16[1,8,32,128]{3,2,1,0:T(8,128)(2,1)} %param.16) | copy-start | bytes 196612
  2.5 16.9 %all-to-all-start = ((bf16[8,144,128]{2,1,0:T(8,128)(2,1)}), bf16[8,144,128]{2,1,0:T(8,128)(2,1)S(1)}, u32[]{:S(2)}, u32[]{:S(2)}) async-start(bf16[8,144,128]{2,1,0:T(8,128)(2,1)} %shard_map.160), calls=%async_computation | async-start | bytes 589824 | tf_op jit(solution)/shard_map/all_to_all | solution.py:325
  9.8 1.6 %collective-permute-start = (bf16[512,256]{1,0:T(8,128)(2,1)S(1)}, bf16[512,256]{1,0:T(8,128)(2,1)S(1)}, u32[]{:S(2)}, u32[]{:S(2)}) collective-permute-start(bf16[512,256]{1,0:T(8,128)(2,1)S(1)} %bitcast.13), channel_id=1, source_target_pairs={{0,1},{1,0},{2,3},{3,2},{4,5},{5,4},{6,7},{7,6},{8,9},{9,8},{10,11... | collective-permute-start | bytes 786440 | tf_op jit(solution)/shard_map/ppermute | solution.py:309
  9.9 1.5 %collective-permute-start.1 = (s32[1,512]{1,0:T(1,128)S(1)}, s32[1,512]{1,0:T(1,128)S(1)}, u32[]{:S(2)}, u32[]{:S(2)}) collective-permute-start(s32[1,512]{1,0:T(1,128)S(1)} %copy-done.13), channel_id=1, source_target_pairs={{0,1},{1,0},{2,3},{3,2},{4,5},{5,4},{6,7},{7,6},{8,9},{9,8},{10,11... | collective-permute-start | bytes 6152 | tf_op jit(solution)/shard_map/ppermute | solution.py:310
  11.5 7.9 %copy-start.14 = (s32[512]{0:T(512)S(1)}, s32[512]{0:T(512)}, u32[]{:S(2)}) copy-start(s32[512]{0:T(512)} %param.19) | copy-start | bytes 6148
  19.5 8.0 %copy-start.2 = (bf16[3,3,256,256]{3,2,1,0:T(8,128)(2,1)S(1)}, bf16[3,3,256,256]{3,2,1,0:T(8,128)(2,1)}, u32[]{:S(2)}) copy-start(bf16[3,3,256,256]{3,2,1,0:T(8,128)(2,1)} %param.28) | copy-start | bytes 3538948
  19.5 8.0 %copy-start.3 = (bf16[3,3,256,128]{3,2,1,0:T(8,128)(2,1)S(1)}, bf16[3,3,256,128]{3,2,1,0:T(8,128)(2,1)}, u32[]{:S(2)}) copy-start(bf16[3,3,256,128]{3,2,1,0:T(8,128)(2,1)} %param.29) | copy-start | bytes 1769476
  21.9 13.5 %all-to-all-start.1 = ((bf16[8,64,256]{2,1,0:T(8,128)(2,1)}), bf16[8,64,256]{2,1,0:T(8,128)(2,1)S(1)}, u32[]{:S(2)}, u32[]{:S(2)}) async-start(bf16[8,64,256]{2,1,0:T(8,128)(2,1)} %shard_map.161), calls=%async_computation.1 | async-start | bytes 524288 | tf_op jit(solution)/shard_map/all_to_all | solution.py:363
  26.2 1.3 %collective-permute-start.2 = (bf16[128,256]{1,0:T(8,128)(2,1)S(1)}, bf16[128,256]{1,0:T(8,128)(2,1)S(1)}, u32[]{:S(2)}, u32[]{:S(2)}) collective-permute-start(bf16[128,256]{1,0:T(8,128)(2,1)S(1)} %get-tuple-element.6), channel_id=1, source_target_pairs={{0,1},{1,0},{2,3},{3,2},{4,5},{5,4},{6,7},{7,6},{8,9},{9,8},{10,11... | collective-permute-start | bytes 196616 | tf_op jit(solution)/shard_map/ppermute | solution.py:350
  27.5 8.0 %copy-start.1 = (bf16[256,256]{1,0:T(8,128)(2,1)S(1)}, bf16[256,256]{1,0:T(8,128)(2,1)}, u32[]{:S(2)}) copy-start(bf16[256,256]{1,0:T(8,128)(2,1)} %refs_2_.3) | copy-start | bytes 393220

commit v4 on v3

--- a/solution.py
+++ b/solution.py
@@ -10,6 +10,7 @@
 LANES = 128
 MASK_ROWS = 16
 HIDDEN = -1e30
+LOG2E = 1.4426950408889634
 
 f32 = jnp.float32
 bf16 = jnp.bfloat16
@@ -22,50 +23,43 @@
     return jnp.dot(a, b, preferred_element_type=f32)
 
 
-def call(body, out, near, far=(), scratch=(), flops=0, after=(), raw=(), grant=24 * 2**20, place=VMEM):
-    moved = sum(x.size * x.dtype.itemsize for x in (*near, *far))
-
-    def whole(*refs):
-        refs = refs[len(after) :]
-        if not far:
-            return body(*refs)
-        sources = refs[: len(far)]
-        buffers, arrived = refs[-len(far) - 1 : -1], refs[-1]
-        copies = [
-            pltpu.make_async_copy(source, buffer, arrived.at[i])
-            for i, (source, buffer) in enumerate(zip(sources, buffers))
-        ]
-        for copy in copies:
-            copy.start()
-
-        def fetch(copy, buffer):
-            def wait():
-                copy.wait()
-                return buffer
-
-            return wait
-
-        fetched = [fetch(c, b) for c, b in zip(copies, buffers)]
-        return body(*fetched, *refs[len(far) : -len(far) - 1])
-
-    buffers = [pltpu.VMEM(x.shape, x.dtype) for x in far]
-    if far:
-        buffers.append(pltpu.SemaphoreType.DMA((len(far),)))
+def call(body, out, near, scratch=(), flops=0, after=(), raw=(), grant=24 * 2**20, place=VMEM):
+    args = (*raw, *near)
     return pl.pallas_call(
-        whole,
+        lambda *refs: body(*refs[len(after) :]),
         out_shape=out,
-        in_specs=[LATER] * len(after) + [HBM] * len(raw + far) + [VMEM] * len(near),
+        in_specs=[LATER] * len(after) + [HBM] * len(raw) + [VMEM] * len(near),
         out_specs=jax.tree.map(lambda _: place, out),
-        scratch_shapes=[*scratch, *buffers],
+        scratch_shapes=scratch,
         compiler_params=pltpu.CompilerParams(vmem_limit_bytes=grant),
-        cost_estimate=pl.CostEstimate(flops=flops, bytes_accessed=moved, transcendentals=0),
-    )(*after, *raw, *far, *near)
+        cost_estimate=pl.CostEstimate(
+            flops=flops,
+            bytes_accessed=sum(x.size * x.dtype.itemsize for x in args),
+            transcendentals=0,
+        ),
+    )(*after, *args)
+
+
+def turned(slot, frames):
+    return (slot + frames // 2) % frames
+
+
+def exchange(x):
+    frames = lax.axis_size("frame")
+    return lax.all_to_all(
+        x,
+        "frame",
+        split_axis=0,
+        concat_axis=0,
+        tiled=True,
+        axis_index_groups=[[turned(i, frames) for i in range(frames)]],
+    )
 
 
 def pack_body(tokens, visible, out, flags, packed, sems):
     frames, rows, _ = out.shape
     share = tokens.shape[1]
-    chunks = 2
+    chunks = 4
     step = frames // chunks
     first = pltpu.make_async_copy(visible, flags, sems.at[0])
     first.start()
@@ -75,7 +69,7 @@
         coming.append(
             [
                 pltpu.make_async_copy(
-                    tokens.at[some, :, pl.ds(c * LANES, LANES)],
+                    tokens.at[pl.ds(turned(i * step, frames), step), :, pl.ds(c * LANES, LANES)],
                     packed.at[some, pl.ds(c * share, share), :],
                     sems.at[1 + 2 * i + c],
                 )
@@ -87,7 +81,7 @@
             copy.start()
     first.wait()
     for g in range(frames):
-        group = flags[g * share // LANES, :].astype(f32)
+        group = flags[turned(g, frames) * share // LANES, :].astype(f32)
         packed[g, 2 * share :, :] = jnp.broadcast_to(group[None], (MASK_ROWS, LANES)).astype(bf16)
     going = []
     for i, copies in enumerate(coming):
@@ -100,53 +94,58 @@
         copy.wait()
 
 
+def project_body(
+    pixels, tokens, w_query, w_key, w_value, w_time_query, w_time_key, w_time_value, query, key, value, w_time
+):
+    query[...] = dot(pixels[...], w_query[...]).astype(bf16)
+    key[...] = dot(tokens[...], w_key[...]).astype(bf16)
+    value[...] = dot(tokens[...], w_value[...]).astype(bf16)
+    channels = w_time_query.shape[0]
+    for i, weight in enumerate((w_time_query, w_time_key, w_time_value)):
+        w_time[i * channels : (i + 1) * channels, :] = weight[...].astype(f32).T.astype(bf16)
+
+
 def attend_body(
-    pixels,
-    tokens,
-    w_query,
-    w_key,
-    w_value,
-    visible,
-    w_out,
-    state,
-    w_time_query,
-    w_time_key,
-    w_time_value,
-    other,
-    flags,
-    context,
-    edge,
-    w_time,
+    query, key, value, other, visible, flags, w_key, w_value, w_out, state, context, edge
 ):
-    half, channels = other.shape
+    channels = query.shape[1]
     head_dim = channels // HEADS
-    query = dot(pixels()[...], w_query()[...]).astype(bf16)
-    rows = jnp.concatenate([tokens()[...], other[...]], axis=0)
-    key = dot(rows, w_key()[...]).astype(bf16)
-    value = dot(rows, w_value()[...]).astype(bf16)
-    bias = jnp.where(jnp.concatenate([visible()[...], flags[...]], axis=1) > 0, 0.0, HIDDEN)
-    head_of = lax.broadcasted_iota(jnp.int32, (1, channels), 1) // head_dim
-    scale = head_dim**-0.5
-    attended = jnp.zeros(query.shape, f32)
-    for head in range(HEADS):
-        mine = head_of == head
-        masked = jnp.where(mine, query, jnp.zeros_like(query))
-        scores = lax.dot_general(
-            masked, key, (((1,), (1,)), ((), ())), preferred_element_type=f32
-        )
-        scores = scores + bias
-        top = jnp.max(scores, axis=1, keepdims=True)
-        weights = jnp.exp((scores - top) * scale)
-        total = jnp.sum(weights, axis=1, keepdims=True)
-        summed = dot(weights.astype(bf16), value)
-        attended = jnp.where(mine, summed / total, attended)
-    context[...] = dot(attended.astype(bf16), w_out()[...]).astype(bf16)
+    keys = jnp.concatenate([key[...], dot(other[...], w_key[...]).astype(bf16)], axis=0)
+    values = jnp.concatenate([value[...], dot(other[...], w_value[...]).astype(bf16)], axis=0)
+    tracks = keys.shape[0]
+    seen = jnp.concatenate([visible[...], flags[...]], axis=1).astype(f32)
+    seen = [seen[:, i * LANES : (i + 1) * LANES] for i in range(tracks // LANES)]
+    seen = jnp.concatenate(seen, axis=0).T
+    seen = jnp.concatenate([seen[:, i : i + 1] for i in range(tracks // LANES)], axis=0)
+    bias = jnp.where(seen > 0.5, 0.0, HIDDEN).astype(bf16)
+    lane = lax.broadcasted_iota(jnp.int32, (1, LANES), 1)
+    one = jnp.ones((1, 1), bf16)
+    scale = LOG2E * head_dim**-0.5
+    attended = []
+    for tile in range(channels // LANES):
+        some = slice(tile * LANES, (tile + 1) * LANES)
+        spares = (0, LANES - 1)
+        key_of = {x: jnp.where(lane == x, bias, keys[:, some]) for x in spares}
+        value_of = {x: jnp.where(lane == x, one, values[:, some]) for x in spares}
+        result = jnp.zeros((query.shape[0], LANES), f32)
+        for head in range(LANES // head_dim):
+            mine = lane // head_dim == head
+            spare = spares[0] if head else spares[1]
+            asking = jnp.where(mine, query[:, some], jnp.where(lane == spare, one, 0 * one))
+            scores = lax.dot_general(
+                asking, key_of[spare], (((1,), (1,)), ((), ())), preferred_element_type=f32
+            )
+            top = jnp.max(scores, axis=1, keepdims=True)
+            weights = jnp.exp2((scores - top) * scale).astype(bf16)
+            summed = dot(weights, value_of[spare])
+            total = summed[:, spare : spare + 1]
+            result = jnp.where(mine, summed * (1.0 / total), result)
+        attended.append(result.astype(bf16))
+    context[...] = dot(jnp.concatenate(attended, axis=1), w_out[...]).astype(bf16)
     count = edge.shape[0]
     start = pl.multiple_of((1 - lax.axis_index("band")) * (query.shape[0] - count), count)
-    edge[:, :LANES] = state()[pl.ds(start, count), :]
+    edge[:, :LANES] = state[pl.ds(start, count), :]
     edge[:, LANES:] = context[pl.ds(start, count), :]
-    for i, weight in enumerate((w_time_query, w_time_key, w_time_value)):
-        w_time[i * channels : (i + 1) * channels, :] = weight()[...].astype(f32).T.astype(bf16)
 
 
 def temporal_body(packed, query_frame, w_all, out, result, sems):
@@ -194,7 +193,7 @@
     )
     anchor = jnp.zeros((channels, LANES), f32)
     for tile in range(tiles):
-        frame = (piece + tile * beside).astype(f32)
+        frame = turned(piece + tile * beside, frames).astype(f32)
         anchor = anchor + jnp.where(asked == frame, query[tile], 0.0)
     anchor = fold(anchor)
 
@@ -272,7 +271,11 @@
 
 
 def output_body(returned, tokens, w_out, out):
-    out[...] = (tokens[...].astype(f32) + dot(returned[...], w_out[...])).astype(bf16)
+    rows = returned.shape[0] // 2
+    for i in range(2):
+        mine = slice(turned(i, 2) * rows, (turned(i, 2) + 1) * rows)
+        added = dot(returned[i * rows : (i + 1) * rows, :], w_out[...])
+        out[mine, :] = (tokens[mine, :].astype(f32) + added).astype(bf16)
 
 
 def on_device(
@@ -315,36 +318,42 @@
         scratch=[
             pltpu.VMEM((groups, LANES), jnp.int32),
             pltpu.VMEM((frames, 2 * share + MASK_ROWS, LANES), bf16),
-            pltpu.SemaphoreType.DMA((7,)),
+            pltpu.SemaphoreType.DMA((13,)),
         ],
         raw=(local_tokens.reshape(frames, share, channels), visible.reshape(groups, LANES)),
         flops=10**10,
         grant=60 * 2**20,
         place=HBM,
     )
-    arrived = lax.all_to_all(packed, "frame", split_axis=0, concat_axis=0, tiled=True)
-
-    context, edge, w_time = call(
-        attend_body,
+    arrived = exchange(packed)
+
+    query, key, value, w_time = call(
+        project_body,
         (
-            jax.ShapeDtypeStruct((local, hidden), bf16),
-            jax.ShapeDtypeStruct((beyond, 2 * hidden), bf16),
+            jax.ShapeDtypeStruct((local, channels), bf16),
+            jax.ShapeDtypeStruct((half, channels), bf16),
+            jax.ShapeDtypeStruct((half, channels), bf16),
             jax.ShapeDtypeStruct((3 * channels, channels), bf16),
         ),
-        (other, flags),
         (
             pixels.reshape(local, channels),
             local_tokens,
             pixel_query,
             pixel_key,
             pixel_value,
-            visible,
-            pixel_out,
-            flat_state,
             time_query,
             time_key,
             time_value,
         ),
+        flops=2 * (local + 2 * half) * channels * channels,
+    )
+    context, edge = call(
+        attend_body,
+        (
+            jax.ShapeDtypeStruct((local, hidden), bf16),
+            jax.ShapeDtypeStruct((beyond, 2 * hidden), bf16),
+        ),
+        (query, key, value, other, visible, flags, pixel_key, pixel_value, pixel_out, flat_state),
         flops=4 * local * 2 * half * channels * HEADS,
     )
     halo = lax.ppermute(edge, "band", swap)
@@ -353,6 +362,7 @@
         temporal_body,
         jax.ShapeDtypeStruct((frames, share, channels), bf16),
         (arrived, query_frame.reshape(groups, LANES), w_time),
+        after=(edge,),
         scratch=[
             pltpu.VMEM((frames, share, channels), bf16),
             pltpu.SemaphoreType.DMA((frames,)),
@@ -360,7 +370,7 @@
         place=HBM,
         flops=6 * half * channels * channels * 4,
     )
-    returned = lax.all_to_all(attended, "frame", split_axis=0, concat_axis=0, tiled=True)
+    returned = exchange(attended)
 
     refined = call(
         refine_body,

time: 36.7 us -> 32.9 us (0.90)
  waiting for transfers between devices: 7.04 us -> 2.83 us
  starting transfers between devices: 12.2 us -> 14 us
  Pallas kernels: 16.3 us -> 14.9 us
    all_to_all x2, waiting for transfers between devices: 4.76 us -> 0.97 us  [exchange(): lax.all_to_all(x, 'frame', split_axis=0, concat_axis=0, tiled=True, axis_...]
    all_to_all x2, starting transfers between devices: 11.6 us -> 13.5 us  [exchange(): lax.all_to_all(x, 'frame', split_axis=0, concat_axis=0, tiled=True, axis_...]
    pallas_call x5 -> x6, Pallas kernels: 16.3 us -> 14.9 us  [call(): pl.pallas_call(lambda *refs: body(*refs[len(after):]), out_shape=out, in_...]
    ppermute x1, waiting for transfers between devices: 1.02 us -> 0.61 us  [on_device(): flags = lax.ppermute(visible, 'band', swap)]
  transfers between devices with their start and end apart: 5 -> 5, of which waited for: 4 -> 3; matrix products, arithmetic and copies ran while one was open for 0% -> 0% of each run, Pallas kernels for 31% -> 30%
where the time goes in v4:
time: 32.9 us; the launch traced here: 32.5 us
  Pallas kernels  14.9 us (45%)
  starting transfers between devices  14 us (43%)
  waiting for transfers between devices  2.83 us (9%)
  between operations  0.8 us (2%)
    pallas_call x6, Pallas kernels, call(): pl.pallas_call(lambda *refs: body(*refs[len(after):]), out_shape=out, in_...  14.9 us
    all_to_all x2, starting transfers between devices, exchange(): lax.all_to_all(x, 'frame', split_axis=0, concat_axis=0, tiled=True, axis_...  13.5 us
    ppermute x1, waiting for transfers between devices, on_device(): halo = lax.ppermute(edge, 'band', swap)  1.25 us
    all_to_all x2, waiting for transfers between devices, exchange(): lax.all_to_all(x, 'frame', split_axis=0, concat_axis=0, tiled=True, axis_...  0.97 us
  transfers between devices with their start and end apart: 5, of which 3 were waited for; matrix products, arithmetic and copies ran while one was open for 0% of the time, Pallas kernels for 30%

profile of v4, /device:TPU:0, one launch (start us, length us, event | category | flops | bytes accessed | tf_op | source)
XLA Modules:
  0.0 32.5 jit_solution(16521912729041871684)
XLA Ops:
  0.6 0.0 copy-start
  0.6 0.0 copy-start.13
  0.7 0.0 copy-start.1
  0.7 0.0 copy-start.2
  0.7 0.0 copy-start.3
  0.7 0.0 copy-start.4
  0.7 0.0 copy-start.5
  0.7 1.7 %shard_map.161 = bf16[8,144,128]{2,1,0:T(8,128)(2,1)} custom-call(bf16[8,64,256]{2,1,0:T(8,128)(2,1)} %bitcast.12, s32[4,128]{1,0:T(4,128)} %bitcast.21), custom_call_target="tpu_custom_call" | custom-call | flops 10000000000 | bytes 264192 | tf_op jit(solution)/shard_map/pallas_call | solution.py:28
  2.4 0.0 copy-start.11
  2.5 0.0 copy-start.12
  2.5 8.0 %all-to-all-start = ((bf16[8,144,128]{2,1,0:T(8,128)(2,1)}), bf16[8,144,128]{2,1,0:T(8,128)(2,1)S(1)}, u32[]{:S(2)}, u32[]{:S(2)}) async-start(bf16[8,144,128]{2,1,0:T(8,128)(2,1)} %shard_map.161), calls=%async_computation | async-start | bytes 589824 | tf_op jit(solution)/shard_map/all_to_all | solution.py:49
  10.5 0.0 collective-permute-start
  10.5 0.5 %collective-permute-start.1 = (s32[1,512]{1,0:T(1,128)S(1)}, s32[1,512]{1,0:T(1,128)S(1)}, u32[]{:S(2)}, u32[]{:S(2)}) collective-permute-start(s32[1,512]{1,0:T(1,128)S(1)} %copy-done.13), channel_id=1, source_target_pairs={{0,1},{1,0},{2,3},{3,2},{4,5},{5,4},{6,7},{7,6},{8,9},{9,8},{10,11... | collective-permute-start | bytes 6152 | tf_op jit(solution)/shard_map/ppermute | solution.py:313
  11.0 0.0 copy-done.1
  11.0 0.0 copy-done.5
  11.0 0.0 copy-done.6
  11.0 0.0 copy-done.7
  11.0 0.4 %shard_map.158 = (bf16[256,256]{1,0:T(8,128)(2,1)S(1)}, bf16[512,256]{1,0:T(8,128)(2,1)S(1)}, bf16[512,256]{1,0:T(8,128)(2,1)S(1)}, bf16[768,256]{1,0:T(8,128)(2,1)S(1)}) custom-call(bf16[256,256]{1,0:T(8,128)(2,1)S(1)} %bitcast.16, bf16[512,256]{1,0:T(8,128)(2,1)S(1)} %bitcast.14, bf16[256,256]{1,0:T(8,128)(2,1)S(1)} %copy-done.2, ...), custom_call_target="tpu_custom_call" | custom-call | flops 167772160 | bytes 1179648 | tf_op jit(solution)/shard_map/pallas_call | solution.py:28
  11.4 0.6 %collective-permute-done.1.refs_5_ = s32[1,512]{1,0:T(1,128)S(1)} collective-permute-done((s32[1,512]{1,0:T(1,128)S(1)}, s32[1,512]{1,0:T(1,128)S(1)}, u32[]{:S(2)}, u32[]{:S(2)}) %collective-permute-start.1) | collective-permute-done | bytes 2080 | tf_op jit(solution)/shard_map/ppermute | solution.py:313
  12.0 0.0 collective-permute-done.refs_3_
  12.0 0.0 copy-start.14
  12.0 4.5 %shard_map.159 = (bf16[256,128]{1,0:T(8,128)(2,1)S(1)}, bf16[128,256]{1,0:T(8,128)(2,1)S(1)}) custom-call(bf16[256,256]{1,0:T(8,128)(2,1)S(1)} %get-tuple-element.8.refs_0_, bf16[512,256]{1,0:T(8,128)(2,1)S(1)} %get-tuple-element.9.refs_1_, bf16[512,256]{1,0:T(8,128)(2,1)S(1)} %get-tuple-element.10.refs_2_, ...), custom_call_target="tpu_custom_call" | custom-call | flops 2147483648 | bytes 1314816 | tf_op jit(solution)/shard_map/pallas_call | solution.py:28
  16.5 1.0 %all-to-all-done.refs_1_ = bf16[8,144,128]{2,1,0:T(8,128)(2,1)S(1)} async-done(((bf16[8,144,128]{2,1,0:T(8,128)(2,1)}), bf16[8,144,128]{2,1,0:T(8,128)(2,1)S(1)}, u32[]{:S(2)}, u32[]{:S(2)}) %all-to-all-start) | async-done | bytes 294944 | tf_op jit(solution)/shard_map/all_to_all | solution.py:49
  17.5 0.0 copy-done.14
  17.5 2.5 %shard_map.162 = bf16[8,64,256]{2,1,0:T(8,128)(2,1)} custom-call(bf16[128,256]{1,0:T(8,128)(2,1)S(1)} %get-tuple-element.12.refs_0_, bf16[8,144,128]{2,1,0:T(8,128)(2,1)S(1)} %all-to-all-done.refs_1_, s32[4,128]{1,0:T(4,128)S(1)} %bitcast.22, bf16[768,256]{1,0:T(8,128)(2,1)S(1)} %get-tuple-element.13.refs_3_), custom_call_target="tpu_custom_call" | custom-call | flops 805306368 | bytes 690176 | tf_op jit(solution)/shard_map/pallas_call | solution.py:28
  20.0 5.5 %all-to-all-start.1 = ((bf16[8,64,256]{2,1,0:T(8,128)(2,1)}), bf16[8,64,256]{2,1,0:T(8,128)(2,1)S(1)}, u32[]{:S(2)}, u32[]{:S(2)}) async-start(bf16[8,64,256]{2,1,0:T(8,128)(2,1)} %shard_map.162), calls=%async_computation.1 | async-start | bytes 524288 | tf_op jit(solution)/shard_map/all_to_all | solution.py:49
  25.5 0.0 collective-permute-start.2
  25.5 1.3 %collective-permute-done.2.refs_2_ = bf16[128,256]{1,0:T(8,128)(2,1)S(1)} collective-permute-done((bf16[128,256]{1,0:T(8,128)(2,1)S(1)}, bf16[128,256]{1,0:T(8,128)(2,1)S(1)}, u32[]{:S(2)}, u32[]{:S(2)}) %collective-permute-start.2) | collective-permute-done | bytes 65568 | tf_op jit(solution)/shard_map/ppermute | solution.py:359
  26.7 0.0 copy-done.9
  26.7 4.9 %shard_map.160 = bf16[256,128]{1,0:T(8,128)(2,1)} custom-call(bf16[256,128]{1,0:T(8,128)(2,1)S(1)} %bitcast.20, bf16[256,128]{1,0:T(8,128)(2,1)S(1)} %get-tuple-element.11.refs_1_, bf16[128,256]{1,0:T(8,128)(2,1)S(1)} %collective-permute-done.2.refs_2_, bf16[9,256,256]{2,1,0:T(8,128)(2,1)S(1)} %bitcast.17, bf16[9,256,128]{2,1,0:T(8,128)(2,1)S(1)} %bitcast.18), custom_call_target="tpu_custom_call" | custom-call | flops 1358954496 | bytes 1966080 | tf_op jit(solution)/shard_map/pallas_call | solution.py:28
  31.6 0.0 all-to-all-done.1
  31.6 0.9 %shard_map.163 = bf16[512,256]{1,0:T(8,128)(2,1)} custom-call(bf16[512,256]{1,0:T(8,128)(2,1)S(1)} %bitcast.11, bf16[512,256]{1,0:T(8,128)(2,1)S(1)} %bitcast.15, bf16[256,256]{1,0:T(8,128)(2,1)S(1)} %copy-done.8), custom_call_target="tpu_custom_call" | custom-call | flops 67108864 | bytes 655360 | tf_op jit(solution)/shard_map/pallas_call | solution.py:28
  (14 shorter events, 0.0 us)
Async XLA Ops:
  0.6 9.8 %copy-start = (bf16[1,512,256]{2,1,0:T(8,128)(2,1)S(1)}, bf16[1,512,256]{2,1,0:T(8,128)(2,1)}, u32[]{:S(2)}) copy-start(bf16[1,512,256]{2,1,0:T(8,128)(2,1)} %param.17) | copy-start | bytes 786436
  0.6 9.8 %copy-start.13 = (s32[1,512]{1,0:T(1,128)S(1)}, s32[1,512]{1,0:T(1,128)}, u32[]{:S(2)}) copy-start(s32[1,512]{1,0:T(1,128)} %refs_4_.3) | copy-start | bytes 6148
  0.7 10.3 %copy-start.1 = (bf16[1,8,32,256]{3,2,1,0:T(8,128)(2,1)S(1)}, bf16[1,8,32,256]{3,2,1,0:T(8,128)(2,1)}, u32[]{:S(2)}) copy-start(bf16[1,8,32,256]{3,2,1,0:T(8,128)(2,1)} %param.15) | copy-start | bytes 393220
  0.7 10.3 %copy-start.2 = (bf16[256,256]{1,0:T(8,128)(2,1)S(1)}, bf16[256,256]{1,0:T(8,128)(2,1)}, u32[]{:S(2)}) copy-start(bf16[256,256]{1,0:T(8,128)(2,1)} %refs_2_.2) | copy-start | bytes 393220
  0.7 10.3 %copy-start.3 = (bf16[256,256]{1,0:T(8,128)(2,1)S(1)}, bf16[256,256]{1,0:T(8,128)(2,1)}, u32[]{:S(2)}) copy-start(bf16[256,256]{1,0:T(8,128)(2,1)} %refs_5_.1) | copy-start | bytes 393220
  0.7 10.3 %copy-start.4 = (bf16[256,256]{1,0:T(8,128)(2,1)S(1)}, bf16[256,256]{1,0:T(8,128)(2,1)}, u32[]{:S(2)}) copy-start(bf16[256,256]{1,0:T(8,128)(2,1)} %refs_6_.2) | copy-start | bytes 393220
  0.7 10.3 %copy-start.5 = (bf16[256,256]{1,0:T(8,128)(2,1)S(1)}, bf16[256,256]{1,0:T(8,128)(2,1)}, u32[]{:S(2)}) copy-start(bf16[256,256]{1,0:T(8,128)(2,1)} %refs_7_.2) | copy-start | bytes 393220
  0.7 10.3 %copy-start.6 = (bf16[256,256]{1,0:T(8,128)(2,1)S(1)}, bf16[256,256]{1,0:T(8,128)(2,1)}, u32[]{:S(2)}) copy-start(bf16[256,256]{1,0:T(8,128)(2,1)} %refs_6_.3) | copy-start | bytes 393220
  0.7 10.3 %copy-start.7 = (bf16[256,256]{1,0:T(8,128)(2,1)S(1)}, bf16[256,256]{1,0:T(8,128)(2,1)}, u32[]{:S(2)}) copy-start(bf16[256,256]{1,0:T(8,128)(2,1)} %refs_7_.3) | copy-start | bytes 393220
  2.4 9.6 %copy-start.11 = (bf16[256,128]{1,0:T(8,128)(2,1)S(1)}, bf16[256,128]{1,0:T(8,128)(2,1)}, u32[]{:S(2)}) copy-start(bf16[256,128]{1,0:T(8,128)(2,1)} %refs_8_.1) | copy-start | bytes 196612
  2.5 9.5 %copy-start.12 = (bf16[1,8,32,128]{3,2,1,0:T(8,128)(2,1)S(1)}, bf16[1,8,32,128]{3,2,1,0:T(8,128)(2,1)}, u32[]{:S(2)}) copy-start(bf16[1,8,32,128]{3,2,1,0:T(8,128)(2,1)} %param.16) | copy-start | bytes 196612
  2.5 15.0 %all-to-all-start = ((bf16[8,144,128]{2,1,0:T(8,128)(2,1)}), bf16[8,144,128]{2,1,0:T(8,128)(2,1)S(1)}, u32[]{:S(2)}, u32[]{:S(2)}) async-start(bf16[8,144,128]{2,1,0:T(8,128)(2,1)} %shard_map.161), calls=%async_computation | async-start | bytes 589824 | tf_op jit(solution)/shard_map/all_to_all | solution.py:49
  10.5 1.5 %collective-permute-start = (bf16[512,256]{1,0:T(8,128)(2,1)S(1)}, bf16[512,256]{1,0:T(8,128)(2,1)S(1)}, u32[]{:S(2)}, u32[]{:S(2)}) collective-permute-start(bf16[512,256]{1,0:T(8,128)(2,1)S(1)} %bitcast.13), channel_id=1, source_target_pairs={{0,1},{1,0},{2,3},{3,2},{4,5},{5,4},{6,7},{7,6},{8,9},{9,8},{10,11... | collective-permute-start | bytes 786440 | tf_op jit(solution)/shard_map/ppermute | solution.py:312
  10.5 1.5 %collective-permute-start.1 = (s32[1,512]{1,0:T(1,128)S(1)}, s32[1,512]{1,0:T(1,128)S(1)}, u32[]{:S(2)}, u32[]{:S(2)}) collective-permute-start(s32[1,512]{1,0:T(1,128)S(1)} %copy-done.13), channel_id=1, source_target_pairs={{0,1},{1,0},{2,3},{3,2},{4,5},{5,4},{6,7},{7,6},{8,9},{9,8},{10,11... | collective-permute-start | bytes 6152 | tf_op jit(solution)/shard_map/ppermute | solution.py:313
  12.0 5.5 %copy-start.14 = (s32[512]{0:T(512)S(1)}, s32[512]{0:T(512)}, u32[]{:S(2)}) copy-start(s32[512]{0:T(512)} %param.19) | copy-start | bytes 6148
  17.5 9.2 %copy-start.9 = (bf16[3,3,256,256]{3,2,1,0:T(8,128)(2,1)S(1)}, bf16[3,3,256,256]{3,2,1,0:T(8,128)(2,1)}, u32[]{:S(2)}) copy-start(bf16[3,3,256,256]{3,2,1,0:T(8,128)(2,1)} %param.28) | copy-start | bytes 3538948
  17.5 9.2 %copy-start.10 = (bf16[3,3,256,128]{3,2,1,0:T(8,128)(2,1)S(1)}, bf16[3,3,256,128]{3,2,1,0:T(8,128)(2,1)}, u32[]{:S(2)}) copy-start(bf16[3,3,256,128]{3,2,1,0:T(8,128)(2,1)} %param.29) | copy-start | bytes 1769476
  20.0 11.6 %all-to-all-start.1 = ((bf16[8,64,256]{2,1,0:T(8,128)(2,1)}), bf16[8,64,256]{2,1,0:T(8,128)(2,1)S(1)}, u32[]{:S(2)}, u32[]{:S(2)}) async-start(bf16[8,64,256]{2,1,0:T(8,128)(2,1)} %shard_map.162), calls=%async_computation.1 | async-start | bytes 524288 | tf_op jit(solution)/shard_map/all_to_all | solution.py:49
  25.5 1.3 %collective-permute-start.2 = (bf16[128,256]{1,0:T(8,128)(2,1)S(1)}, bf16[128,256]{1,0:T(8,128)(2,1)S(1)}, u32[]{:S(2)}, u32[]{:S(2)}) collective-permute-start(bf16[128,256]{1,0:T(8,128)(2,1)S(1)} %get-tuple-element.12.refs_0_), channel_id=1, source_target_pairs={{0,1},{1,0},{2,3},{3,2},{4,5},{5,4},{6,7},{7,6},{8,9},{9,8},{10,11... | collective-permute-start | bytes 196616 | tf_op jit(solution)/shard_map/ppermute | solution.py:359
  26.7 4.9 %copy-start.8 = (bf16[256,256]{1,0:T(8,128)(2,1)S(1)}, bf16[256,256]{1,0:T(8,128)(2,1)}, u32[]{:S(2)}) copy-start(bf16[256,256]{1,0:T(8,128)(2,1)} %refs_2_.3) | copy-start | bytes 393220

commit v5 on v4

--- a/solution.py
+++ b/solution.py
@@ -8,7 +8,7 @@
 HEADS = 8
 ITERS = 2
 LANES = 128
-MASK_ROWS = 16
+MASK_ROWS = 8
 HIDDEN = -1e30
 LOG2E = 1.4426950408889634
 
@@ -228,7 +228,7 @@
         copy.wait()
 
 
-def refine_body(state, context, halo, w_gates, w_cand, out, field, wide):
+def refine_body(state, context, halo, w_gates, w_cand, out, field, fresh, wide):
     taps, both, _ = w_gates.shape
     local, hidden = state.shape
     beyond = halo.shape[0]
@@ -241,33 +241,41 @@
     wide[:width, :] = jnp.zeros((width, 3 * both), bf16)
     wide[width + pixels :, :] = jnp.zeros((width, 3 * both), bf16)
 
-    def spread(values, lane):
-        before = jnp.where(col == 0, 0.0, pltpu.roll(values, 1, 0))
-        after = jnp.where(col == width - 1, 0.0, pltpu.roll(values, pixels - 1, 0))
+    def window(k, below=0):
+        start = pl.multiple_of(band * k * width, width) + below * width
+        return pl.ds(pl.multiple_of(start, width), pixels - k * width)
+
+    def spread(values, lane, k):
+        count = values.shape[0]
+        before = jnp.where(col[:count] == 0, 0.0, pltpu.roll(values, 1, 0))
+        after = jnp.where(col[:count] == width - 1, 0.0, pltpu.roll(values, count - 1, 0))
         for c, shifted in enumerate((before, values, after)):
             first = c * both + lane
-            wide[width : width + pixels, first : first + hidden] = shifted.astype(bf16)
-
-    def conv(weight):
-        rows = [wide[r * width : r * width + pixels, :] for r in range(3)]
+            wide[window(k, 1), first : first + hidden] = shifted.astype(bf16)
+
+    def conv(weight, k):
+        rows = [wide[window(k, r), :] for r in range(3)]
         return dot(jnp.concatenate(rows, axis=1), weight[...].reshape(taps * both, -1))
 
-    field[pl.ds(here, local), :] = context[...]
-    field[pl.ds(there, beyond), :] = halo[:, hidden:]
-    spread(field[...].astype(f32), hidden)
-    field[pl.ds(here, local), :] = state[...]
-    field[pl.ds(there, beyond), :] = halo[:, :hidden]
-    now = field[...].astype(f32)
-    for _ in range(ITERS):
-        spread(now, 0)
-        gates = conv(w_gates)
-        update = jax.nn.sigmoid(gates[:, :hidden])
+    field[pl.ds(here, local), :] = context[...].astype(f32)
+    field[pl.ds(there, beyond), :] = halo[:, hidden:].astype(f32)
+    spread(field[...], hidden, 0)
+    field[pl.ds(here, local), :] = state[...].astype(f32)
+    field[pl.ds(there, beyond), :] = halo[:, :hidden].astype(f32)
+    spread(field[...], 0, 0)
+    for k in range(1, 2 * ITERS, 2):
+        gates = conv(w_gates, k)
+        fresh[window(k), :] = jax.nn.sigmoid(gates[:, :hidden])
         reset = jax.nn.sigmoid(gates[:, hidden:])
-        spread((reset * now).astype(bf16).astype(f32), 0)
-        cand = jnp.tanh(conv(w_cand))
-        now = ((1.0 - update) * now + update * cand).astype(bf16).astype(f32)
-    field[...] = now.astype(bf16)
-    out[...] = field[pl.ds(here, local), :]
+        spread((reset * field[window(k), :]).astype(bf16).astype(f32), 0, k)
+        cand = jnp.tanh(conv(w_cand, k + 1))
+        update = fresh[window(k + 1), :]
+        now = (1.0 - update) * field[window(k + 1), :] + update * cand
+        if k + 1 < 2 * ITERS:
+            now = now.astype(bf16).astype(f32)
+            field[window(k + 1), :] = now
+            spread(now, 0, k + 1)
+    out[...] = now.astype(bf16)
 
 
 def output_body(returned, tokens, w_out, out):
@@ -383,7 +391,8 @@
             gru_candidate.reshape(9, 2 * hidden, hidden),
         ),
         scratch=[
-            pltpu.VMEM((local + beyond, hidden), bf16),
+            pltpu.VMEM((local + beyond, hidden), f32),
+            pltpu.VMEM((local + beyond, hidden), f32),
             pltpu.VMEM((local + beyond + 2 * width, 6 * hidden), bf16),
         ],
         flops=2 * (local + beyond) * 9 * 2 * hidden * 3 * hidden * ITERS,

time: 32.9 us -> 32.3 us (0.982)
  Pallas kernels: 14.9 us -> 14.1 us
    pallas_call x6, Pallas kernels: 14.9 us -> 14.1 us  [call(): pl.pallas_call(lambda *refs: body(*refs[len(after):]), out_shape=out, in_...]
  transfers between devices with their start and end apart: 5 -> 5, of which waited for: 3 -> 4; matrix products, arithmetic and copies ran while one was open for 0% -> 0% of each run, Pallas kernels for 30% -> 28%
where the time goes in v5:
time: 32.3 us; the launch traced here: 31.9 us
  Pallas kernels  14.1 us (44%)
  starting transfers between devices  13.9 us (43%)
  waiting for transfers between devices  3.05 us (9%)
  between operations  0.8 us (2%)
    pallas_call x6, Pallas kernels, call(): pl.pallas_call(lambda *refs: body(*refs[len(after):]), out_shape=out, in_...  14.1 us
    all_to_all x2, starting transfers between devices, exchange(): lax.all_to_all(x, 'frame', split_axis=0, concat_axis=0, tiled=True, axis_...  13.4 us
    ppermute x1, waiting for transfers between devices, on_device(): halo = lax.ppermute(edge, 'band', swap)  1.25 us
    all_to_all x2, waiting for transfers between devices, exchange(): lax.all_to_all(x, 'frame', split_axis=0, concat_axis=0, tiled=True, axis_...  1.17 us
  transfers between devices with their start and end apart: 5, of which 4 were waited for; matrix products, arithmetic and copies ran while one was open for 0% of the time, Pallas kernels for 28%

profile of v5, /device:TPU:0, one launch (start us, length us, event | category | flops | bytes accessed | tf_op | source)
XLA Modules:
  0.0 31.9 jit_solution(14821212204000893888)
XLA Ops:
  0.6 0.0 copy-start
  0.6 0.0 copy-start.13
  0.7 0.0 copy-start.1
  0.7 0.0 copy-start.2
  0.7 0.0 copy-start.3
  0.7 0.0 copy-start.4
  0.7 0.0 copy-start.5
  0.7 0.0 copy-start.6
  0.7 0.0 copy-start.7
  0.7 1.7 %shard_map.161 = bf16[8,136,128]{2,1,0:T(8,128)(2,1)} custom-call(bf16[8,64,256]{2,1,0:T(8,128)(2,1)} %bitcast.12, s32[4,128]{1,0:T(4,128)} %bitcast.21), custom_call_target="tpu_custom_call" | custom-call | flops 10000000000 | bytes 264192 | tf_op jit(solution)/shard_map/pallas_call | solution.py:28
  2.5 0.0 copy-start.11
  2.5 0.0 copy-start.12
  2.5 8.0 %all-to-all-start = ((bf16[8,136,128]{2,1,0:T(8,128)(2,1)}), bf16[8,136,128]{2,1,0:T(8,128)(2,1)S(1)}, u32[]{:S(2)}, u32[]{:S(2)}) async-start(bf16[8,136,128]{2,1,0:T(8,128)(2,1)} %shard_map.161), calls=%async_computation | async-start | bytes 557056 | tf_op jit(solution)/shard_map/all_to_all | solution.py:49
  10.5 0.0 copy-done
  10.5 0.0 collective-permute-start
  10.5 0.0 copy-done.13
  10.5 0.5 %collective-permute-start.1 = (s32[1,512]{1,0:T(1,128)S(1)}, s32[1,512]{1,0:T(1,128)S(1)}, u32[]{:S(2)}, u32[]{:S(2)}) collective-permute-start(s32[1,512]{1,0:T(1,128)S(1)} %copy-done.13), channel_id=1, source_target_pairs={{0,1},{1,0},{2,3},{3,2},{4,5},{5,4},{6,7},{7,6},{8,9},{9,8},{10,11... | collective-permute-start | bytes 6152 | tf_op jit(solution)/shard_map/ppermute | solution.py:321
  11.0 0.0 copy-done.2
  11.0 0.0 copy-done.4
  11.0 0.4 %shard_map.158 = (bf16[256,256]{1,0:T(8,128)(2,1)S(1)}, bf16[512,256]{1,0:T(8,128)(2,1)S(1)}, bf16[512,256]{1,0:T(8,128)(2,1)S(1)}, bf16[768,256]{1,0:T(8,128)(2,1)S(1)}) custom-call(bf16[256,256]{1,0:T(8,128)(2,1)S(1)} %bitcast.16, bf16[512,256]{1,0:T(8,128)(2,1)S(1)} %bitcast.14, bf16[256,256]{1,0:T(8,128)(2,1)S(1)} %copy-done.2, ...), custom_call_target="tpu_custom_call" | custom-call | flops 167772160 | bytes 1179648 | tf_op jit(solution)/shard_map/pallas_call | solution.py:28
  11.4 0.6 %collective-permute-done.1.refs_5_ = s32[1,512]{1,0:T(1,128)S(1)} collective-permute-done((s32[1,512]{1,0:T(1,128)S(1)}, s32[1,512]{1,0:T(1,128)S(1)}, u32[]{:S(2)}, u32[]{:S(2)}) %collective-permute-start.1) | collective-permute-done | bytes 2080 | tf_op jit(solution)/shard_map/ppermute | solution.py:321
  12.0 0.0 collective-permute-done.refs_3_
  12.0 0.0 copy-start.14
  12.0 4.5 %shard_map.159 = (bf16[256,128]{1,0:T(8,128)(2,1)S(1)}, bf16[128,256]{1,0:T(8,128)(2,1)S(1)}) custom-call(bf16[256,256]{1,0:T(8,128)(2,1)S(1)} %get-tuple-element.8.refs_0_, bf16[512,256]{1,0:T(8,128)(2,1)S(1)} %get-tuple-element.9.refs_1_, bf16[512,256]{1,0:T(8,128)(2,1)S(1)} %get-tuple-element.10.refs_2_, ...), custom_call_target="tpu_custom_call" | custom-call | flops 2147483648 | bytes 1314816 | tf_op jit(solution)/shard_map/pallas_call | solution.py:28
  16.5 0.7 %all-to-all-done.refs_1_ = bf16[8,136,128]{2,1,0:T(8,128)(2,1)S(1)} async-done(((bf16[8,136,128]{2,1,0:T(8,128)(2,1)}), bf16[8,136,128]{2,1,0:T(8,128)(2,1)S(1)}, u32[]{:S(2)}, u32[]{:S(2)}) %all-to-all-start) | async-done | bytes 278560 | tf_op jit(solution)/shard_map/all_to_all | solution.py:49
  17.3 2.5 %shard_map.162 = bf16[8,64,256]{2,1,0:T(8,128)(2,1)} custom-call(bf16[128,256]{1,0:T(8,128)(2,1)S(1)} %get-tuple-element.12.refs_0_, bf16[8,136,128]{2,1,0:T(8,128)(2,1)S(1)} %all-to-all-done.refs_1_, s32[4,128]{1,0:T(4,128)S(1)} %bitcast.22, bf16[768,256]{1,0:T(8,128)(2,1)S(1)} %get-tuple-element.13.refs_3_), custom_call_target="tpu_custom_call" | custom-call | flops 805306368 | bytes 673792 | tf_op jit(solution)/shard_map/pallas_call | solution.py:28
  19.7 5.4 %all-to-all-start.1 = ((bf16[8,64,256]{2,1,0:T(8,128)(2,1)}), bf16[8,64,256]{2,1,0:T(8,128)(2,1)S(1)}, u32[]{:S(2)}, u32[]{:S(2)}) async-start(bf16[8,64,256]{2,1,0:T(8,128)(2,1)} %shard_map.162), calls=%async_computation.1 | async-start | bytes 524288 | tf_op jit(solution)/shard_map/all_to_all | solution.py:49
  25.1 0.0 collective-permute-start.2
  25.1 1.3 %collective-permute-done.2.refs_2_ = bf16[128,256]{1,0:T(8,128)(2,1)S(1)} collective-permute-done((bf16[128,256]{1,0:T(8,128)(2,1)S(1)}, bf16[128,256]{1,0:T(8,128)(2,1)S(1)}, u32[]{:S(2)}, u32[]{:S(2)}) %collective-permute-start.2) | collective-permute-done | bytes 65568 | tf_op jit(solution)/shard_map/ppermute | solution.py:367
  26.4 4.2 %shard_map.160 = bf16[256,128]{1,0:T(8,128)(2,1)} custom-call(bf16[256,128]{1,0:T(8,128)(2,1)S(1)} %bitcast.20, bf16[256,128]{1,0:T(8,128)(2,1)S(1)} %get-tuple-element.11.refs_1_, bf16[128,256]{1,0:T(8,128)(2,1)S(1)} %collective-permute-done.2.refs_2_, bf16[9,256,256]{2,1,0:T(8,128)(2,1)S(1)} %bitcast.17, bf16[9,256,128]{2,1,0:T(8,128)(2,1)S(1)} %bitcast.18), custom_call_target="tpu_custom_call" | custom-call | flops 1358954496 | bytes 1966080 | tf_op jit(solution)/shard_map/pallas_call | solution.py:28
  30.6 0.5 %all-to-all-done.1 = bf16[8,64,256]{2,1,0:T(8,128)(2,1)S(1)} async-done(((bf16[8,64,256]{2,1,0:T(8,128)(2,1)}), bf16[8,64,256]{2,1,0:T(8,128)(2,1)S(1)}, u32[]{:S(2)}, u32[]{:S(2)}) %all-to-all-start.1) | async-done | bytes 262176 | tf_op jit(solution)/shard_map/all_to_all | solution.py:49
  31.0 0.9 %shard_map.163 = bf16[512,256]{1,0:T(8,128)(2,1)} custom-call(bf16[512,256]{1,0:T(8,128)(2,1)S(1)} %bitcast.11, bf16[512,256]{1,0:T(8,128)(2,1)S(1)} %bitcast.15, bf16[256,256]{1,0:T(8,128)(2,1)S(1)} %copy-done.8), custom_call_target="tpu_custom_call" | custom-call | flops 67108864 | bytes 655360 | tf_op jit(solution)/shard_map/pallas_call | solution.py:28
  (14 shorter events, 0.0 us)
Async XLA Ops:
  0.6 9.8 %copy-start = (bf16[1,512,256]{2,1,0:T(8,128)(2,1)S(1)}, bf16[1,512,256]{2,1,0:T(8,128)(2,1)}, u32[]{:S(2)}) copy-start(bf16[1,512,256]{2,1,0:T(8,128)(2,1)} %param.17) | copy-start | bytes 786436
  0.6 9.8 %copy-start.13 = (s32[1,512]{1,0:T(1,128)S(1)}, s32[1,512]{1,0:T(1,128)}, u32[]{:S(2)}) copy-start(s32[1,512]{1,0:T(1,128)} %refs_4_.3) | copy-start | bytes 6148
  0.7 10.3 %copy-start.1 = (bf16[1,8,32,256]{3,2,1,0:T(8,128)(2,1)S(1)}, bf16[1,8,32,256]{3,2,1,0:T(8,128)(2,1)}, u32[]{:S(2)}) copy-start(bf16[1,8,32,256]{3,2,1,0:T(8,128)(2,1)} %param.15) | copy-start | bytes 393220
  0.7 10.3 %copy-start.2 = (bf16[256,256]{1,0:T(8,128)(2,1)S(1)}, bf16[256,256]{1,0:T(8,128)(2,1)}, u32[]{:S(2)}) copy-start(bf16[256,256]{1,0:T(8,128)(2,1)} %refs_2_.2) | copy-start | bytes 393220
  0.7 10.3 %copy-start.3 = (bf16[256,256]{1,0:T(8,128)(2,1)S(1)}, bf16[256,256]{1,0:T(8,128)(2,1)}, u32[]{:S(2)}) copy-start(bf16[256,256]{1,0:T(8,128)(2,1)} %refs_5_.1) | copy-start | bytes 393220
  0.7 10.3 %copy-start.4 = (bf16[256,256]{1,0:T(8,128)(2,1)S(1)}, bf16[256,256]{1,0:T(8,128)(2,1)}, u32[]{:S(2)}) copy-start(bf16[256,256]{1,0:T(8,128)(2,1)} %refs_6_.2) | copy-start | bytes 393220
  0.7 10.3 %copy-start.5 = (bf16[256,256]{1,0:T(8,128)(2,1)S(1)}, bf16[256,256]{1,0:T(8,128)(2,1)}, u32[]{:S(2)}) copy-start(bf16[256,256]{1,0:T(8,128)(2,1)} %refs_7_.2) | copy-start | bytes 393220
  0.7 10.3 %copy-start.6 = (bf16[256,256]{1,0:T(8,128)(2,1)S(1)}, bf16[256,256]{1,0:T(8,128)(2,1)}, u32[]{:S(2)}) copy-start(bf16[256,256]{1,0:T(8,128)(2,1)} %refs_6_.3) | copy-start | bytes 393220
  0.7 10.3 %copy-start.7 = (bf16[256,256]{1,0:T(8,128)(2,1)S(1)}, bf16[256,256]{1,0:T(8,128)(2,1)}, u32[]{:S(2)}) copy-start(bf16[256,256]{1,0:T(8,128)(2,1)} %refs_7_.3) | copy-start | bytes 393220
  2.5 9.6 %copy-start.11 = (bf16[256,128]{1,0:T(8,128)(2,1)S(1)}, bf16[256,128]{1,0:T(8,128)(2,1)}, u32[]{:S(2)}) copy-start(bf16[256,128]{1,0:T(8,128)(2,1)} %refs_8_.1) | copy-start | bytes 196612
  2.5 9.5 %copy-start.12 = (bf16[1,8,32,128]{3,2,1,0:T(8,128)(2,1)S(1)}, bf16[1,8,32,128]{3,2,1,0:T(8,128)(2,1)}, u32[]{:S(2)}) copy-start(bf16[1,8,32,128]{3,2,1,0:T(8,128)(2,1)} %param.16) | copy-start | bytes 196612
  2.5 14.8 %all-to-all-start = ((bf16[8,136,128]{2,1,0:T(8,128)(2,1)}), bf16[8,136,128]{2,1,0:T(8,128)(2,1)S(1)}, u32[]{:S(2)}, u32[]{:S(2)}) async-start(bf16[8,136,128]{2,1,0:T(8,128)(2,1)} %shard_map.161), calls=%async_computation | async-start | bytes 557056 | tf_op jit(solution)/shard_map/all_to_all | solution.py:49
  10.5 1.5 %collective-permute-start = (bf16[512,256]{1,0:T(8,128)(2,1)S(1)}, bf16[512,256]{1,0:T(8,128)(2,1)S(1)}, u32[]{:S(2)}, u32[]{:S(2)}) collective-permute-start(bf16[512,256]{1,0:T(8,128)(2,1)S(1)} %bitcast.13), channel_id=1, source_target_pairs={{0,1},{1,0},{2,3},{3,2},{4,5},{5,4},{6,7},{7,6},{8,9},{9,8},{10,11... | collective-permute-start | bytes 786440 | tf_op jit(solution)/shard_map/ppermute | solution.py:320
  10.5 1.5 %collective-permute-start.1 = (s32[1,512]{1,0:T(1,128)S(1)}, s32[1,512]{1,0:T(1,128)S(1)}, u32[]{:S(2)}, u32[]{:S(2)}) collective-permute-start(s32[1,512]{1,0:T(1,128)S(1)} %copy-done.13), channel_id=1, source_target_pairs={{0,1},{1,0},{2,3},{3,2},{4,5},{5,4},{6,7},{7,6},{8,9},{9,8},{10,11... | collective-permute-start | bytes 6152 | tf_op jit(solution)/shard_map/ppermute | solution.py:321
  12.0 5.3 %copy-start.14 = (s32[512]{0:T(512)S(1)}, s32[512]{0:T(512)}, u32[]{:S(2)}) copy-start(s32[512]{0:T(512)} %param.19) | copy-start | bytes 6148
  17.3 9.1 %copy-start.9 = (bf16[3,3,256,256]{3,2,1,0:T(8,128)(2,1)S(1)}, bf16[3,3,256,256]{3,2,1,0:T(8,128)(2,1)}, u32[]{:S(2)}) copy-start(bf16[3,3,256,256]{3,2,1,0:T(8,128)(2,1)} %param.28) | copy-start | bytes 3538948
  17.3 9.1 %copy-start.10 = (bf16[3,3,256,128]{3,2,1,0:T(8,128)(2,1)S(1)}, bf16[3,3,256,128]{3,2,1,0:T(8,128)(2,1)}, u32[]{:S(2)}) copy-start(bf16[3,3,256,128]{3,2,1,0:T(8,128)(2,1)} %param.29) | copy-start | bytes 1769476
  19.7 11.3 %all-to-all-start.1 = ((bf16[8,64,256]{2,1,0:T(8,128)(2,1)}), bf16[8,64,256]{2,1,0:T(8,128)(2,1)S(1)}, u32[]{:S(2)}, u32[]{:S(2)}) async-start(bf16[8,64,256]{2,1,0:T(8,128)(2,1)} %shard_map.162), calls=%async_computation.1 | async-start | bytes 524288 | tf_op jit(solution)/shard_map/all_to_all | solution.py:49
  25.1 1.3 %collective-permute-start.2 = (bf16[128,256]{1,0:T(8,128)(2,1)S(1)}, bf16[128,256]{1,0:T(8,128)(2,1)S(1)}, u32[]{:S(2)}, u32[]{:S(2)}) collective-permute-start(bf16[128,256]{1,0:T(8,128)(2,1)S(1)} %get-tuple-element.12.refs_0_), channel_id=1, source_target_pairs={{0,1},{1,0},{2,3},{3,2},{4,5},{5,4},{6,7},{7,6},{8,9},{9,8},{10,11... | collective-permute-start | bytes 196616 | tf_op jit(solution)/shard_map/ppermute | solution.py:367
  26.4 4.6 %copy-start.8 = (bf16[256,256]{1,0:T(8,128)(2,1)S(1)}, bf16[256,256]{1,0:T(8,128)(2,1)}, u32[]{:S(2)}) copy-start(bf16[256,256]{1,0:T(8,128)(2,1)} %refs_2_.3) | copy-start | bytes 393220

commit v6 on v5

--- a/solution.py
+++ b/solution.py
@@ -95,14 +95,35 @@
 
 
 def project_body(
-    pixels, tokens, w_query, w_key, w_value, w_time_query, w_time_key, w_time_value, query, key, value, w_time
+    pixels,
+    tokens,
+    w_query,
+    w_key,
+    w_value,
+    w_time_query,
+    w_time_key,
+    w_time_value,
+    w_time_out,
+    query,
+    key,
+    value,
+    w_time,
+    w_out,
 ):
     query[...] = dot(pixels[...], w_query[...]).astype(bf16)
     key[...] = dot(tokens[...], w_key[...]).astype(bf16)
     value[...] = dot(tokens[...], w_value[...]).astype(bf16)
-    channels = w_time_query.shape[0]
+    channels = w_time_out.shape[0]
+    line = lax.broadcasted_iota(jnp.int32, (channels, channels), 0)
+    column = lax.broadcasted_iota(jnp.int32, (channels, channels), 1)
+    order = line % HEADS * (channels // HEADS) + line // HEADS
+    order = jnp.where(column == order, 1.0, 0.0).astype(bf16)
     for i, weight in enumerate((w_time_query, w_time_key, w_time_value)):
-        w_time[i * channels : (i + 1) * channels, :] = weight[...].astype(f32).T.astype(bf16)
+        moved = lax.dot_general(
+            order, weight[...], (((1,), (1,)), ((), ())), preferred_element_type=f32
+        )
+        w_time[i * channels : (i + 1) * channels, :] = moved.astype(bf16)
+    w_out[...] = dot(order, w_time_out[...]).astype(bf16)
 
 
 def attend_body(
@@ -166,6 +187,22 @@
     def everywhere(x, which):
         return fold(jnp.where(piece == which, x, 0.0))
 
+    def apart(x):
+        if beside == 2:
+            other = pltpu.roll(x, share, 1)
+            return [jnp.where(piece == 0, x, other), jnp.where(piece == 0, other, x)]
+        return [everywhere(x, o) for o in range(beside)]
+
+    def together(parts):
+        if beside == 2:
+            a, b = parts
+            other = pltpu.roll(jnp.where(piece == 0, b, a), share, 1)
+            return jnp.where(piece == 0, a, b) + other
+        x = jnp.zeros_like(parts[0])
+        for o, part in enumerate(parts):
+            x = jnp.where(piece == o, fold(part), x)
+        return x
+
     asked = query_frame[pl.ds(me * share // LANES, 1), :].astype(f32)
     asked = everywhere(asked, me % beside)
     flags = everywhere(packed[:, 2 * share, :].astype(f32), me % beside)
@@ -198,14 +235,15 @@
     anchor = fold(anchor)
 
     copies = []
+    by_head = (head_dim, HEADS, LANES)
     for tile in range(tiles):
-        attended = jnp.zeros((channels, LANES), f32)
-        for o in range(beside):
-            joint = (everywhere(query[tile], o) + anchor).astype(bf16).astype(f32)
+        parts = []
+        for asking in apart(query[tile]):
+            joint = (asking + anchor).astype(bf16).astype(f32)
             scores = []
             for other in range(tiles):
-                product = (key[other] * joint).reshape(HEADS, head_dim, LANES)
-                score = jnp.sum(product, axis=1) * head_dim**-0.5
+                product = (key[other] * joint).reshape(by_head)
+                score = jnp.sum(product, axis=0) * head_dim**-0.5
                 scores.append(jnp.where(seen[other], score, HIDDEN))
             top = scores[0]
             for score in scores[1:]:
@@ -213,15 +251,14 @@
             top = fold(top, jnp.maximum)
             raised = [jnp.exp(score - top) for score in scores]
             total = fold(sum(raised[1:], raised[0]))
-            summed = jnp.zeros((HEADS, head_dim, LANES), f32)
+            summed = None
             for other in range(tiles):
                 weight = (raised[other] / total).astype(bf16).astype(f32)
-                here = value[other].reshape(HEADS, head_dim, LANES)
-                summed = summed + here * weight[:, None, :]
-            summed = fold(summed.reshape(channels, LANES))
-            attended = jnp.where(piece == o, summed, attended)
+                term = value[other].reshape(by_head) * weight[None]
+                summed = term if summed is None else summed + term
+            parts.append(summed.reshape(channels, LANES))
         some = pl.ds(tile * beside, beside)
-        result[some] = attended.T.astype(bf16).reshape(beside, share, channels)
+        result[some] = together(parts).T.astype(bf16).reshape(beside, share, channels)
         copies.append(pltpu.make_async_copy(result.at[some], out.at[some], sems.at[tile]))
         copies[-1].start()
     for copy in copies:
@@ -335,13 +372,14 @@
     )
     arrived = exchange(packed)
 
-    query, key, value, w_time = call(
+    query, key, value, w_time, w_out = call(
         project_body,
         (
             jax.ShapeDtypeStruct((local, channels), bf16),
             jax.ShapeDtypeStruct((half, channels), bf16),
             jax.ShapeDtypeStruct((half, channels), bf16),
             jax.ShapeDtypeStruct((3 * channels, channels), bf16),
+            jax.ShapeDtypeStruct((channels, channels), bf16),
         ),
         (
             pixels.reshape(local, channels),
@@ -352,6 +390,7 @@
             time_query,
             time_key,
             time_value,
+            time_out,
         ),
         flops=2 * (local + 2 * half) * channels * channels,
     )
@@ -400,7 +439,7 @@
     track_out = call(
         output_body,
         jax.ShapeDtypeStruct((half, channels), bf16),
-        (returned.reshape(half, channels), local_tokens, time_out),
+        (returned.reshape(half, channels), local_tokens, w_out),
         flops=2 * half * channels * channels,
     )
     return refined.reshape(gru_state.shape), track_out[None]

time: 32.3 us -> 32 us (level)
  transfers between devices with their start and end apart: 5 -> 5, of which waited for: 4 -> 4; matrix products, arithmetic and copies ran while one was open for 0% -> 0% of each run, Pallas kernels for 28% -> 29%
where the time goes in v6:
time: 32 us; the launch traced here: 31.6 us
  Pallas kernels  13.9 us (43%)
  starting transfers between devices  13.9 us (43%)
  waiting for transfers between devices  2.91 us (9%)
  between operations  0.82 us (3%)
    pallas_call x6, Pallas kernels, call(): pl.pallas_call(lambda *refs: body(*refs[len(after):]), out_shape=out, in_...  13.9 us
    all_to_all x2, starting transfers between devices, exchange(): lax.all_to_all(x, 'frame', split_axis=0, concat_axis=0, tiled=True, axis_...  13.4 us
    ppermute x1, waiting for transfers between devices, on_device(): halo = lax.ppermute(edge, 'band', swap)  1.25 us
    all_to_all x2, waiting for transfers between devices, exchange(): lax.all_to_all(x, 'frame', split_axis=0, concat_axis=0, tiled=True, axis_...  1.17 us
  transfers between devices with their start and end apart: 5, of which 4 were waited for; matrix products, arithmetic and copies ran while one was open for 0% of the time, Pallas kernels for 29%

profile of v6, /device:TPU:0, one launch (start us, length us, event | category | flops | bytes accessed | tf_op | source)
XLA Modules:
  0.0 31.6 jit_solution(12442235003050657683)
XLA Ops:
  0.6 0.0 copy-start
  0.6 0.0 copy-start.13
  0.7 0.0 copy-start.1
  0.7 0.0 copy-start.2
  0.7 0.0 copy-start.3
  0.7 0.0 copy-start.4
  0.7 0.0 copy-start.5
  0.7 0.0 copy-start.6
  0.7 0.0 copy-start.7
  0.7 0.0 copy-start.8
  0.7 1.7 %shard_map.161 = bf16[8,136,128]{2,1,0:T(8,128)(2,1)} custom-call(bf16[8,64,256]{2,1,0:T(8,128)(2,1)} %bitcast.11, s32[4,128]{1,0:T(4,128)} %bitcast.21), custom_call_target="tpu_custom_call" | custom-call | flops 10000000000 | bytes 264192 | tf_op jit(solution)/shard_map/pallas_call | solution.py:28
  2.5 0.0 copy-start.11
  2.5 0.0 copy-start.12
  2.5 8.0 %all-to-all-start = ((bf16[8,136,128]{2,1,0:T(8,128)(2,1)}), bf16[8,136,128]{2,1,0:T(8,128)(2,1)S(1)}, u32[]{:S(2)}, u32[]{:S(2)}) async-start(bf16[8,136,128]{2,1,0:T(8,128)(2,1)} %shard_map.161), calls=%async_computation | async-start | bytes 557056 | tf_op jit(solution)/shard_map/all_to_all | solution.py:49
  10.5 0.0 copy-done
  10.5 0.0 collective-permute-start
  10.5 0.5 %collective-permute-start.1 = (s32[1,512]{1,0:T(1,128)S(1)}, s32[1,512]{1,0:T(1,128)S(1)}, u32[]{:S(2)}, u32[]{:S(2)}) collective-permute-start(s32[1,512]{1,0:T(1,128)S(1)} %copy-done.13), channel_id=1, source_target_pairs={{0,1},{1,0},{2,3},{3,2},{4,5},{5,4},{6,7},{7,6},{8,9},{9,8},{10,11... | collective-permute-start | bytes 6152 | tf_op jit(solution)/shard_map/ppermute | solution.py:358
  11.1 0.5 %shard_map.158 = (bf16[256,256]{1,0:T(8,128)(2,1)S(1)}, bf16[512,256]{1,0:T(8,128)(2,1)S(1)}, bf16[512,256]{1,0:T(8,128)(2,1)S(1)}, bf16[768,256]{1,0:T(8,128)(2,1)S(1)}, bf16[256,256]{1,0:T(8,128)(2,1)S(1)}) custom-call(bf16[256,256]{1,0:T(8,128)(2,1)S(1)} %bitcast.16, bf16[512,256]{1,0:T(8,128)(2,1)S(1)} %bitcast.13, bf16[256,256]{1,0:T(8,128)(2,1)S(1)} %copy-done.2, ...), custom_call_target="tpu_custom_call" | custom-call | flops 167772160 | bytes 1310720 | tf_op jit(solution)/shard_map/pallas_call | solution.py:28
  11.5 0.5 %collective-permute-done.1.refs_5_ = s32[1,512]{1,0:T(1,128)S(1)} collective-permute-done((s32[1,512]{1,0:T(1,128)S(1)}, s32[1,512]{1,0:T(1,128)S(1)}, u32[]{:S(2)}, u32[]{:S(2)}) %collective-permute-start.1) | collective-permute-done | bytes 2080 | tf_op jit(solution)/shard_map/ppermute | solution.py:358
  12.0 0.0 collective-permute-done.refs_3_
  12.0 0.0 copy-done.11
  12.0 0.0 copy-start.14
  12.0 4.5 %shard_map.159 = (bf16[256,128]{1,0:T(8,128)(2,1)S(1)}, bf16[128,256]{1,0:T(8,128)(2,1)S(1)}) custom-call(bf16[256,256]{1,0:T(8,128)(2,1)S(1)} %get-tuple-element.9.refs_0_, bf16[512,256]{1,0:T(8,128)(2,1)S(1)} %get-tuple-element.10.refs_1_, bf16[512,256]{1,0:T(8,128)(2,1)S(1)} %get-tuple-element.11.refs_2_, ...), custom_call_target="tpu_custom_call" | custom-call | flops 2147483648 | bytes 1314816 | tf_op jit(solution)/shard_map/pallas_call | solution.py:28
  16.6 0.7 %all-to-all-done.refs_1_ = bf16[8,136,128]{2,1,0:T(8,128)(2,1)S(1)} async-done(((bf16[8,136,128]{2,1,0:T(8,128)(2,1)}), bf16[8,136,128]{2,1,0:T(8,128)(2,1)S(1)}, u32[]{:S(2)}, u32[]{:S(2)}) %all-to-all-start) | async-done | bytes 278560 | tf_op jit(solution)/shard_map/all_to_all | solution.py:49
  17.3 2.1 %shard_map.162 = bf16[8,64,256]{2,1,0:T(8,128)(2,1)} custom-call(bf16[128,256]{1,0:T(8,128)(2,1)S(1)} %get-tuple-element.13.refs_0_, bf16[8,136,128]{2,1,0:T(8,128)(2,1)S(1)} %all-to-all-done.refs_1_, s32[4,128]{1,0:T(4,128)S(1)} %bitcast.22, bf16[768,256]{1,0:T(8,128)(2,1)S(1)} %get-tuple-element.14.refs_3_), custom_call_target="tpu_custom_call" | custom-call | flops 805306368 | bytes 673792 | tf_op jit(solution)/shard_map/pallas_call | solution.py:28
  19.4 5.4 %all-to-all-start.1 = ((bf16[8,64,256]{2,1,0:T(8,128)(2,1)}), bf16[8,64,256]{2,1,0:T(8,128)(2,1)S(1)}, u32[]{:S(2)}, u32[]{:S(2)}) async-start(bf16[8,64,256]{2,1,0:T(8,128)(2,1)} %shard_map.162), calls=%async_computation.1 | async-start | bytes 524288 | tf_op jit(solution)/shard_map/all_to_all | solution.py:49
  24.8 0.0 collective-permute-start.2
  24.8 1.3 %collective-permute-done.2.refs_2_ = bf16[128,256]{1,0:T(8,128)(2,1)S(1)} collective-permute-done((bf16[128,256]{1,0:T(8,128)(2,1)S(1)}, bf16[128,256]{1,0:T(8,128)(2,1)S(1)}, u32[]{:S(2)}, u32[]{:S(2)}) %collective-permute-start.2) | collective-permute-done | bytes 65568 | tf_op jit(solution)/shard_map/ppermute | solution.py:406
  26.0 0.0 copy-done.10
  26.0 4.2 %shard_map.160 = bf16[256,128]{1,0:T(8,128)(2,1)} custom-call(bf16[256,128]{1,0:T(8,128)(2,1)S(1)} %bitcast.20, bf16[256,128]{1,0:T(8,128)(2,1)S(1)} %get-tuple-element.12.refs_1_, bf16[128,256]{1,0:T(8,128)(2,1)S(1)} %collective-permute-done.2.refs_2_, bf16[9,256,256]{2,1,0:T(8,128)(2,1)S(1)} %bitcast.17, bf16[9,256,128]{2,1,0:T(8,128)(2,1)S(1)} %bitcast.18), custom_call_target="tpu_custom_call" | custom-call | flops 1358954496 | bytes 1966080 | tf_op jit(solution)/shard_map/pallas_call | solution.py:28
  30.2 0.5 %all-to-all-done.1 = bf16[8,64,256]{2,1,0:T(8,128)(2,1)S(1)} async-done(((bf16[8,64,256]{2,1,0:T(8,128)(2,1)}), bf16[8,64,256]{2,1,0:T(8,128)(2,1)S(1)}, u32[]{:S(2)}, u32[]{:S(2)}) %all-to-all-start.1) | async-done | bytes 262176 | tf_op jit(solution)/shard_map/all_to_all | solution.py:49
  30.7 0.9 %shard_map.163 = bf16[512,256]{1,0:T(8,128)(2,1)} custom-call(bf16[512,256]{1,0:T(8,128)(2,1)S(1)} %bitcast.15, bf16[512,256]{1,0:T(8,128)(2,1)S(1)} %bitcast.14, bf16[256,256]{1,0:T(8,128)(2,1)S(1)} %get-tuple-element.15.refs_2_), custom_call_target="tpu_custom_call" | custom-call | flops 67108864 | bytes 655360 | tf_op jit(solution)/shard_map/pallas_call | solution.py:28
  (14 shorter events, 0.0 us)
Async XLA Ops:
  0.6 9.9 %copy-start = (bf16[1,512,256]{2,1,0:T(8,128)(2,1)S(1)}, bf16[1,512,256]{2,1,0:T(8,128)(2,1)}, u32[]{:S(2)}) copy-start(bf16[1,512,256]{2,1,0:T(8,128)(2,1)} %param.17) | copy-start | bytes 786436
  0.6 9.9 %copy-start.13 = (s32[1,512]{1,0:T(1,128)S(1)}, s32[1,512]{1,0:T(1,128)}, u32[]{:S(2)}) copy-start(s32[1,512]{1,0:T(1,128)} %refs_4_.3) | copy-start | bytes 6148
  0.7 10.4 %copy-start.1 = (bf16[1,8,32,256]{3,2,1,0:T(8,128)(2,1)S(1)}, bf16[1,8,32,256]{3,2,1,0:T(8,128)(2,1)}, u32[]{:S(2)}) copy-start(bf16[1,8,32,256]{3,2,1,0:T(8,128)(2,1)} %param.15) | copy-start | bytes 393220
  0.7 10.3 %copy-start.2 = (bf16[256,256]{1,0:T(8,128)(2,1)S(1)}, bf16[256,256]{1,0:T(8,128)(2,1)}, u32[]{:S(2)}) copy-start(bf16[256,256]{1,0:T(8,128)(2,1)} %refs_2_.1) | copy-start | bytes 393220
  0.7 10.3 %copy-start.3 = (bf16[256,256]{1,0:T(8,128)(2,1)S(1)}, bf16[256,256]{1,0:T(8,128)(2,1)}, u32[]{:S(2)}) copy-start(bf16[256,256]{1,0:T(8,128)(2,1)} %refs_5_.1) | copy-start | bytes 393220
  0.7 10.3 %copy-start.4 = (bf16[256,256]{1,0:T(8,128)(2,1)S(1)}, bf16[256,256]{1,0:T(8,128)(2,1)}, u32[]{:S(2)}) copy-start(bf16[256,256]{1,0:T(8,128)(2,1)} %refs_6_.2) | copy-start | bytes 393220
  0.7 10.3 %copy-start.5 = (bf16[256,256]{1,0:T(8,128)(2,1)S(1)}, bf16[256,256]{1,0:T(8,128)(2,1)}, u32[]{:S(2)}) copy-start(bf16[256,256]{1,0:T(8,128)(2,1)} %refs_7_.2) | copy-start | bytes 393220
  0.7 10.3 %copy-start.6 = (bf16[256,256]{1,0:T(8,128)(2,1)S(1)}, bf16[256,256]{1,0:T(8,128)(2,1)}, u32[]{:S(2)}) copy-start(bf16[256,256]{1,0:T(8,128)(2,1)} %refs_8_.2) | copy-start | bytes 393220
  0.7 10.3 %copy-start.7 = (bf16[256,256]{1,0:T(8,128)(2,1)S(1)}, bf16[256,256]{1,0:T(8,128)(2,1)}, u32[]{:S(2)}) copy-start(bf16[256,256]{1,0:T(8,128)(2,1)} %refs_6_.3) | copy-start | bytes 393220
  0.7 10.3 %copy-start.8 = (bf16[256,256]{1,0:T(8,128)(2,1)S(1)}, bf16[256,256]{1,0:T(8,128)(2,1)}, u32[]{:S(2)}) copy-start(bf16[256,256]{1,0:T(8,128)(2,1)} %refs_7_.3) | copy-start | bytes 393220
  2.5 9.6 %copy-start.11 = (bf16[256,128]{1,0:T(8,128)(2,1)S(1)}, bf16[256,128]{1,0:T(8,128)(2,1)}, u32[]{:S(2)}) copy-start(bf16[256,128]{1,0:T(8,128)(2,1)} %refs_8_.3) | copy-start | bytes 196612
  2.5 9.5 %copy-start.12 = (bf16[1,8,32,128]{3,2,1,0:T(8,128)(2,1)S(1)}, bf16[1,8,32,128]{3,2,1,0:T(8,128)(2,1)}, u32[]{:S(2)}) copy-start(bf16[1,8,32,128]{3,2,1,0:T(8,128)(2,1)} %param.16) | copy-start | bytes 196612
  2.5 14.8 %all-to-all-start = ((bf16[8,136,128]{2,1,0:T(8,128)(2,1)}), bf16[8,136,128]{2,1,0:T(8,128)(2,1)S(1)}, u32[]{:S(2)}, u32[]{:S(2)}) async-start(bf16[8,136,128]{2,1,0:T(8,128)(2,1)} %shard_map.161), calls=%async_computation | async-start | bytes 557056 | tf_op jit(solution)/shard_map/all_to_all | solution.py:49
  10.5 1.5 %collective-permute-start = (bf16[512,256]{1,0:T(8,128)(2,1)S(1)}, bf16[512,256]{1,0:T(8,128)(2,1)S(1)}, u32[]{:S(2)}, u32[]{:S(2)}) collective-permute-start(bf16[512,256]{1,0:T(8,128)(2,1)S(1)} %bitcast.12), channel_id=1, source_target_pairs={{0,1},{1,0},{2,3},{3,2},{4,5},{5,4},{6,7},{7,6},{8,9},{9,8},{10,11... | collective-permute-start | bytes 786440 | tf_op jit(solution)/shard_map/ppermute | solution.py:357
  10.5 1.5 %collective-permute-start.1 = (s32[1,512]{1,0:T(1,128)S(1)}, s32[1,512]{1,0:T(1,128)S(1)}, u32[]{:S(2)}, u32[]{:S(2)}) collective-permute-start(s32[1,512]{1,0:T(1,128)S(1)} %copy-done.13), channel_id=1, source_target_pairs={{0,1},{1,0},{2,3},{3,2},{4,5},{5,4},{6,7},{7,6},{8,9},{9,8},{10,11... | collective-permute-start | bytes 6152 | tf_op jit(solution)/shard_map/ppermute | solution.py:358
  12.0 5.3 %copy-start.14 = (s32[512]{0:T(512)S(1)}, s32[512]{0:T(512)}, u32[]{:S(2)}) copy-start(s32[512]{0:T(512)} %param.19) | copy-start | bytes 6148
  17.3 8.7 %copy-start.9 = (bf16[3,3,256,256]{3,2,1,0:T(8,128)(2,1)S(1)}, bf16[3,3,256,256]{3,2,1,0:T(8,128)(2,1)}, u32[]{:S(2)}) copy-start(bf16[3,3,256,256]{3,2,1,0:T(8,128)(2,1)} %param.28) | copy-start | bytes 3538948
  17.3 8.7 %copy-start.10 = (bf16[3,3,256,128]{3,2,1,0:T(8,128)(2,1)S(1)}, bf16[3,3,256,128]{3,2,1,0:T(8,128)(2,1)}, u32[]{:S(2)}) copy-start(bf16[3,3,256,128]{3,2,1,0:T(8,128)(2,1)} %param.29) | copy-start | bytes 1769476
  19.4 11.3 %all-to-all-start.1 = ((bf16[8,64,256]{2,1,0:T(8,128)(2,1)}), bf16[8,64,256]{2,1,0:T(8,128)(2,1)S(1)}, u32[]{:S(2)}, u32[]{:S(2)}) async-start(bf16[8,64,256]{2,1,0:T(8,128)(2,1)} %shard_map.162), calls=%async_computation.1 | async-start | bytes 524288 | tf_op jit(solution)/shard_map/all_to_all | solution.py:49
  24.8 1.3 %collective-permute-start.2 = (bf16[128,256]{1,0:T(8,128)(2,1)S(1)}, bf16[128,256]{1,0:T(8,128)(2,1)S(1)}, u32[]{:S(2)}, u32[]{:S(2)}) collective-permute-start(bf16[128,256]{1,0:T(8,128)(2,1)S(1)} %get-tuple-element.13.refs_0_), channel_id=1, source_target_pairs={{0,1},{1,0},{2,3},{3,2},{4,5},{5,4},{6,7},{7,6},{8,9},{9,8},{10,11... | collective-permute-start | bytes 196616 | tf_op jit(solution)/shard_map/ppermute | solution.py:406

commit v7 on v6

--- a/solution.py
+++ b/solution.py
@@ -69,7 +69,7 @@
         coming.append(
             [
                 pltpu.make_async_copy(
-                    tokens.at[pl.ds(turned(i * step, frames), step), :, pl.ds(c * LANES, LANES)],
+                    tokens.at[some, :, pl.ds(c * LANES, LANES)],
                     packed.at[some, pl.ds(c * share, share), :],
                     sems.at[1 + 2 * i + c],
                 )
@@ -81,7 +81,7 @@
             copy.start()
     first.wait()
     for g in range(frames):
-        group = flags[turned(g, frames) * share // LANES, :].astype(f32)
+        group = flags[g * share // LANES, :].astype(f32)
         packed[g, 2 * share :, :] = jnp.broadcast_to(group[None], (MASK_ROWS, LANES)).astype(bf16)
     going = []
     for i, copies in enumerate(coming):
@@ -169,12 +169,12 @@
     edge[:, LANES:] = context[pl.ds(start, count), :]
 
 
-def temporal_body(packed, query_frame, w_all, out, result, sems):
+def temporal_body(packed, query_frame, w_all, w_out, out, result, sems):
     frames, share, channels = out.shape
     head_dim = channels // HEADS
     tiles = frames * share // LANES
     beside = LANES // share
-    me = lax.axis_index("frame")
+    mine = (lax.axis_index("frame") + frames - turned(0, frames)) % frames
     piece = lax.broadcasted_iota(jnp.int32, (1, LANES), 1) // share
 
     def fold(x, add=jnp.add):
@@ -203,9 +203,9 @@
             x = jnp.where(piece == o, fold(part), x)
         return x
 
-    asked = query_frame[pl.ds(me * share // LANES, 1), :].astype(f32)
-    asked = everywhere(asked, me % beside)
-    flags = everywhere(packed[:, 2 * share, :].astype(f32), me % beside)
+    asked = query_frame[pl.ds(mine * share // LANES, 1), :].astype(f32)
+    asked = everywhere(asked, mine % beside)
+    flags = everywhere(packed[:, 2 * share, :].astype(f32), mine % beside)
     seen = []
     for tile in range(tiles):
         row = jnp.zeros((1, LANES), f32)
@@ -258,7 +258,9 @@
                 summed = term if summed is None else summed + term
             parts.append(summed.reshape(channels, LANES))
         some = pl.ds(tile * beside, beside)
-        result[some] = together(parts).T.astype(bf16).reshape(beside, share, channels)
+        added = dot(together(parts).T.astype(bf16), w_out[...])
+        total = rows[tile * LANES : (tile + 1) * LANES, :].astype(f32) + added
+        result[some] = total.astype(bf16).reshape(beside, share, channels)
         copies.append(pltpu.make_async_copy(result.at[some], out.at[some], sems.at[tile]))
         copies[-1].start()
     for copy in copies:
@@ -313,14 +315,6 @@
             field[window(k + 1), :] = now
             spread(now, 0, k + 1)
     out[...] = now.astype(bf16)
-
-
-def output_body(returned, tokens, w_out, out):
-    rows = returned.shape[0] // 2
-    for i in range(2):
-        mine = slice(turned(i, 2) * rows, (turned(i, 2) + 1) * rows)
-        added = dot(returned[i * rows : (i + 1) * rows, :], w_out[...])
-        out[mine, :] = (tokens[mine, :].astype(f32) + added).astype(bf16)
 
 
 def on_device(
@@ -405,10 +399,10 @@
     )
     halo = lax.ppermute(edge, "band", swap)
 
-    attended = call(
+    tracked = call(
         temporal_body,
         jax.ShapeDtypeStruct((frames, share, channels), bf16),
-        (arrived, query_frame.reshape(groups, LANES), w_time),
+        (arrived, query_frame.reshape(groups, LANES), w_time, w_out),
         after=(edge,),
         scratch=[
             pltpu.VMEM((frames, share, channels), bf16),
@@ -417,7 +411,7 @@
         place=HBM,
         flops=6 * half * channels * channels * 4,
     )
-    returned = exchange(attended)
+    track_out = exchange(tracked)
 
     refined = call(
         refine_body,
@@ -436,13 +430,7 @@
         ],
         flops=2 * (local + beyond) * 9 * 2 * hidden * 3 * hidden * ITERS,
     )
-    track_out = call(
-        output_body,
-        jax.ShapeDtypeStruct((half, channels), bf16),
-        (returned.reshape(half, channels), local_tokens, w_out),
-        flops=2 * half * channels * channels,
-    )
-    return refined.reshape(gru_state.shape), track_out[None]
+    return refined.reshape(gru_state.shape), track_out.reshape(tokens.shape)
 
 
 def solution(mesh):

time: 32 us -> 31.8 us (level)
  Pallas kernels: 13.9 us -> 13 us
  local copies, waits for them, and re-layouts: 0.07 us -> 0.77 us
    pallas_call x6 -> x5, Pallas kernels: 13.9 us -> 13 us  [call(): pl.pallas_call(lambda *refs: body(*refs[len(after):]), out_shape=out, in_...]
    unnamed x30 -> x31, local copies, waits for them, and re-layouts: 0.07 us -> 0.77 us
where the time goes in v7:
time: 31.8 us; the launch traced here: 31.4 us
  starting transfers between devices  13.9 us (44%)
  Pallas kernels  13 us (41%)
  waiting for transfers between devices  2.9 us (9%)
  between operations  0.82 us (3%)
  local copies, waits for them, and re-layouts  0.77 us (2%)
    all_to_all x2, starting transfers between devices, exchange(): lax.all_to_all(x, 'frame', split_axis=0, concat_axis=0, tiled=True, axis_...  13.4 us
    pallas_call x5, Pallas kernels, call(): pl.pallas_call(lambda *refs: body(*refs[len(after):]), out_shape=out, in_...  13 us
    ppermute x1, waiting for transfers between devices, on_device(): halo = lax.ppermute(edge, 'band', swap)  1.25 us
    all_to_all x2, waiting for transfers between devices, exchange(): lax.all_to_all(x, 'frame', split_axis=0, concat_axis=0, tiled=True, axis_...  1.17 us
    unnamed x31, local copies, waits for them, and re-layouts  0.77 us
  transfers between devices with their start and end apart: 5, of which 4 were waited for; matrix products, arithmetic and copies ran while one was open for 0% of the time, Pallas kernels for 29%

profile of v7, /device:TPU:0, one launch (start us, length us, event | category | flops | bytes accessed | tf_op | source)
XLA Modules:
  0.0 31.4 jit_solution(11166736715455915470)
XLA Ops:
  0.6 0.0 copy-start
  0.6 0.0 copy-start.13
  0.7 0.0 copy-start.1
  0.7 0.0 copy-start.2
  0.7 0.0 copy-start.3
  0.7 0.0 copy-start.4
  0.7 0.0 copy-start.5
  0.7 0.0 copy-start.6
  0.7 0.0 copy-start.7
  0.7 0.0 copy-start.8
  0.7 1.7 %shard_map.161 = bf16[8,136,128]{2,1,0:T(8,128)(2,1)} custom-call(bf16[8,64,256]{2,1,0:T(8,128)(2,1)} %bitcast.10, s32[4,128]{1,0:T(4,128)} %bitcast.18), custom_call_target="tpu_custom_call" | custom-call | flops 10000000000 | bytes 264192 | tf_op jit(solution)/shard_map/pallas_call | solution.py:28
  2.5 0.0 copy-start.11
  2.5 0.0 copy-start.12
  2.5 8.0 %all-to-all-start = ((bf16[8,136,128]{2,1,0:T(8,128)(2,1)}), bf16[8,136,128]{2,1,0:T(8,128)(2,1)S(1)}, u32[]{:S(2)}, u32[]{:S(2)}) async-start(bf16[8,136,128]{2,1,0:T(8,128)(2,1)} %shard_map.161), calls=%async_computation | async-start | bytes 557056 | tf_op jit(solution)/shard_map/all_to_all | solution.py:49
  10.5 0.0 copy-done
  10.5 0.0 collective-permute-start
  10.5 0.5 %collective-permute-start.1 = (s32[1,512]{1,0:T(1,128)S(1)}, s32[1,512]{1,0:T(1,128)S(1)}, u32[]{:S(2)}, u32[]{:S(2)}) collective-permute-start(s32[1,512]{1,0:T(1,128)S(1)} %copy-done.13), channel_id=1, source_target_pairs={{0,1},{1,0},{2,3},{3,2},{4,5},{5,4},{6,7},{7,6},{8,9},{9,8},{10,11... | collective-permute-start | bytes 6152 | tf_op jit(solution)/shard_map/ppermute | solution.py:352
  11.0 0.0 copy-done.2
  11.1 0.5 %shard_map.158 = (bf16[256,256]{1,0:T(8,128)(2,1)S(1)}, bf16[512,256]{1,0:T(8,128)(2,1)S(1)}, bf16[512,256]{1,0:T(8,128)(2,1)S(1)}, bf16[768,256]{1,0:T(8,128)(2,1)S(1)}, bf16[256,256]{1,0:T(8,128)(2,1)S(1)}) custom-call(bf16[256,256]{1,0:T(8,128)(2,1)S(1)} %bitcast.13, bf16[512,256]{1,0:T(8,128)(2,1)S(1)} %bitcast.12, bf16[256,256]{1,0:T(8,128)(2,1)S(1)} %copy-done.2, ...), custom_call_target="tpu_custom_call" | custom-call | flops 167772160 | bytes 1310720 | tf_op jit(solution)/shard_map/pallas_call | solution.py:28
  11.5 0.5 %collective-permute-done.1.refs_5_ = s32[1,512]{1,0:T(1,128)S(1)} collective-permute-done((s32[1,512]{1,0:T(1,128)S(1)}, s32[1,512]{1,0:T(1,128)S(1)}, u32[]{:S(2)}, u32[]{:S(2)}) %collective-permute-start.1) | collective-permute-done | bytes 2080 | tf_op jit(solution)/shard_map/ppermute | solution.py:352
  12.0 0.0 collective-permute-done.refs_3_
  12.0 0.0 copy-done.11
  12.0 0.0 copy-start.14
  12.0 4.5 %shard_map.159 = (bf16[256,128]{1,0:T(8,128)(2,1)S(1)}, bf16[128,256]{1,0:T(8,128)(2,1)S(1)}) custom-call(bf16[256,256]{1,0:T(8,128)(2,1)S(1)} %get-tuple-element.9.refs_0_, bf16[512,256]{1,0:T(8,128)(2,1)S(1)} %get-tuple-element.10.refs_1_, bf16[512,256]{1,0:T(8,128)(2,1)S(1)} %get-tuple-element.11.refs_2_, ...), custom_call_target="tpu_custom_call" | custom-call | flops 2147483648 | bytes 1314816 | tf_op jit(solution)/shard_map/pallas_call | solution.py:28
  16.6 0.7 %all-to-all-done.refs_1_ = bf16[8,136,128]{2,1,0:T(8,128)(2,1)S(1)} async-done(((bf16[8,136,128]{2,1,0:T(8,128)(2,1)}), bf16[8,136,128]{2,1,0:T(8,128)(2,1)S(1)}, u32[]{:S(2)}, u32[]{:S(2)}) %all-to-all-start) | async-done | bytes 278560 | tf_op jit(solution)/shard_map/all_to_all | solution.py:49
  17.3 2.1 %shard_map.162 = bf16[8,64,256]{2,1,0:T(8,128)(2,1)} custom-call(bf16[128,256]{1,0:T(8,128)(2,1)S(1)} %get-tuple-element.13.refs_0_, bf16[8,136,128]{2,1,0:T(8,128)(2,1)S(1)} %all-to-all-done.refs_1_, s32[4,128]{1,0:T(4,128)S(1)} %bitcast.19, bf16[768,256]{1,0:T(8,128)(2,1)S(1)} %get-tuple-element.14.refs_3_, bf16[256,256]{1,0:T(8,128)(2,1)S(1)} %get-tuple-element.15.refs_4_), custom_call_target="tpu_custom_call" | custom-call | flops 805306368 | bytes 804864 | tf_op jit(solution)/shard_map/pallas_call | solution.py:28
  19.4 5.4 %all-to-all-start.1 = ((bf16[8,64,256]{2,1,0:T(8,128)(2,1)}), bf16[8,64,256]{2,1,0:T(8,128)(2,1)S(1)}, u32[]{:S(2)}, u32[]{:S(2)}) async-start(bf16[8,64,256]{2,1,0:T(8,128)(2,1)} %shard_map.162), calls=%async_computation.1 | async-start | bytes 524288 | tf_op jit(solution)/shard_map/all_to_all | solution.py:49
  24.8 0.0 collective-permute-start.2
  24.8 1.3 %collective-permute-done.2.refs_2_ = bf16[128,256]{1,0:T(8,128)(2,1)S(1)} collective-permute-done((bf16[128,256]{1,0:T(8,128)(2,1)S(1)}, bf16[128,256]{1,0:T(8,128)(2,1)S(1)}, u32[]{:S(2)}, u32[]{:S(2)}) %collective-permute-start.2) | collective-permute-done | bytes 65568 | tf_op jit(solution)/shard_map/ppermute | solution.py:400
  26.1 4.2 %shard_map.160 = bf16[256,128]{1,0:T(8,128)(2,1)} custom-call(bf16[256,128]{1,0:T(8,128)(2,1)S(1)} %bitcast.17, bf16[256,128]{1,0:T(8,128)(2,1)S(1)} %get-tuple-element.12.refs_1_, bf16[128,256]{1,0:T(8,128)(2,1)S(1)} %collective-permute-done.2.refs_2_, bf16[9,256,256]{2,1,0:T(8,128)(2,1)S(1)} %bitcast.14, bf16[9,256,128]{2,1,0:T(8,128)(2,1)S(1)} %bitcast.15), custom_call_target="tpu_custom_call" | custom-call | flops 1358954496 | bytes 1966080 | tf_op jit(solution)/shard_map/pallas_call | solution.py:28
  30.3 0.5 %all-to-all-done.1 = bf16[8,64,256]{2,1,0:T(8,128)(2,1)S(1)} async-done(((bf16[8,64,256]{2,1,0:T(8,128)(2,1)}), bf16[8,64,256]{2,1,0:T(8,128)(2,1)S(1)}, u32[]{:S(2)}, u32[]{:S(2)}) %all-to-all-start.1) | async-done | bytes 262176 | tf_op jit(solution)/shard_map/all_to_all | solution.py:49
  30.7 0.7 %copy.18 = bf16[1,512,256]{2,1,0:T(8,128)(2,1)} copy(bf16[1,512,256]{2,1,0:T(8,128)(2,1)S(1)} %bitcast.20) | data formatting | bytes 524288
  (14 shorter events, 0.0 us)
Async XLA Ops:
  0.6 9.9 %copy-start = (bf16[1,512,256]{2,1,0:T(8,128)(2,1)S(1)}, bf16[1,512,256]{2,1,0:T(8,128)(2,1)}, u32[]{:S(2)}) copy-start(bf16[1,512,256]{2,1,0:T(8,128)(2,1)} %param.17) | copy-start | bytes 786436
  0.6 9.9 %copy-start.13 = (s32[1,512]{1,0:T(1,128)S(1)}, s32[1,512]{1,0:T(1,128)}, u32[]{:S(2)}) copy-start(s32[1,512]{1,0:T(1,128)} %refs_4_.3) | copy-start | bytes 6148
  0.7 10.4 %copy-start.1 = (bf16[1,8,32,256]{3,2,1,0:T(8,128)(2,1)S(1)}, bf16[1,8,32,256]{3,2,1,0:T(8,128)(2,1)}, u32[]{:S(2)}) copy-start(bf16[1,8,32,256]{3,2,1,0:T(8,128)(2,1)} %param.15) | copy-start | bytes 393220
  0.7 10.3 %copy-start.2 = (bf16[256,256]{1,0:T(8,128)(2,1)S(1)}, bf16[256,256]{1,0:T(8,128)(2,1)}, u32[]{:S(2)}) copy-start(bf16[256,256]{1,0:T(8,128)(2,1)} %refs_2_.1) | copy-start | bytes 393220
  0.7 10.3 %copy-start.3 = (bf16[256,256]{1,0:T(8,128)(2,1)S(1)}, bf16[256,256]{1,0:T(8,128)(2,1)}, u32[]{:S(2)}) copy-start(bf16[256,256]{1,0:T(8,128)(2,1)} %refs_5_.1) | copy-start | bytes 393220
  0.7 10.3 %copy-start.4 = (bf16[256,256]{1,0:T(8,128)(2,1)S(1)}, bf16[256,256]{1,0:T(8,128)(2,1)}, u32[]{:S(2)}) copy-start(bf16[256,256]{1,0:T(8,128)(2,1)} %refs_6_.2) | copy-start | bytes 393220
  0.7 10.3 %copy-start.5 = (bf16[256,256]{1,0:T(8,128)(2,1)S(1)}, bf16[256,256]{1,0:T(8,128)(2,1)}, u32[]{:S(2)}) copy-start(bf16[256,256]{1,0:T(8,128)(2,1)} %refs_7_.2) | copy-start | bytes 393220
  0.7 10.3 %copy-start.6 = (bf16[256,256]{1,0:T(8,128)(2,1)S(1)}, bf16[256,256]{1,0:T(8,128)(2,1)}, u32[]{:S(2)}) copy-start(bf16[256,256]{1,0:T(8,128)(2,1)} %refs_8_.2) | copy-start | bytes 393220
  0.7 10.3 %copy-start.7 = (bf16[256,256]{1,0:T(8,128)(2,1)S(1)}, bf16[256,256]{1,0:T(8,128)(2,1)}, u32[]{:S(2)}) copy-start(bf16[256,256]{1,0:T(8,128)(2,1)} %refs_6_.3) | copy-start | bytes 393220
  0.7 10.3 %copy-start.8 = (bf16[256,256]{1,0:T(8,128)(2,1)S(1)}, bf16[256,256]{1,0:T(8,128)(2,1)}, u32[]{:S(2)}) copy-start(bf16[256,256]{1,0:T(8,128)(2,1)} %refs_7_.3) | copy-start | bytes 393220
  2.5 9.6 %copy-start.11 = (bf16[256,128]{1,0:T(8,128)(2,1)S(1)}, bf16[256,128]{1,0:T(8,128)(2,1)}, u32[]{:S(2)}) copy-start(bf16[256,128]{1,0:T(8,128)(2,1)} %refs_8_.3) | copy-start | bytes 196612
  2.5 9.5 %copy-start.12 = (bf16[1,8,32,128]{3,2,1,0:T(8,128)(2,1)S(1)}, bf16[1,8,32,128]{3,2,1,0:T(8,128)(2,1)}, u32[]{:S(2)}) copy-start(bf16[1,8,32,128]{3,2,1,0:T(8,128)(2,1)} %param.16) | copy-start | bytes 196612
  2.5 14.8 %all-to-all-start = ((bf16[8,136,128]{2,1,0:T(8,128)(2,1)}), bf16[8,136,128]{2,1,0:T(8,128)(2,1)S(1)}, u32[]{:S(2)}, u32[]{:S(2)}) async-start(bf16[8,136,128]{2,1,0:T(8,128)(2,1)} %shard_map.161), calls=%async_computation | async-start | bytes 557056 | tf_op jit(solution)/shard_map/all_to_all | solution.py:49
  10.5 1.5 %collective-permute-start = (bf16[512,256]{1,0:T(8,128)(2,1)S(1)}, bf16[512,256]{1,0:T(8,128)(2,1)S(1)}, u32[]{:S(2)}, u32[]{:S(2)}) collective-permute-start(bf16[512,256]{1,0:T(8,128)(2,1)S(1)} %bitcast.11), channel_id=1, source_target_pairs={{0,1},{1,0},{2,3},{3,2},{4,5},{5,4},{6,7},{7,6},{8,9},{9,8},{10,11... | collective-permute-start | bytes 786440 | tf_op jit(solution)/shard_map/ppermute | solution.py:351
  10.5 1.5 %collective-permute-start.1 = (s32[1,512]{1,0:T(1,128)S(1)}, s32[1,512]{1,0:T(1,128)S(1)}, u32[]{:S(2)}, u32[]{:S(2)}) collective-permute-start(s32[1,512]{1,0:T(1,128)S(1)} %copy-done.13), channel_id=1, source_target_pairs={{0,1},{1,0},{2,3},{3,2},{4,5},{5,4},{6,7},{7,6},{8,9},{9,8},{10,11... | collective-permute-start | bytes 6152 | tf_op jit(solution)/shard_map/ppermute | solution.py:352
  12.0 5.3 %copy-start.14 = (s32[512]{0:T(512)S(1)}, s32[512]{0:T(512)}, u32[]{:S(2)}) copy-start(s32[512]{0:T(512)} %param.19) | copy-start | bytes 6148
  17.3 8.8 %copy-start.9 = (bf16[3,3,256,256]{3,2,1,0:T(8,128)(2,1)S(1)}, bf16[3,3,256,256]{3,2,1,0:T(8,128)(2,1)}, u32[]{:S(2)}) copy-start(bf16[3,3,256,256]{3,2,1,0:T(8,128)(2,1)} %param.28) | copy-start | bytes 3538948
  17.3 8.8 %copy-start.10 = (bf16[3,3,256,128]{3,2,1,0:T(8,128)(2,1)S(1)}, bf16[3,3,256,128]{3,2,1,0:T(8,128)(2,1)}, u32[]{:S(2)}) copy-start(bf16[3,3,256,128]{3,2,1,0:T(8,128)(2,1)} %param.29) | copy-start | bytes 1769476
  19.4 11.3 %all-to-all-start.1 = ((bf16[8,64,256]{2,1,0:T(8,128)(2,1)}), bf16[8,64,256]{2,1,0:T(8,128)(2,1)S(1)}, u32[]{:S(2)}, u32[]{:S(2)}) async-start(bf16[8,64,256]{2,1,0:T(8,128)(2,1)} %shard_map.162), calls=%async_computation.1 | async-start | bytes 524288 | tf_op jit(solution)/shard_map/all_to_all | solution.py:49
  24.8 1.3 %collective-permute-start.2 = (bf16[128,256]{1,0:T(8,128)(2,1)S(1)}, bf16[128,256]{1,0:T(8,128)(2,1)S(1)}, u32[]{:S(2)}, u32[]{:S(2)}) collective-permute-start(bf16[128,256]{1,0:T(8,128)(2,1)S(1)} %get-tuple-element.13.refs_0_), channel_id=1, source_target_pairs={{0,1},{1,0},{2,3},{3,2},{4,5},{5,4},{6,7},{7,6},{8,9},{9,8},{10,11... | collective-permute-start | bytes 196616 | tf_op jit(solution)/shard_map/ppermute | solution.py:400

commit v8 on v7

--- a/solution.py
+++ b/solution.py
@@ -10,6 +10,7 @@
 LANES = 128
 MASK_ROWS = 8
 HIDDEN = -1e30
+ORDERS = ((4, 3, 7, 6, 2, 0, 5, 1),)
 LOG2E = 1.4426950408889634
 
 f32 = jnp.float32
@@ -40,8 +41,11 @@
     )(*after, *args)
 
 
-def turned(slot, frames):
-    return (slot + frames // 2) % frames
+def group_order(frames):
+    for order in ORDERS:
+        if len(order) == frames:
+            return list(order)
+    return [(slot + frames // 2) % frames for slot in range(frames)]
 
 
 def exchange(x):
@@ -52,7 +56,7 @@
         split_axis=0,
         concat_axis=0,
         tiled=True,
-        axis_index_groups=[[turned(i, frames) for i in range(frames)]],
+        axis_index_groups=[group_order(frames)],
     )
 
 
@@ -174,7 +178,11 @@
     head_dim = channels // HEADS
     tiles = frames * share // LANES
     beside = LANES // share
-    mine = (lax.axis_index("frame") + frames - turned(0, frames)) % frames
+    order = group_order(frames)
+    me = lax.axis_index("frame")
+    mine = 0
+    for j in range(1, frames):
+        mine = jnp.where(me == order[j], j, mine)
     piece = lax.broadcasted_iota(jnp.int32, (1, LANES), 1) // share
 
     def fold(x, add=jnp.add):
@@ -230,7 +238,9 @@
     )
     anchor = jnp.zeros((channels, LANES), f32)
     for tile in range(tiles):
-        frame = turned(piece + tile * beside, frames).astype(f32)
+        frame = jnp.zeros((1, LANES), f32)
+        for o in range(beside):
+            frame = jnp.where(piece == o, float(order[tile * beside + o]), frame)
         anchor = anchor + jnp.where(asked == frame, query[tile], 0.0)
     anchor = fold(anchor)
 

time: 31.8 us -> 31.1 us (0.978)
  waiting for transfers between devices: 2.9 us -> 1.74 us
  starting transfers between devices: 13.9 us -> 14.4 us
    all_to_all x2, waiting for transfers between devices: 1.17 us -> 0.01 us  [exchange(): lax.all_to_all(x, 'frame', split_axis=0, concat_axis=0, tiled=True, axis_...]
    all_to_all x2, starting transfers between devices: 13.4 us -> 13.8 us  [exchange(): lax.all_to_all(x, 'frame', split_axis=0, concat_axis=0, tiled=True, axis_...]
  transfers between devices with their start and end apart: 5 -> 5, of which waited for: 4 -> 2; matrix products, arithmetic and copies ran while one was open for 0% -> 0% of each run, Pallas kernels for 29% -> 30%
where the time goes in v8:
time: 31.1 us; the launch traced here: 30.8 us
  starting transfers between devices  14.4 us (46%)
  Pallas kernels  13 us (42%)
  waiting for transfers between devices  1.74 us (6%)
  between operations  0.84 us (3%)
  local copies, waits for them, and re-layouts  0.78 us (3%)
    all_to_all x2, starting transfers between devices, exchange(): lax.all_to_all(x, 'frame', split_axis=0, concat_axis=0, tiled=True, axis_...  13.8 us
    pallas_call x5, Pallas kernels, call(): pl.pallas_call(lambda *refs: body(*refs[len(after):]), out_shape=out, in_...  13 us
    ppermute x1, waiting for transfers between devices, on_device(): halo = lax.ppermute(edge, 'band', swap)  1.25 us
    unnamed x31, local copies, waits for them, and re-layouts  0.78 us
  transfers between devices with their start and end apart: 5, of which 2 were waited for; matrix products, arithmetic and copies ran while one was open for 0% of the time, Pallas kernels for 30%

profile of v8, /device:TPU:0, one launch (start us, length us, event | category | flops | bytes accessed | tf_op | source)
XLA Modules:
  0.0 30.8 jit_solution(3235002596133279457)
XLA Ops:
  0.6 0.0 copy-start
  0.6 0.0 copy-start.13
  0.7 0.0 copy-start.1
  0.7 0.0 copy-start.2
  0.7 0.0 copy-start.3
  0.7 0.0 copy-start.4
  0.7 0.0 copy-start.5
  0.7 0.0 copy-start.6
  0.7 1.7 %shard_map.161 = bf16[8,136,128]{2,1,0:T(8,128)(2,1)} custom-call(bf16[8,64,256]{2,1,0:T(8,128)(2,1)} %bitcast.10, s32[4,128]{1,0:T(4,128)} %bitcast.18), custom_call_target="tpu_custom_call" | custom-call | flops 10000000000 | bytes 264192 | tf_op jit(solution)/shard_map/pallas_call | solution.py:29
  2.5 0.0 copy-start.11
  2.5 0.0 copy-start.12
  2.5 8.0 %all-to-all-start = ((bf16[8,136,128]{2,1,0:T(8,128)(2,1)}), bf16[8,136,128]{2,1,0:T(8,128)(2,1)S(1)}, u32[]{:S(2)}, u32[]{:S(2)}) async-start(bf16[8,136,128]{2,1,0:T(8,128)(2,1)} %shard_map.161), calls=%async_computation | async-start | bytes 557056 | tf_op jit(solution)/shard_map/all_to_all | solution.py:53
  10.5 0.0 copy-done
  10.5 0.0 collective-permute-start
  10.5 0.0 copy-done.13
  10.5 0.5 %collective-permute-start.1 = (s32[1,512]{1,0:T(1,128)S(1)}, s32[1,512]{1,0:T(1,128)S(1)}, u32[]{:S(2)}, u32[]{:S(2)}) collective-permute-start(s32[1,512]{1,0:T(1,128)S(1)} %copy-done.13), channel_id=1, source_target_pairs={{0,1},{1,0},{2,3},{3,2},{4,5},{5,4},{6,7},{7,6},{8,9},{9,8},{10,11... | collective-permute-start | bytes 6152 | tf_op jit(solution)/shard_map/ppermute | solution.py:362
  11.1 0.5 %shard_map.158 = (bf16[256,256]{1,0:T(8,128)(2,1)S(1)}, bf16[512,256]{1,0:T(8,128)(2,1)S(1)}, bf16[512,256]{1,0:T(8,128)(2,1)S(1)}, bf16[768,256]{1,0:T(8,128)(2,1)S(1)}, bf16[256,256]{1,0:T(8,128)(2,1)S(1)}) custom-call(bf16[256,256]{1,0:T(8,128)(2,1)S(1)} %bitcast.13, bf16[512,256]{1,0:T(8,128)(2,1)S(1)} %bitcast.12, bf16[256,256]{1,0:T(8,128)(2,1)S(1)} %copy-done.2, ...), custom_call_target="tpu_custom_call" | custom-call | flops 167772160 | bytes 1310720 | tf_op jit(solution)/shard_map/pallas_call | solution.py:29
  11.5 0.5 %collective-permute-done.1.refs_5_ = s32[1,512]{1,0:T(1,128)S(1)} collective-permute-done((s32[1,512]{1,0:T(1,128)S(1)}, s32[1,512]{1,0:T(1,128)S(1)}, u32[]{:S(2)}, u32[]{:S(2)}) %collective-permute-start.1) | collective-permute-done | bytes 2080 | tf_op jit(solution)/shard_map/ppermute | solution.py:362
  12.0 0.0 collective-permute-done.refs_3_
  12.0 0.0 copy-start.14
  12.0 4.5 %shard_map.159 = (bf16[256,128]{1,0:T(8,128)(2,1)S(1)}, bf16[128,256]{1,0:T(8,128)(2,1)S(1)}) custom-call(bf16[256,256]{1,0:T(8,128)(2,1)S(1)} %get-tuple-element.9.refs_0_, bf16[512,256]{1,0:T(8,128)(2,1)S(1)} %get-tuple-element.10.refs_1_, bf16[512,256]{1,0:T(8,128)(2,1)S(1)} %get-tuple-element.11.refs_2_, ...), custom_call_target="tpu_custom_call" | custom-call | flops 2147483648 | bytes 1314816 | tf_op jit(solution)/shard_map/pallas_call | solution.py:29
  16.6 0.0 all-to-all-done.refs_1_
  16.6 0.0 copy-start.9
  16.6 0.0 copy-start.10
  16.6 2.1 %shard_map.162 = bf16[8,64,256]{2,1,0:T(8,128)(2,1)} custom-call(bf16[128,256]{1,0:T(8,128)(2,1)S(1)} %get-tuple-element.13.refs_0_, bf16[8,136,128]{2,1,0:T(8,128)(2,1)S(1)} %all-to-all-done.refs_1_, s32[4,128]{1,0:T(4,128)S(1)} %bitcast.19, bf16[768,256]{1,0:T(8,128)(2,1)S(1)} %get-tuple-element.14.refs_3_, bf16[256,256]{1,0:T(8,128)(2,1)S(1)} %get-tuple-element.15.refs_4_), custom_call_target="tpu_custom_call" | custom-call | flops 805306368 | bytes 804864 | tf_op jit(solution)/shard_map/pallas_call | solution.py:29
  18.8 5.9 %all-to-all-start.1 = ((bf16[8,64,256]{2,1,0:T(8,128)(2,1)}), bf16[8,64,256]{2,1,0:T(8,128)(2,1)S(1)}, u32[]{:S(2)}, u32[]{:S(2)}) async-start(bf16[8,64,256]{2,1,0:T(8,128)(2,1)} %shard_map.162), calls=%async_computation.1 | async-start | bytes 524288 | tf_op jit(solution)/shard_map/all_to_all | solution.py:53
  24.6 0.0 collective-permute-start.2
  24.6 1.3 %collective-permute-done.2.refs_2_ = bf16[128,256]{1,0:T(8,128)(2,1)S(1)} collective-permute-done((bf16[128,256]{1,0:T(8,128)(2,1)S(1)}, bf16[128,256]{1,0:T(8,128)(2,1)S(1)}, u32[]{:S(2)}, u32[]{:S(2)}) %collective-permute-start.2) | collective-permute-done | bytes 65568 | tf_op jit(solution)/shard_map/ppermute | solution.py:410
  25.9 0.0 copy-done.9
  25.9 4.2 %shard_map.160 = bf16[256,128]{1,0:T(8,128)(2,1)} custom-call(bf16[256,128]{1,0:T(8,128)(2,1)S(1)} %bitcast.17, bf16[256,128]{1,0:T(8,128)(2,1)S(1)} %get-tuple-element.12.refs_1_, bf16[128,256]{1,0:T(8,128)(2,1)S(1)} %collective-permute-done.2.refs_2_, bf16[9,256,256]{2,1,0:T(8,128)(2,1)S(1)} %bitcast.14, bf16[9,256,128]{2,1,0:T(8,128)(2,1)S(1)} %bitcast.15), custom_call_target="tpu_custom_call" | custom-call | flops 1358954496 | bytes 1966080 | tf_op jit(solution)/shard_map/pallas_call | solution.py:29
  30.0 0.0 all-to-all-done.1
  30.0 0.7 %copy.18 = bf16[1,512,256]{2,1,0:T(8,128)(2,1)} copy(bf16[1,512,256]{2,1,0:T(8,128)(2,1)S(1)} %bitcast.20) | data formatting | bytes 524288
  (14 shorter events, 0.0 us)
Async XLA Ops:
  0.6 9.9 %copy-start = (bf16[1,512,256]{2,1,0:T(8,128)(2,1)S(1)}, bf16[1,512,256]{2,1,0:T(8,128)(2,1)}, u32[]{:S(2)}) copy-start(bf16[1,512,256]{2,1,0:T(8,128)(2,1)} %param.17) | copy-start | bytes 786436
  0.6 9.9 %copy-start.13 = (s32[1,512]{1,0:T(1,128)S(1)}, s32[1,512]{1,0:T(1,128)}, u32[]{:S(2)}) copy-start(s32[1,512]{1,0:T(1,128)} %refs_4_.3) | copy-start | bytes 6148
  0.7 10.4 %copy-start.1 = (bf16[1,8,32,256]{3,2,1,0:T(8,128)(2,1)S(1)}, bf16[1,8,32,256]{3,2,1,0:T(8,128)(2,1)}, u32[]{:S(2)}) copy-start(bf16[1,8,32,256]{3,2,1,0:T(8,128)(2,1)} %param.15) | copy-start | bytes 393220
  0.7 10.3 %copy-start.2 = (bf16[256,256]{1,0:T(8,128)(2,1)S(1)}, bf16[256,256]{1,0:T(8,128)(2,1)}, u32[]{:S(2)}) copy-start(bf16[256,256]{1,0:T(8,128)(2,1)} %refs_2_.1) | copy-start | bytes 393220
  0.7 10.3 %copy-start.3 = (bf16[256,256]{1,0:T(8,128)(2,1)S(1)}, bf16[256,256]{1,0:T(8,128)(2,1)}, u32[]{:S(2)}) copy-start(bf16[256,256]{1,0:T(8,128)(2,1)} %refs_5_.1) | copy-start | bytes 393220
  0.7 10.3 %copy-start.4 = (bf16[256,256]{1,0:T(8,128)(2,1)S(1)}, bf16[256,256]{1,0:T(8,128)(2,1)}, u32[]{:S(2)}) copy-start(bf16[256,256]{1,0:T(8,128)(2,1)} %refs_6_.2) | copy-start | bytes 393220
  0.7 10.3 %copy-start.5 = (bf16[256,256]{1,0:T(8,128)(2,1)S(1)}, bf16[256,256]{1,0:T(8,128)(2,1)}, u32[]{:S(2)}) copy-start(bf16[256,256]{1,0:T(8,128)(2,1)} %refs_7_.2) | copy-start | bytes 393220
  0.7 10.3 %copy-start.6 = (bf16[256,256]{1,0:T(8,128)(2,1)S(1)}, bf16[256,256]{1,0:T(8,128)(2,1)}, u32[]{:S(2)}) copy-start(bf16[256,256]{1,0:T(8,128)(2,1)} %refs_8_.2) | copy-start | bytes 393220
  0.7 10.3 %copy-start.7 = (bf16[256,256]{1,0:T(8,128)(2,1)S(1)}, bf16[256,256]{1,0:T(8,128)(2,1)}, u32[]{:S(2)}) copy-start(bf16[256,256]{1,0:T(8,128)(2,1)} %refs_6_.3) | copy-start | bytes 393220
  0.7 10.3 %copy-start.8 = (bf16[256,256]{1,0:T(8,128)(2,1)S(1)}, bf16[256,256]{1,0:T(8,128)(2,1)}, u32[]{:S(2)}) copy-start(bf16[256,256]{1,0:T(8,128)(2,1)} %refs_7_.3) | copy-start | bytes 393220
  2.5 9.6 %copy-start.11 = (bf16[256,128]{1,0:T(8,128)(2,1)S(1)}, bf16[256,128]{1,0:T(8,128)(2,1)}, u32[]{:S(2)}) copy-start(bf16[256,128]{1,0:T(8,128)(2,1)} %refs_8_.3) | copy-start | bytes 196612
  2.5 9.5 %copy-start.12 = (bf16[1,8,32,128]{3,2,1,0:T(8,128)(2,1)S(1)}, bf16[1,8,32,128]{3,2,1,0:T(8,128)(2,1)}, u32[]{:S(2)}) copy-start(bf16[1,8,32,128]{3,2,1,0:T(8,128)(2,1)} %param.16) | copy-start | bytes 196612
  2.5 14.1 %all-to-all-start = ((bf16[8,136,128]{2,1,0:T(8,128)(2,1)}), bf16[8,136,128]{2,1,0:T(8,128)(2,1)S(1)}, u32[]{:S(2)}, u32[]{:S(2)}) async-start(bf16[8,136,128]{2,1,0:T(8,128)(2,1)} %shard_map.161), calls=%async_computation | async-start | bytes 557056 | tf_op jit(solution)/shard_map/all_to_all | solution.py:53
  10.5 1.5 %collective-permute-start = (bf16[512,256]{1,0:T(8,128)(2,1)S(1)}, bf16[512,256]{1,0:T(8,128)(2,1)S(1)}, u32[]{:S(2)}, u32[]{:S(2)}) collective-permute-start(bf16[512,256]{1,0:T(8,128)(2,1)S(1)} %bitcast.11), channel_id=1, source_target_pairs={{0,1},{1,0},{2,3},{3,2},{4,5},{5,4},{6,7},{7,6},{8,9},{9,8},{10,11... | collective-permute-start | bytes 786440 | tf_op jit(solution)/shard_map/ppermute | solution.py:361
  10.5 1.5 %collective-permute-start.1 = (s32[1,512]{1,0:T(1,128)S(1)}, s32[1,512]{1,0:T(1,128)S(1)}, u32[]{:S(2)}, u32[]{:S(2)}) collective-permute-start(s32[1,512]{1,0:T(1,128)S(1)} %copy-done.13), channel_id=1, source_target_pairs={{0,1},{1,0},{2,3},{3,2},{4,5},{5,4},{6,7},{7,6},{8,9},{9,8},{10,11... | collective-permute-start | bytes 6152 | tf_op jit(solution)/shard_map/ppermute | solution.py:362
  12.0 4.5 %copy-start.14 = (s32[512]{0:T(512)S(1)}, s32[512]{0:T(512)}, u32[]{:S(2)}) copy-start(s32[512]{0:T(512)} %param.19) | copy-start | bytes 6148
  16.6 9.3 %copy-start.9 = (bf16[3,3,256,256]{3,2,1,0:T(8,128)(2,1)S(1)}, bf16[3,3,256,256]{3,2,1,0:T(8,128)(2,1)}, u32[]{:S(2)}) copy-start(bf16[3,3,256,256]{3,2,1,0:T(8,128)(2,1)} %param.28) | copy-start | bytes 3538948
  16.6 9.3 %copy-start.10 = (bf16[3,3,256,128]{3,2,1,0:T(8,128)(2,1)S(1)}, bf16[3,3,256,128]{3,2,1,0:T(8,128)(2,1)}, u32[]{:S(2)}) copy-start(bf16[3,3,256,128]{3,2,1,0:T(8,128)(2,1)} %param.29) | copy-start | bytes 1769476
  18.8 11.3 %all-to-all-start.1 = ((bf16[8,64,256]{2,1,0:T(8,128)(2,1)}), bf16[8,64,256]{2,1,0:T(8,128)(2,1)S(1)}, u32[]{:S(2)}, u32[]{:S(2)}) async-start(bf16[8,64,256]{2,1,0:T(8,128)(2,1)} %shard_map.162), calls=%async_computation.1 | async-start | bytes 524288 | tf_op jit(solution)/shard_map/all_to_all | solution.py:53
  24.6 1.3 %collective-permute-start.2 = (bf16[128,256]{1,0:T(8,128)(2,1)S(1)}, bf16[128,256]{1,0:T(8,128)(2,1)S(1)}, u32[]{:S(2)}, u32[]{:S(2)}) collective-permute-start(bf16[128,256]{1,0:T(8,128)(2,1)S(1)} %get-tuple-element.13.refs_0_), channel_id=1, source_target_pairs={{0,1},{1,0},{2,3},{3,2},{4,5},{5,4},{6,7},{7,6},{8,9},{9,8},{10,11... | collective-permute-start | bytes 196616 | tf_op jit(solution)/shard_map/ppermute | solution.py:410

commit v9 on v8

--- a/solution.py
+++ b/solution.py
@@ -8,7 +8,7 @@
 HEADS = 8
 ITERS = 2
 LANES = 128
-MASK_ROWS = 8
+MASK_ROWS = 16
 HIDDEN = -1e30
 ORDERS = ((4, 3, 7, 6, 2, 0, 5, 1),)
 LOG2E = 1.4426950408889634

time: 31.1 us -> 31.5 us (1.013)
    all_to_all x2, starting transfers between devices: 13.8 us -> 14.2 us  [exchange(): lax.all_to_all(x, 'frame', split_axis=0, concat_axis=0, tiled=True, axis_...]
  transfers between devices with their start and end apart: 5 -> 5, of which waited for: 2 -> 2; matrix products, arithmetic and copies ran while one was open for 0% -> 0% of each run, Pallas kernels for 30% -> 29%
where the time goes in v9:
time: 31.5 us; the launch traced here: 31.1 us
  starting transfers between devices  14.7 us (47%)
  Pallas kernels  13 us (41%)
  waiting for transfers between devices  1.74 us (6%)
  between operations  0.84 us (3%)
  local copies, waits for them, and re-layouts  0.78 us (2%)
    all_to_all x2, starting transfers between devices, exchange(): lax.all_to_all(x, 'frame', split_axis=0, concat_axis=0, tiled=True, axis_...  14.2 us
    pallas_call x5, Pallas kernels, call(): pl.pallas_call(lambda *refs: body(*refs[len(after):]), out_shape=out, in_...  13 us
    ppermute x1, waiting for transfers between devices, on_device(): halo = lax.ppermute(edge, 'band', swap)  1.25 us
    unnamed x31, local copies, waits for them, and re-layouts  0.78 us
  transfers between devices with their start and end apart: 5, of which 2 were waited for; matrix products, arithmetic and copies ran while one was open for 0% of the time, Pallas kernels for 29%

profile of v9, /device:TPU:0, one launch (start us, length us, event | category | flops | bytes accessed | tf_op | source)
XLA Modules:
  0.0 31.1 jit_solution(9318420673742581305)
XLA Ops:
  0.6 0.0 copy-start
  0.6 0.0 copy-start.13
  0.7 0.0 copy-start.1
  0.7 0.0 copy-start.2
  0.7 0.0 copy-start.3
  0.7 0.0 copy-start.4
  0.7 0.0 copy-start.5
  0.7 0.0 copy-start.6
  0.7 0.0 copy-start.7
  0.7 0.0 copy-start.8
  0.7 1.7 %shard_map.161 = bf16[8,144,128]{2,1,0:T(8,128)(2,1)} custom-call(bf16[8,64,256]{2,1,0:T(8,128)(2,1)} %bitcast.10, s32[4,128]{1,0:T(4,128)} %bitcast.18), custom_call_target="tpu_custom_call" | custom-call | flops 10000000000 | bytes 264192 | tf_op jit(solution)/shard_map/pallas_call | solution.py:29
  2.5 0.0 copy-start.11
  2.5 0.0 copy-start.12
  2.5 8.0 %all-to-all-start = ((bf16[8,144,128]{2,1,0:T(8,128)(2,1)}), bf16[8,144,128]{2,1,0:T(8,128)(2,1)S(1)}, u32[]{:S(2)}, u32[]{:S(2)}) async-start(bf16[8,144,128]{2,1,0:T(8,128)(2,1)} %shard_map.161), calls=%async_computation | async-start | bytes 589824 | tf_op jit(solution)/shard_map/all_to_all | solution.py:53
  10.5 0.0 collective-permute-start
  10.5 0.5 %collective-permute-start.1 = (s32[1,512]{1,0:T(1,128)S(1)}, s32[1,512]{1,0:T(1,128)S(1)}, u32[]{:S(2)}, u32[]{:S(2)}) collective-permute-start(s32[1,512]{1,0:T(1,128)S(1)} %copy-done.13), channel_id=1, source_target_pairs={{0,1},{1,0},{2,3},{3,2},{4,5},{5,4},{6,7},{7,6},{8,9},{9,8},{10,11... | collective-permute-start | bytes 6152 | tf_op jit(solution)/shard_map/ppermute | solution.py:362
  11.0 0.0 copy-done.4
  11.1 0.5 %shard_map.158 = (bf16[256,256]{1,0:T(8,128)(2,1)S(1)}, bf16[512,256]{1,0:T(8,128)(2,1)S(1)}, bf16[512,256]{1,0:T(8,128)(2,1)S(1)}, bf16[768,256]{1,0:T(8,128)(2,1)S(1)}, bf16[256,256]{1,0:T(8,128)(2,1)S(1)}) custom-call(bf16[256,256]{1,0:T(8,128)(2,1)S(1)} %bitcast.13, bf16[512,256]{1,0:T(8,128)(2,1)S(1)} %bitcast.12, bf16[256,256]{1,0:T(8,128)(2,1)S(1)} %copy-done.2, ...), custom_call_target="tpu_custom_call" | custom-call | flops 167772160 | bytes 1310720 | tf_op jit(solution)/shard_map/pallas_call | solution.py:29
  11.5 0.5 %collective-permute-done.1.refs_5_ = s32[1,512]{1,0:T(1,128)S(1)} collective-permute-done((s32[1,512]{1,0:T(1,128)S(1)}, s32[1,512]{1,0:T(1,128)S(1)}, u32[]{:S(2)}, u32[]{:S(2)}) %collective-permute-start.1) | collective-permute-done | bytes 2080 | tf_op jit(solution)/shard_map/ppermute | solution.py:362
  12.0 0.0 collective-permute-done.refs_3_
  12.0 0.0 copy-start.14
  12.0 4.5 %shard_map.159 = (bf16[256,128]{1,0:T(8,128)(2,1)S(1)}, bf16[128,256]{1,0:T(8,128)(2,1)S(1)}) custom-call(bf16[256,256]{1,0:T(8,128)(2,1)S(1)} %get-tuple-element.9.refs_0_, bf16[512,256]{1,0:T(8,128)(2,1)S(1)} %get-tuple-element.10.refs_1_, bf16[512,256]{1,0:T(8,128)(2,1)S(1)} %get-tuple-element.11.refs_2_, ...), custom_call_target="tpu_custom_call" | custom-call | flops 2147483648 | bytes 1314816 | tf_op jit(solution)/shard_map/pallas_call | solution.py:29
  16.6 0.0 all-to-all-done.refs_1_
  16.6 0.0 copy-start.9
  16.6 0.0 copy-start.10
  16.6 2.1 %shard_map.162 = bf16[8,64,256]{2,1,0:T(8,128)(2,1)} custom-call(bf16[128,256]{1,0:T(8,128)(2,1)S(1)} %get-tuple-element.13.refs_0_, bf16[8,144,128]{2,1,0:T(8,128)(2,1)S(1)} %all-to-all-done.refs_1_, s32[4,128]{1,0:T(4,128)S(1)} %bitcast.19, bf16[768,256]{1,0:T(8,128)(2,1)S(1)} %get-tuple-element.14.refs_3_, bf16[256,256]{1,0:T(8,128)(2,1)S(1)} %get-tuple-element.15.refs_4_), custom_call_target="tpu_custom_call" | custom-call | flops 805306368 | bytes 821248 | tf_op jit(solution)/shard_map/pallas_call | solution.py:29
  18.8 6.2 %all-to-all-start.1 = ((bf16[8,64,256]{2,1,0:T(8,128)(2,1)}), bf16[8,64,256]{2,1,0:T(8,128)(2,1)S(1)}, u32[]{:S(2)}, u32[]{:S(2)}) async-start(bf16[8,64,256]{2,1,0:T(8,128)(2,1)} %shard_map.162), calls=%async_computation.1 | async-start | bytes 524288 | tf_op jit(solution)/shard_map/all_to_all | solution.py:53
  25.0 0.0 collective-permute-start.2
  25.0 1.3 %collective-permute-done.2.refs_2_ = bf16[128,256]{1,0:T(8,128)(2,1)S(1)} collective-permute-done((bf16[128,256]{1,0:T(8,128)(2,1)S(1)}, bf16[128,256]{1,0:T(8,128)(2,1)S(1)}, u32[]{:S(2)}, u32[]{:S(2)}) %collective-permute-start.2) | collective-permute-done | bytes 65568 | tf_op jit(solution)/shard_map/ppermute | solution.py:410
  26.2 4.2 %shard_map.160 = bf16[256,128]{1,0:T(8,128)(2,1)} custom-call(bf16[256,128]{1,0:T(8,128)(2,1)S(1)} %bitcast.17, bf16[256,128]{1,0:T(8,128)(2,1)S(1)} %get-tuple-element.12.refs_1_, bf16[128,256]{1,0:T(8,128)(2,1)S(1)} %collective-permute-done.2.refs_2_, bf16[9,256,256]{2,1,0:T(8,128)(2,1)S(1)} %bitcast.14, bf16[9,256,128]{2,1,0:T(8,128)(2,1)S(1)} %bitcast.15), custom_call_target="tpu_custom_call" | custom-call | flops 1358954496 | bytes 1966080 | tf_op jit(solution)/shard_map/pallas_call | solution.py:29
  30.4 0.0 all-to-all-done.1
  30.4 0.7 %copy.18 = bf16[1,512,256]{2,1,0:T(8,128)(2,1)} copy(bf16[1,512,256]{2,1,0:T(8,128)(2,1)S(1)} %bitcast.20) | data formatting | bytes 524288
  (14 shorter events, 0.0 us)
Async XLA Ops:
  0.6 9.9 %copy-start = (bf16[1,512,256]{2,1,0:T(8,128)(2,1)S(1)}, bf16[1,512,256]{2,1,0:T(8,128)(2,1)}, u32[]{:S(2)}) copy-start(bf16[1,512,256]{2,1,0:T(8,128)(2,1)} %param.17) | copy-start | bytes 786436
  0.6 9.9 %copy-start.13 = (s32[1,512]{1,0:T(1,128)S(1)}, s32[1,512]{1,0:T(1,128)}, u32[]{:S(2)}) copy-start(s32[1,512]{1,0:T(1,128)} %refs_4_.3) | copy-start | bytes 6148
  0.7 10.4 %copy-start.1 = (bf16[1,8,32,256]{3,2,1,0:T(8,128)(2,1)S(1)}, bf16[1,8,32,256]{3,2,1,0:T(8,128)(2,1)}, u32[]{:S(2)}) copy-start(bf16[1,8,32,256]{3,2,1,0:T(8,128)(2,1)} %param.15) | copy-start | bytes 393220
  0.7 10.3 %copy-start.2 = (bf16[256,256]{1,0:T(8,128)(2,1)S(1)}, bf16[256,256]{1,0:T(8,128)(2,1)}, u32[]{:S(2)}) copy-start(bf16[256,256]{1,0:T(8,128)(2,1)} %refs_2_.1) | copy-start | bytes 393220
  0.7 10.3 %copy-start.3 = (bf16[256,256]{1,0:T(8,128)(2,1)S(1)}, bf16[256,256]{1,0:T(8,128)(2,1)}, u32[]{:S(2)}) copy-start(bf16[256,256]{1,0:T(8,128)(2,1)} %refs_5_.1) | copy-start | bytes 393220
  0.7 10.3 %copy-start.4 = (bf16[256,256]{1,0:T(8,128)(2,1)S(1)}, bf16[256,256]{1,0:T(8,128)(2,1)}, u32[]{:S(2)}) copy-start(bf16[256,256]{1,0:T(8,128)(2,1)} %refs_6_.2) | copy-start | bytes 393220
  0.7 10.3 %copy-start.5 = (bf16[256,256]{1,0:T(8,128)(2,1)S(1)}, bf16[256,256]{1,0:T(8,128)(2,1)}, u32[]{:S(2)}) copy-start(bf16[256,256]{1,0:T(8,128)(2,1)} %refs_7_.2) | copy-start | bytes 393220
  0.7 10.3 %copy-start.6 = (bf16[256,256]{1,0:T(8,128)(2,1)S(1)}, bf16[256,256]{1,0:T(8,128)(2,1)}, u32[]{:S(2)}) copy-start(bf16[256,256]{1,0:T(8,128)(2,1)} %refs_8_.2) | copy-start | bytes 393220
  0.7 10.3 %copy-start.7 = (bf16[256,256]{1,0:T(8,128)(2,1)S(1)}, bf16[256,256]{1,0:T(8,128)(2,1)}, u32[]{:S(2)}) copy-start(bf16[256,256]{1,0:T(8,128)(2,1)} %refs_6_.3) | copy-start | bytes 393220
  0.7 10.3 %copy-start.8 = (bf16[256,256]{1,0:T(8,128)(2,1)S(1)}, bf16[256,256]{1,0:T(8,128)(2,1)}, u32[]{:S(2)}) copy-start(bf16[256,256]{1,0:T(8,128)(2,1)} %refs_7_.3) | copy-start | bytes 393220
  2.5 9.6 %copy-start.11 = (bf16[256,128]{1,0:T(8,128)(2,1)S(1)}, bf16[256,128]{1,0:T(8,128)(2,1)}, u32[]{:S(2)}) copy-start(bf16[256,128]{1,0:T(8,128)(2,1)} %refs_8_.3) | copy-start | bytes 196612
  2.5 9.5 %copy-start.12 = (bf16[1,8,32,128]{3,2,1,0:T(8,128)(2,1)S(1)}, bf16[1,8,32,128]{3,2,1,0:T(8,128)(2,1)}, u32[]{:S(2)}) copy-start(bf16[1,8,32,128]{3,2,1,0:T(8,128)(2,1)} %param.16) | copy-start | bytes 196612
  2.5 14.1 %all-to-all-start = ((bf16[8,144,128]{2,1,0:T(8,128)(2,1)}), bf16[8,144,128]{2,1,0:T(8,128)(2,1)S(1)}, u32[]{:S(2)}, u32[]{:S(2)}) async-start(bf16[8,144,128]{2,1,0:T(8,128)(2,1)} %shard_map.161), calls=%async_computation | async-start | bytes 589824 | tf_op jit(solution)/shard_map/all_to_all | solution.py:53
  10.5 1.5 %collective-permute-start = (bf16[512,256]{1,0:T(8,128)(2,1)S(1)}, bf16[512,256]{1,0:T(8,128)(2,1)S(1)}, u32[]{:S(2)}, u32[]{:S(2)}) collective-permute-start(bf16[512,256]{1,0:T(8,128)(2,1)S(1)} %bitcast.11), channel_id=1, source_target_pairs={{0,1},{1,0},{2,3},{3,2},{4,5},{5,4},{6,7},{7,6},{8,9},{9,8},{10,11... | collective-permute-start | bytes 786440 | tf_op jit(solution)/shard_map/ppermute | solution.py:361
  10.5 1.5 %collective-permute-start.1 = (s32[1,512]{1,0:T(1,128)S(1)}, s32[1,512]{1,0:T(1,128)S(1)}, u32[]{:S(2)}, u32[]{:S(2)}) collective-permute-start(s32[1,512]{1,0:T(1,128)S(1)} %copy-done.13), channel_id=1, source_target_pairs={{0,1},{1,0},{2,3},{3,2},{4,5},{5,4},{6,7},{7,6},{8,9},{9,8},{10,11... | collective-permute-start | bytes 6152 | tf_op jit(solution)/shard_map/ppermute | solution.py:362
  12.0 4.5 %copy-start.14 = (s32[512]{0:T(512)S(1)}, s32[512]{0:T(512)}, u32[]{:S(2)}) copy-start(s32[512]{0:T(512)} %param.19) | copy-start | bytes 6148
  16.6 9.7 %copy-start.9 = (bf16[3,3,256,256]{3,2,1,0:T(8,128)(2,1)S(1)}, bf16[3,3,256,256]{3,2,1,0:T(8,128)(2,1)}, u32[]{:S(2)}) copy-start(bf16[3,3,256,256]{3,2,1,0:T(8,128)(2,1)} %param.28) | copy-start | bytes 3538948
  16.6 9.6 %copy-start.10 = (bf16[3,3,256,128]{3,2,1,0:T(8,128)(2,1)S(1)}, bf16[3,3,256,128]{3,2,1,0:T(8,128)(2,1)}, u32[]{:S(2)}) copy-start(bf16[3,3,256,128]{3,2,1,0:T(8,128)(2,1)} %param.29) | copy-start | bytes 1769476
  18.8 11.6 %all-to-all-start.1 = ((bf16[8,64,256]{2,1,0:T(8,128)(2,1)}), bf16[8,64,256]{2,1,0:T(8,128)(2,1)S(1)}, u32[]{:S(2)}, u32[]{:S(2)}) async-start(bf16[8,64,256]{2,1,0:T(8,128)(2,1)} %shard_map.162), calls=%async_computation.1 | async-start | bytes 524288 | tf_op jit(solution)/shard_map/all_to_all | solution.py:53
  25.0 1.3 %collective-permute-start.2 = (bf16[128,256]{1,0:T(8,128)(2,1)S(1)}, bf16[128,256]{1,0:T(8,128)(2,1)S(1)}, u32[]{:S(2)}, u32[]{:S(2)}) collective-permute-start(bf16[128,256]{1,0:T(8,128)(2,1)S(1)} %get-tuple-element.13.refs_0_), channel_id=1, source_target_pairs={{0,1},{1,0},{2,3},{3,2},{4,5},{5,4},{6,7},{7,6},{8,9},{9,8},{10,11... | collective-permute-start | bytes 196616 | tf_op jit(solution)/shard_map/ppermute | solution.py:410
